TPU v7x, 512 devices: a whole 4x8x8 slice. The times are simulated.
512 devices in a mesh: tm: 32 (over y, x), chan: 16 (over z, core).
Axes of the slice: x: 4, y: 8, z: 8, core: 2. Of those that a mesh axis runs over, the one named last changes fastest.
Arguments:
- records: bfloat16 [1, 128, 1048576], P(None, 'chan', 'tm'), may hold values from -6 to 6
- spectral_weight: bfloat16 [2048, 2, 128, 128], P(('tm', 'chan')), may hold values from -6 to 6
- skip_weight: bfloat16 [128, 128], P('chan'), may hold values from -0.5 to 0.5
- skip_bias: float32 [128], P('chan'), may hold values from -3 to 3
Outputs:
- layer_out: bfloat16 [1, 128, 1048576], P(None, 'chan', 'tm')
All inputs are finite; a program needn't handle non-finite values.
Results may differ from a plain program's by a relative error of at most 0.02.
Values may be sent and summed in bfloat16 or wider, within the bound.
No kernel may reach another device: no remote copies, remote signals or barrier semaphores. Data moves between devices by JAX's collectives and lax.ppermute only.
A program may use at most 128 MiB of HBM per device.

v0:
```python
import math

import jax
import jax.numpy as jnp
from jax import lax
from jax.sharding import PartitionSpec as P

MODES = 2048


def shards(records, spectral_weight, skip_weight, skip_bias):
    groups, chan_dev, time_dev = records.shape
    tm_count = lax.axis_size("tm")
    chan_count = lax.axis_size("chan")
    steps_all = time_dev * tm_count
    block_len = min(256, time_dev)
    block_count = time_dev // block_len
    turns = math.gcd(8, block_count)
    per_turn = block_count // turns
    row_count = groups * chan_dev
    time_start = lax.axis_index("tm") * time_dev
    angle_unit = 2.0 * math.pi / steps_all
    mode_pos = jnp.arange(MODES, dtype=jnp.int32)
    inner_pos = jnp.arange(block_len, dtype=jnp.int32)
    inner_phase = inner_pos[:, None] * mode_pos[None, :] % steps_all
    inner_angle = inner_phase.astype(jnp.float32) * angle_unit
    both_tables = jnp.concatenate([jnp.cos(inner_angle), -jnp.sin(inner_angle)], axis=1).astype(
        jnp.bfloat16
    )

    def twiddles(turn):
        block_ids = turn * per_turn + jnp.arange(per_turn, dtype=jnp.int32)
        starts = time_start + block_ids * block_len
        phase = starts[:, None] * mode_pos[None, :] % steps_all
        angle = phase.astype(jnp.float32) * angle_unit
        return (jnp.cos(angle), jnp.sin(angle))

    def forward_turn(carry, turn):
        sum_real, sum_imag = carry
        segment = lax.dynamic_slice_in_dim(
            records, turn * (per_turn * block_len), per_turn * block_len, 2
        )
        seg_rows = segment.reshape(row_count * per_turn, block_len)
        product = jnp.dot(seg_rows, both_tables, preferred_element_type=jnp.float32)
        product = product.reshape(row_count, per_turn, 2, MODES)
        cos_turn, sin_turn = twiddles(turn)
        neg_turn = -sin_turn
        first_part = product[:, :, 0, :]
        second_part = product[:, :, 1, :]
        sum_real = sum_real + jnp.sum(
            first_part * cos_turn[None] - second_part * neg_turn[None], axis=1
        )
        sum_imag = sum_imag + jnp.sum(
            first_part * neg_turn[None] + second_part * cos_turn[None], axis=1
        )
        return ((sum_real, sum_imag), None)

    zero_modes = jnp.zeros((row_count, MODES), jnp.float32)
    turn_ids = jnp.arange(turns, dtype=jnp.int32)
    (sum_real, sum_imag), _ = lax.scan(forward_turn, (zero_modes, zero_modes), turn_ids)
    partial_value = jnp.stack([sum_real, sum_imag], axis=1).reshape(groups, chan_dev, 2, MODES)
    spectrum = lax.psum_scatter(
        partial_value.astype(jnp.bfloat16), "tm", scatter_dimension=3, tiled=True
    )
    block_modes = MODES // (tm_count * chan_count)
    mode_first = lax.axis_index("tm") * (MODES // tm_count) + lax.axis_index("chan") * block_modes
    local_modes = mode_first + jnp.arange(block_modes, dtype=jnp.int32)
    scaling = jnp.where(local_modes == 0, 1.0, 2.0).astype(jnp.float32) / steps_all
    w_real = spectral_weight[:, 0]
    w_imag = spectral_weight[:, 1]
    gathered = lax.all_to_all(spectrum, "chan", split_axis=3, concat_axis=1, tiled=True)
    real_in = gathered[:, :, 0, :]
    imag_in = gathered[:, :, 1, :]
    real_out = jnp.einsum(
        "bik,kio->bok", real_in, w_real, preferred_element_type=jnp.float32
    ) - jnp.einsum("bik,kio->bok", imag_in, w_imag, preferred_element_type=jnp.float32)
    imag_out = jnp.einsum(
        "bik,kio->bok", real_in, w_imag, preferred_element_type=jnp.float32
    ) + jnp.einsum("bik,kio->bok", imag_in, w_real, preferred_element_type=jnp.float32)
    mixed_block = (jnp.stack([real_out, imag_out], axis=2) * scaling).astype(jnp.bfloat16)
    mixed = lax.all_to_all(mixed_block, "chan", split_axis=1, concat_axis=3, tiled=True)
    all_modes = lax.all_gather(mixed, "tm", axis=3, tiled=True)
    mode_real = all_modes[:, :, 0, :].reshape(row_count, MODES).astype(jnp.float32)
    mode_imag = all_modes[:, :, 1, :].reshape(row_count, MODES).astype(jnp.float32)
    contract_modes = (((1,), (1,)), ((), ()))

    def inverse_turn(carry, turn):
        cos_turn, sin_turn = twiddles(turn)
        turned_real = (
            mode_real[:, None, :] * cos_turn[None] - mode_imag[:, None, :] * sin_turn[None]
        )
        turned_imag = (
            mode_real[:, None, :] * sin_turn[None] + mode_imag[:, None, :] * cos_turn[None]
        )
        turned = jnp.concatenate([turned_real, turned_imag], axis=2).reshape(
            row_count * per_turn, 2 * MODES
        )
        upper = turned.astype(jnp.bfloat16)
        lower = (turned - upper.astype(jnp.float32)).astype(jnp.bfloat16)
        values = lax.dot_general(
            upper, both_tables, contract_modes, preferred_element_type=jnp.float32
        )
        values = values + lax.dot_general(
            lower, both_tables, contract_modes, preferred_element_type=jnp.float32
        )
        return (carry, values.reshape(row_count, per_turn * block_len))

    _, pieces = lax.scan(inverse_turn, jnp.zeros((), jnp.float32), turn_ids)
    spectral = jnp.moveaxis(pieces, 0, 1).reshape(groups, chan_dev, time_dev)
    skip = jnp.einsum(
        "oi,bit->bot",
        skip_weight,
        lax.all_gather(records, "chan", axis=1, tiled=True),
        preferred_element_type=jnp.float32,
    )
    combined = spectral + skip + skip_bias[None, :, None]
    return jax.nn.gelu(combined, approximate=False).astype(jnp.bfloat16)


def solution(mesh):
    return jax.shard_map(
        shards,
        mesh=mesh,
        in_specs=(
            P(None, "chan", "tm"),
            P(("tm", "chan"), None, None, None),
            P("chan", None),
            P("chan"),
        ),
        out_specs=P(None, "chan", "tm"),
        check_vma=False,
    )
```

profile of v0, /device:TPU:1, one launch (start us, length us, event | category | flops | bytes accessed | tf_op | source)
XLA Modules:
  0.0 407.1 jit_solution(4962634687900721269)
XLA Ops:
  7.4 9.2 %negate_convert_fusion = (bf16[256,2048]{0,1:T(8,128)(2,1)S(1)}, bf16[256,2048]{0,1:T(8,128)(2,1)}) fusion(), kind=kLoop, calls=%fused_computation.59 | loop fusion | flops 8912896 | bytes 2097152 | tf_op jit(solution)/shard_map/convert.7
  16.6 1.4 pad_maximum_fusion.1
  17.9 38.0 %while.29 = (s32[]{:T(128)}, f32[8,2048]{1,0:T(8,128)S(1)}, f32[8,2048]{1,0:T(8,128)S(1)}, s32[8]{0:T(128)S(1)}, bf16[1,8,32768]{2,1,0:T(8,128)(2,1)}, /*index=5...) while((s32[]{:T(128)}, f32[8,2048]{1,0:T(8,128)S(1)}, ...), condition=%wide.region_3.4_spmd.clone, body=%wide.region_0.3_spmd.clone.sunk | while | flops 271056960 | bytes 7536977 | solution.py:60
  56.8 1.3 reshape.328
  58.1 218.7 %reduce-scatter.4.cloned.1.call-done = bf16[64,16]{1,0:T(8,128)(2,1)} async-done(((bf16[2048,16]{1,0:T(8,128)(2,1)}), bf16[64,16]{1,0:T(8,128)(2,1)}) %reduce-scatter.4.cloned.1.call-update) | async-done | bytes 2064
  276.8 1.4 reshape.329
  278.2 13.2 %all-to-all-start = ((bf16[1,8,2,64]{1,2,0,3:T(2,128)(2,1)}), bf16[1,8,2,64]{1,2,0,3:T(2,128)(2,1)S(1)}, u32[]{:S(2)}, u32[]{:S(2)}) async-start(bf16[1,8,2,64]{1,2,0,3:T(2,128)(2,1)} %bitcast.47), calls=%async_computation | async-start | bytes 65536 | tf_op jit(solution)/shard_map/all_to_all | solution.py:71
  291.5 7.4 %all-to-all-done = bf16[1,8,2,64]{1,2,0,3:T(2,128)(2,1)S(1)} async-done(((bf16[1,8,2,64]{1,2,0,3:T(2,128)(2,1)}), bf16[1,8,2,64]{1,2,0,3:T(2,128)(2,1)S(1)}, u32[]{:S(2)}, u32[]{:S(2)}) %all-to-all-start) | async-done | bytes 2080 | tf_op jit(solution)/shard_map/all_to_all | solution.py:71
  300.4 3.7 all-to-all-start.1
  304.7 2.9 copy.43
  307.6 4.3 %all-to-all-done.1 = bf16[1,128,2,4]{3,2,0,1:T(2,128)(2,1)S(1)} async-done(((bf16[1,128,2,4]{3,2,0,1:T(2,128)(2,1)}), bf16[1,128,2,4]{3,2,0,1:T(2,128)(2,1)S(1)}, u32[]{:S(2)}, u32[]{:S(2)}) %all-to-all-start.1) | async-done | bytes 2080 | tf_op jit(solution)/shard_map/all_to_all | solution.py:81
  312.3 40.7 %all_gather.6 = bf16[1,8,2,2048]{1,3,2,0:T(8,128)(2,1)S(1)} all-gather(bf16[1,8,2,64]{1,3,2,0:T(8,128)(2,1)S(1)} %bitcast.158), channel_id=1, replica_groups=mesh['tm'=32,'chan'=16] {'tm'}, dimensions={3}, use_global_device_ids=true | all-gather | bytes 67584 | tf_op jit(solution)/shard_map/all_gather | solution.py:82
  353.0 1.1 fusion.47
  354.1 1.5 copy.41
  356.0 36.5 %while.28 = (s32[]{:T(128)}, f32[8,8,4096]{2,1,0:T(8,128)}, f32[8,2048]{1,0:T(8,128)S(1)}, s32[]{:T(128)}, s32[8]{0:T(128)S(1)}, /*index=5*/f32[8,2048]{1,0:T(8,...) while((s32[]{:T(128)}, f32[8,8,4096]{2,1,0:T(8,128)}, f32[8,2048]{1,0:T(8,128)S(1)}, ...), condition=%wide.region_6.7_spmd.clone, body=%wide.region_5.6_spmd.clone.sunk | while | flops 543653952 | bytes 12059389 | solution.py:108
  358.1 0.9 fusion.83
  362.7 0.9 fusion.83
  363.5 0.9 convolution_add_fusion.2
  371.8 0.9 fusion.83
  376.4 0.9 fusion.83
  380.9 0.9 fusion.83
  385.5 0.9 fusion.83
  390.0 0.9 fusion.83
  392.5 7.2 %fusion.37 = bf16[1,8,32768]{2,1,0:T(8,128)(2,1)} fusion(f32[1,8,32768]{2,1,0:T(8,128)} %bitcast.164, bf16[8,128]{1,0:T(8,128)(2,1)S(1)} %copy-done, bf16[1,128,32768]{2,1,0:T(8,128)(2,1)} %all-gather.2.cloned.1.call-done, f32[8]{0:T(128)S(1)} %copy-done.3), kind=kOutput, calls=%fused_computation.67 | convolution fusion | flops 84672512 | bytes 9963552 | tf_op jit(solution)/shard_map/oi,bit->bot/dot_general | solution.py:110
  (150 shorter events, 55.3 us)
Async XLA Ops:
  7.4 385.1 %copy-start = (bf16[8,128]{1,0:T(8,128)(2,1)S(1)}, bf16[8,128]{1,0:T(8,128)(2,1)}, u32[]{:S(2)}) copy-start(bf16[8,128]{1,0:T(8,128)(2,1)} %param.10) | copy-start | bytes 6148
  7.4 269.4 %reduce-scatter.4.cloned.1.call-start = ((), (), s32[]{:S(2)}) async-start(), calls=%async_computation.4 | async-start | bytes 540672
  56.0 243.5 %copy-start.1 = (bf16[256,4096]{0,1:T(8,128)(2,1)}, bf16[256,4096]{0,1:T(8,128)(2,1)S(1)}, u32[]{:S(2)}) copy-start(bf16[256,4096]{0,1:T(8,128)(2,1)S(1)} %get-tuple-element.505) | copy-start | bytes 6291460
  56.0 243.0 %copy-start.2 = (bf16[4,2,128,128]{3,2,1,0:T(8,128)(2,1)S(1)}, bf16[4,2,128,128]{3,2,1,0:T(8,128)(2,1)}, u32[]{:S(2)}) copy-start(bf16[4,2,128,128]{3,2,1,0:T(8,128)(2,1)} %param.9) | copy-start | bytes 786436
  278.2 20.6 %all-to-all-start = ((bf16[1,8,2,64]{1,2,0,3:T(2,128)(2,1)}), bf16[1,8,2,64]{1,2,0,3:T(2,128)(2,1)S(1)}, u32[]{:S(2)}, u32[]{:S(2)}) async-start(bf16[1,8,2,64]{1,2,0,3:T(2,128)(2,1)} %bitcast.47), calls=%async_computation | async-start | bytes 65536 | tf_op jit(solution)/shard_map/all_to_all | solution.py:71
  300.4 11.5 %all-to-all-start.1 = ((bf16[1,128,2,4]{3,2,0,1:T(2,128)(2,1)}), bf16[1,128,2,4]{3,2,0,1:T(2,128)(2,1)S(1)}, u32[]{:S(2)}, u32[]{:S(2)}) async-start(bf16[1,128,2,4]{3,2,0,1:T(2,128)(2,1)} %copy.38), calls=%async_computation.1 | async-start | bytes 131072 | tf_op jit(solution)/shard_map/all_to_all | solution.py:81
  304.1 88.3 %all-gather.2.cloned.1.call-start = ((), (), s32[]{:S(2)}) async-start(), calls=%async_computation.3 | async-start | bytes 8912896 | tf_op jit(solution)/shard_map/all_gather | solution.py:113
  356.0 36.5 %copy-start.3 = (f32[8]{0:T(128)S(1)}, f32[8]{0:T(128)}, u32[]{:S(2)}) copy-start(f32[8]{0:T(128)} %param.11) | copy-start | bytes 100
Sparse Core Ops, SparseCore 0:
  58.2 218.5 reduce-scatter.3
Sparse Core Ops, SparseCore 1:
  306.9 57.7 all-gather.1
where the time goes:
time: 414 us; the launch traced here: 407 us
  waiting for transfers between devices  231 us (56%)
  blocking collectives  40.7 us (10%)
  local copies, waits for them, and re-layouts  31.6 us (8%)
  other arithmetic  28 us (7%)
  matrix products  27.9 us (7%)
  starting transfers between devices  17 us (4%)
  loops' own time  16 us (4%)
  between operations  15 us (4%)
    unnamed x3, waiting for transfers between devices  219 us
    all_gather x1, blocking collectives, shards(): all_modes = lax.all_gather(mixed, 'tm', axis=3, tiled=True)  40.7 us
    all_to_all x1, starting transfers between devices, shards(): lax.all_to_all(spectrum, 'chan', split_axis=3, concat_axis=1, tiled=True)  13.2 us
    another operation x1, loops' own time, shards(): lax.scan(forward_turn, (zero_modes, zero_modes), turn_ids)  10.4 us
    dynamic_slice x16, local copies, waits for them, and re-layouts, shards(): lax.scan(forward_turn, (zero_modes, zero_modes), turn_ids)  9.84 us
    cos x16, other arithmetic, twiddles(): return (jnp.cos(angle), jnp.sin(angle))  9.53 us
    another operation x1, other arithmetic  9.2 us
  transfers between devices with their start and end apart: 4, of which 3 were waited for; matrix products, arithmetic and copies ran while one was open for 9% of the time, Pallas kernels for 0%

commit v1 on v0

v1 whole, which is shorter than its diff:
```python
import math

import jax
import jax.numpy as jnp
import numpy as np
from jax import lax
from jax.experimental import pallas as pl
from jax.experimental.pallas import tpu as pltpu
from jax.sharding import PartitionSpec as P

MODES = 2048
INNER = 512
CHUNK = 256


def tables(steps_all, time_dev):
    blocks = time_dev // INNER
    tm_count = steps_all // time_dev
    modes = np.arange(MODES, dtype=np.int64)

    def turn(positions):
        phase = positions[:, None] * modes[None, :] % steps_all
        angle = phase * (2.0 * math.pi / steps_all)
        return np.cos(angle), np.sin(angle)

    inner_cos, inner_sin = turn(np.arange(INNER, dtype=np.int64))
    chunks = MODES // CHUNK
    split = lambda a: a.reshape(INNER, chunks, CHUNK)
    forward = np.stack([split(inner_cos), split(inner_sin)], axis=2).reshape(INNER, 2 * MODES)
    inverse = np.stack([split(inner_cos), -split(inner_sin)], axis=2).reshape(INNER, 2 * MODES).T
    block_turn = np.stack(turn(np.arange(blocks, dtype=np.int64) * INNER))
    start_turn = np.stack(turn(np.arange(tm_count, dtype=np.int64) * time_dev), axis=1)
    return (
        np.ascontiguousarray(forward).astype(jnp.bfloat16),
        np.ascontiguousarray(inverse).astype(jnp.bfloat16),
        block_turn.astype(np.float32),
        start_turn.astype(np.float32),
    )


def forward_kernel(where_ref, x_ref, table_ref, block_ref, start_ref, out_ref, rows_ref):
    blocks = block_ref.shape[1]
    half = 64

    @pl.when(pl.program_id(0) == 0)
    def _():
        for pair in range(blocks // 2):
            first = x_ref[:, pl.ds(2 * pair * INNER, INNER)].astype(jnp.float32)
            second = x_ref[:, pl.ds((2 * pair + 1) * INNER, INNER)].astype(jnp.float32)
            rows_ref[pl.ds(16 * pair, 16), :] = jnp.concatenate([first, second], axis=0).astype(
                jnp.bfloat16
            )

    real = jnp.zeros((8, CHUNK), jnp.float32)
    imag = jnp.zeros((8, CHUNK), jnp.float32)
    group = 16
    for g in range(blocks // group):
        product = jnp.dot(
            rows_ref[pl.ds(g * group * 8, group * 8), :],
            table_ref[...],
            preferred_element_type=jnp.float32,
        )
        for b in range(group):
            by_cos = product[8 * b : 8 * b + 8, :CHUNK]
            by_sin = product[8 * b : 8 * b + 8, CHUNK:]
            cos_b = block_ref[0, pl.ds(g * group + b, 1), :]
            sin_b = block_ref[1, pl.ds(g * group + b, 1), :]
            real = real + (by_cos * cos_b - by_sin * sin_b)
            imag = imag + (by_cos * sin_b + by_sin * cos_b)
    cos_s = start_ref[0, 0:1, :]
    sin_s = start_ref[0, 1:2, :]
    out_real = real * cos_s - imag * sin_s
    out_imag = -(real * sin_s + imag * cos_s)
    low = lax.broadcasted_iota(jnp.int32, (8, 128), 1) < half
    for tile in range(CHUNK // 128):
        re = out_real[:, 128 * tile : 128 * tile + 128]
        im = out_imag[:, 128 * tile : 128 * tile + 128]
        out_ref[2 * tile] = jnp.where(low, re, pltpu.roll(im, half, 1)).astype(out_ref.dtype)
        out_ref[2 * tile + 1] = jnp.where(low, pltpu.roll(re, half, 1), im).astype(out_ref.dtype)


def forward(where, x, table, block_turn, start_turn):
    chan_dev, time_dev = x.shape
    blocks = time_dev // INNER
    chunks = MODES // CHUNK
    owners = MODES // 64
    return pl.pallas_call(
        forward_kernel,
        grid_spec=pltpu.PrefetchScalarGridSpec(
            num_scalar_prefetch=1,
            grid=(chunks,),
            in_specs=[
                pl.BlockSpec((chan_dev, time_dev), lambda i, w: (0, 0)),
                pl.BlockSpec((INNER, 2 * CHUNK), lambda i, w: (0, i)),
                pl.BlockSpec((2, blocks, CHUNK), lambda i, w: (0, 0, i)),
                pl.BlockSpec((1, 2, CHUNK), lambda i, w: (w[0], 0, i)),
            ],
            out_specs=pl.BlockSpec((owners // chunks, chan_dev, 128), lambda i, w: (i, 0, 0)),
            scratch_shapes=[pltpu.VMEM((blocks * chan_dev, INNER), jnp.bfloat16)],
        ),
        out_shape=jax.ShapeDtypeStruct((owners, chan_dev, 128), jnp.bfloat16),
        compiler_params=pltpu.CompilerParams(vmem_limit_bytes=24 << 20),
        cost_estimate=pl.CostEstimate(
            flops=4 * chan_dev * time_dev * MODES, bytes_accessed=6 << 20, transcendentals=0
        ),
        name="forward_modes",
    )(where, x, table, block_turn, start_turn)


def inverse_kernel(where_ref, mixed_ref, table_ref, block_ref, start_ref, out_ref, turned_ref, sum_ref):
    blocks = block_ref.shape[1]
    half = 64
    step = pl.program_id(0)
    low = lax.broadcasted_iota(jnp.int32, (8, 128), 1) < half
    reals, imags = [], []
    for tile in range(CHUNK // 128):
        even = mixed_ref[2 * tile].astype(jnp.float32)
        odd = mixed_ref[2 * tile + 1].astype(jnp.float32)
        reals.append(jnp.where(low, even, pltpu.roll(odd, half, 1)))
        imags.append(jnp.where(low, pltpu.roll(even, half, 1), odd))
    in_real = jnp.concatenate(reals, axis=1)
    in_imag = jnp.concatenate(imags, axis=1)
    cos_s = start_ref[0, 0:1, :]
    sin_s = start_ref[0, 1:2, :]
    real = in_real * cos_s - in_imag * sin_s
    imag = in_real * sin_s + in_imag * cos_s
    group = 16
    for g in range(blocks // group):
        for pair in range(group // 2):
            parts = []
            for b in (g * group + 2 * pair, g * group + 2 * pair + 1):
                cos_b = block_ref[0, pl.ds(b, 1), :]
                sin_b = block_ref[1, pl.ds(b, 1), :]
                parts.append(
                    jnp.concatenate(
                        [real * cos_b - imag * sin_b, real * sin_b + imag * cos_b], axis=1
                    )
                )
            turned_ref[pl.ds((g * group + 2 * pair) * 8, 16), :] = jnp.concatenate(
                parts, axis=0
            ).astype(jnp.bfloat16)
        rows = pl.ds(g * group * 8, group * 8)
        part = jnp.dot(turned_ref[rows, :], table_ref[...], preferred_element_type=jnp.float32)

        @pl.when(step == 0)
        def _():
            sum_ref[rows, :] = part

        @pl.when(step > 0)
        def _():
            sum_ref[rows, :] += part

    @pl.when(step == pl.num_programs(0) - 1)
    def _():
        for b in range(blocks):
            out_ref[:, pl.ds(b * INNER, INNER)] = sum_ref[pl.ds(8 * b, 8), :]


def inverse(where, mixed, table, block_turn, start_turn, time_dev):
    owners, chan_dev, _ = mixed.shape
    blocks = time_dev // INNER
    chunks = MODES // CHUNK
    return pl.pallas_call(
        inverse_kernel,
        grid_spec=pltpu.PrefetchScalarGridSpec(
            num_scalar_prefetch=1,
            grid=(chunks,),
            in_specs=[
                pl.BlockSpec((owners // chunks, chan_dev, 128), lambda i, w: (i, 0, 0)),
                pl.BlockSpec((2 * CHUNK, INNER), lambda i, w: (i, 0)),
                pl.BlockSpec((2, blocks, CHUNK), lambda i, w: (0, 0, i)),
                pl.BlockSpec((1, 2, CHUNK), lambda i, w: (w[0], 0, i)),
            ],
            out_specs=pl.BlockSpec((chan_dev, time_dev), lambda i, w: (0, 0)),
            scratch_shapes=[
                pltpu.VMEM((blocks * chan_dev, 2 * CHUNK), jnp.bfloat16),
                pltpu.VMEM((blocks * chan_dev, INNER), jnp.float32),
            ],
        ),
        out_shape=jax.ShapeDtypeStruct((chan_dev, time_dev), jnp.float32),
        compiler_params=pltpu.CompilerParams(vmem_limit_bytes=24 << 20),
        cost_estimate=pl.CostEstimate(
            flops=4 * chan_dev * time_dev * MODES, bytes_accessed=6 << 20, transcendentals=0
        ),
        name="inverse_modes",
    )(where, mixed, table, block_turn, start_turn)


def mix_kernel(where_ref, spec_ref, weight_ref, scale_ref, out_ref, turned_ref, mixed_ref):
    chan = where_ref[0]
    turned_ref[...] = spec_ref[...].astype(jnp.float32).T
    mixed_ref[...] = jnp.zeros_like(mixed_ref)
    block_modes = weight_ref.shape[0]
    for m in range(block_modes):
        re_row = turned_ref[pl.ds(chan * block_modes + m, 1), :]
        im_row = turned_ref[pl.ds(64 + chan * block_modes + m, 1), :]
        both = jnp.concatenate([re_row, im_row, jnp.zeros((6, 128), jnp.float32)], axis=0).astype(
            jnp.bfloat16
        )
        by_real = jnp.dot(both, weight_ref[m, 0], preferred_element_type=jnp.float32)
        by_imag = jnp.dot(both, weight_ref[m, 1], preferred_element_type=jnp.float32)
        mode = chan * block_modes + m
        scale = scale_ref[pl.ds(mode, 1), :]
        mixed_ref[pl.ds(mode, 1), :] = (by_real[0:1] - by_imag[1:2]) * scale
        mixed_ref[pl.ds(64 + mode, 1), :] = (by_imag[0:1] + by_real[1:2]) * scale
    out_ref[...] = mixed_ref[...].T.astype(out_ref.dtype)


def mix(chan, spec, weight, scale):
    return pl.pallas_call(
        mix_kernel,
        in_specs=[
            pl.BlockSpec(memory_space=pltpu.SMEM),
            pl.BlockSpec(memory_space=pltpu.VMEM),
            pl.BlockSpec(memory_space=pltpu.VMEM),
            pl.BlockSpec(memory_space=pltpu.VMEM),
        ],
        out_specs=pl.BlockSpec(memory_space=pltpu.VMEM),
        scratch_shapes=[pltpu.VMEM((128, 128), jnp.float32), pltpu.VMEM((128, 128), jnp.float32)],
        out_shape=jax.ShapeDtypeStruct((128, 128), jnp.bfloat16),
        compiler_params=pltpu.CompilerParams(vmem_limit_bytes=16 << 20),
        name="mix_modes",
    )(chan, spec, weight, scale)


def shards(records, spectral_weight, skip_weight, skip_bias):
    groups, chan_dev, time_dev = records.shape
    tm_count = lax.axis_size("tm")
    chan_count = lax.axis_size("chan")
    steps_all = time_dev * tm_count
    forward_table, inverse_table, block_turn, start_turn = tables(steps_all, time_dev)
    owner_modes = MODES // tm_count
    time_index = lax.axis_index("tm").astype(jnp.int32).reshape(1)
    chan_index = lax.axis_index("chan").astype(jnp.int32).reshape(1)
    x = records.reshape(chan_dev, time_dev)

    gathered = lax.all_gather(x, "chan", axis=0, tiled=True)

    partial = forward(time_index, x, forward_table, block_turn, start_turn)
    arrived = lax.all_to_all(partial, "tm", 0, 0, tiled=True)
    spectrum = jnp.sum(arrived.astype(jnp.float32), axis=0).astype(jnp.bfloat16)
    spectrum = jnp.broadcast_to(spectrum[None], (chan_count, chan_dev, 128))
    spectrum = lax.all_to_all(spectrum, "chan", 0, 0, tiled=True).reshape(128, 128)

    own = lax.axis_index("tm") * owner_modes + jnp.arange(owner_modes, dtype=jnp.int32)
    scale = jnp.where(own == 0, 1.0, 2.0).astype(jnp.float32) / steps_all
    scale = jnp.broadcast_to(scale[:, None], (owner_modes, 128))
    mixed = mix(chan_index, spectrum, spectral_weight, scale)
    mixed = lax.all_to_all(mixed.reshape(chan_count, chan_dev, 128), "chan", 0, 0, tiled=True)
    mixed = jnp.sum(mixed.astype(jnp.float32), axis=0).astype(jnp.bfloat16)
    mixed = jnp.broadcast_to(mixed[None], (tm_count, chan_dev, 128))
    mixed = lax.all_to_all(mixed, "tm", 0, 0, tiled=True)

    spectral = inverse(time_index, mixed, inverse_table, block_turn, start_turn, time_dev)
    skip = jnp.dot(skip_weight, gathered, preferred_element_type=jnp.float32)
    combined = spectral + skip + skip_bias[:, None]
    out = jax.nn.gelu(combined, approximate=False).astype(jnp.bfloat16)
    return out.reshape(groups, chan_dev, time_dev)


def solution(mesh):
    return jax.shard_map(
        shards,
        mesh=mesh,
        in_specs=(
            P(None, "chan", "tm"),
            P(("tm", "chan"), None, None, None),
            P("chan", None),
            P("chan"),
        ),
        out_specs=P(None, "chan", "tm"),
        check_vma=False,
    )
```

time: 414 us -> 107 us (0.26); the launches traced: 407 us -> 106 us
  waiting for transfers between devices: 231 us -> 17.2 us
  other arithmetic: 28 us -> 0.06 us
  local copies, waits for them, and re-layouts: 31.6 us -> 8.4 us
  matrix products: 27.9 us -> 6.97 us
  blocking collectives: 40.7 us -> 22.3 us
  loops' own time: 16 us -> 0 us
  Pallas kernels: 0 us -> 14.7 us
  starting transfers between devices: 17 us -> 22.9 us
    unnamed x3 -> x1, waiting for transfers between devices: 219 us -> 0.71 us
    all_gather x1 -> x0, blocking collectives: 40.7 us -> none  [shards(): all_modes = lax.all_gather(mixed, 'tm', axis=3, tiled=True)]
    all_to_all x0 -> x2, blocking collectives: none -> 22.3 us  [the longest x1 11.8 us: shards(): mixed = lax.all_to_all(mixed, 'tm', 0, 0, tiled=True)]
    dot_general x29 -> x1, matrix products: 27.9 us -> 6.97 us  [shards(): skip = jnp.dot(skip_weight, gathered, preferred_element_type=jnp.float32)]
    dynamic_slice x24 -> x0, local copies, waits for them, and re-layouts: 16.6 us -> none  [the longest x16 9.84 us: shards(): lax.scan(forward_turn, (zero_modes, zero_modes), turn_ids)]
    another operation x2 -> x0, loops' own time: 16 us -> none  [the longest x1 10.4 us: shards(): lax.scan(forward_turn, (zero_modes, zero_modes), turn_ids)]
    pallas_call x0 -> x3, Pallas kernels: none -> 14.7 us  [the longest x1 8.97 us: inverse(): pl.pallas_call(inverse_kernel, grid_spec=pltpu.PrefetchScalarGridSpec(num...]
    cos x16 -> x0, other arithmetic: 9.53 us -> none  [twiddles(): return (jnp.cos(angle), jnp.sin(angle))]
  transfers between devices with their start and end apart: 4 -> 3, of which waited for: 3 -> 2; matrix products, arithmetic and copies ran while one was open for 9% -> 1% of each run, Pallas kernels for 0% -> 14%
where the time goes in v1:
time: 107 us; the launch traced here: 106 us
  starting transfers between devices  22.9 us (21%)
  blocking collectives  22.3 us (21%)
  waiting for transfers between devices  17.2 us (16%)
  Pallas kernels  14.7 us (14%)
  between operations  13.5 us (13%)
  local copies, waits for them, and re-layouts  8.4 us (8%)
  matrix products  6.97 us (7%)
    all_to_all x1, starting transfers between devices, shards(): lax.all_to_all(spectrum, 'chan', 0, 0, tiled=True).reshape(128, 128)  12.4 us
    all_to_all x1, blocking collectives, shards(): mixed = lax.all_to_all(mixed, 'tm', 0, 0, tiled=True)  11.8 us
    all_to_all x1, starting transfers between devices, shards(): arrived = lax.all_to_all(partial, 'tm', 0, 0, tiled=True)  10.5 us
    all_to_all x1, blocking collectives, shards(): lax.all_to_all(mixed.reshape(chan_count, chan_dev, 128), 'chan', 0, 0, ti...  10.4 us
    pallas_call x1, Pallas kernels, inverse(): pl.pallas_call(inverse_kernel, grid_spec=pltpu.PrefetchScalarGridSpec(num...  8.97 us
    all_to_all x1, waiting for transfers between devices, shards(): arrived = lax.all_to_all(partial, 'tm', 0, 0, tiled=True)  8.82 us
    unnamed x20, local copies, waits for them, and re-layouts  7.7 us
    all_to_all x1, waiting for transfers between devices, shards(): lax.all_to_all(spectrum, 'chan', 0, 0, tiled=True).reshape(128, 128)  7.67 us
  transfers between devices with their start and end apart: 3, of which 2 were waited for; matrix products, arithmetic and copies ran while one was open for 1% of the time, Pallas kernels for 14%

profile of v1, /device:TPU:1, one launch (start us, length us, event | category | flops | bytes accessed | tf_op | source)
XLA Modules:
  0.0 106.0 jit_solution(12130715043663169935)
XLA Ops:
  6.5 0.0 copy-start
  6.5 0.0 all-gather.3.cloned.1.call-start
  6.5 0.7 all-gather.3.cloned.1.call-update
  7.3 0.0 copy-start.1
  7.3 1.0 copy-done.1
  8.3 2.2 %copy-done.4 = bf16[512,4096]{1,0:T(8,128)(2,1)S(1)} copy-done((bf16[512,4096]{1,0:T(8,128)(2,1)S(1)}, bf16[512,4096]{1,0:T(8,128)(2,1)}, u32[]{:S(2)}) %copy-start.4) | copy-done | bytes 4194328
  10.5 1.2 %copy-done.5 = f32[2,64,2048]{2,1,0:T(8,128)S(1)} copy-done((f32[2,64,2048]{2,1,0:T(8,128)S(1)}, f32[2,64,2048]{2,1,0:T(8,128)}, u32[]{:S(2)}) %copy-start.5) | copy-done | bytes 1048600
  11.7 1.0 copy-done.7
  12.8 5.4 %forward_modes.1 = bf16[32,8,128]{2,1,0:T(8,128)(2,1)} custom-call(s32[1]{0:T(128)} %bitcast.where_ref, bf16[8,32768]{1,0:T(8,128)(2,1)S(1)} %bitcast.15, bf16[512,4096]{1,0:T(8,128)(2,1)S(1)} %copy-done.4, f32[2,64,2048]{2,1,0:T(8,128)S(1)} %copy-done.5, f32[32,2,2048]{2,1,0:T(2,128)S(1)} %copy-done.7), custom_call_target="tpu_custom_call" | custom-call | flops 2147483648 | bytes 6291456 | tf_op jit(solution)/shard_map/forward_modes/pallas_call | solution.py:87
  18.1 10.5 %all-to-all-start = ((bf16[32,8,128]{2,1,0:T(8,128)(2,1)}), bf16[32,8,128]{2,1,0:T(8,128)(2,1)S(1)}, u32[]{:S(2)}, u32[]{:S(2)}) async-start(bf16[32,8,128]{2,1,0:T(8,128)(2,1)} %forward_modes.1), calls=%async_computation | async-start | bytes 131072 | tf_op jit(solution)/shard_map/all_to_all | solution.py:240
  28.6 8.8 %all-to-all-done = bf16[32,8,128]{2,1,0:T(8,128)(2,1)S(1)} async-done(((bf16[32,8,128]{2,1,0:T(8,128)(2,1)}), bf16[32,8,128]{2,1,0:T(8,128)(2,1)S(1)}, u32[]{:S(2)}, u32[]{:S(2)}) %all-to-all-start) | async-done | bytes 65568 | tf_op jit(solution)/shard_map/all_to_all | solution.py:240
  37.5 0.6 broadcast_in_dim.14
  38.1 12.4 %all-to-all-start.1 = ((bf16[16,8,128]{2,1,0:T(8,128)(2,1)}), bf16[16,8,128]{2,1,0:T(8,128)(2,1)S(1)}, u32[]{:S(2)}, u32[]{:S(2)}) async-start(bf16[16,8,128]{2,1,0:T(8,128)(2,1)} %broadcast_in_dim.14), calls=%async_computation.1 | async-start | bytes 65536 | tf_op jit(solution)/shard_map/all_to_all | solution.py:243
  50.6 7.7 %all-to-all-done.1 = bf16[16,8,128]{2,1,0:T(8,128)(2,1)S(1)} async-done(((bf16[16,8,128]{2,1,0:T(8,128)(2,1)}), bf16[16,8,128]{2,1,0:T(8,128)(2,1)S(1)}, u32[]{:S(2)}, u32[]{:S(2)}) %all-to-all-start.1) | async-done | bytes 32800 | tf_op jit(solution)/shard_map/all_to_all | solution.py:243
  58.2 0.1 broadcast_in_dim.30.scale_ref
  58.3 0.0 copy-done.2
  58.3 0.4 mix_modes.1
  58.7 10.4 %all_to_all.20 = bf16[16,8,128]{2,1,0:T(8,128)(2,1)S(1)} all-to-all(bf16[16,8,128]{2,1,0:T(8,128)(2,1)S(1)} %bitcast.17), channel_id=1, replica_groups=mesh['tm'=32,'chan'=16] {'chan'}, dimensions={0} | all-to-all | bytes 65536 | tf_op jit(solution)/shard_map/all_to_all | solution.py:249
  69.2 11.8 %all_to_all.21.mixed_ref = bf16[32,8,128]{2,1,0:T(8,128)(2,1)S(1)} all-to-all(bf16[32,8,128]{2,1,0:T(8,128)(2,1)S(1)} %broadcast_in_dim.31), channel_id=1, replica_groups=mesh['tm'=32,'chan'=16] {'tm'}, dimensions={0} | all-to-all | bytes 131072 | tf_op jit(solution)/shard_map/all_to_all | solution.py:252
  81.0 0.0 copy-done.6
  81.0 2.2 %copy-done.3 = bf16[4096,512]{1,0:T(8,128)(2,1)S(1)} copy-done((bf16[4096,512]{1,0:T(8,128)(2,1)S(1)}, bf16[4096,512]{1,0:T(8,128)(2,1)}, u32[]{:S(2)}) %copy-start.3) | copy-done | bytes 4194328
  83.2 9.0 %inverse_modes.1 = f32[8,32768]{1,0:T(8,128)S(1)} custom-call(s32[1]{0:T(128)} %bitcast.where_ref, bf16[32,8,128]{2,1,0:T(8,128)(2,1)S(1)} %all_to_all.21.mixed_ref, bf16[4096,512]{1,0:T(8,128)(2,1)S(1)} %copy-done.3, f32[2,64,2048]{2,1,0:T(8,128)S(1)} %copy-done.6, f32[32,2,2048]{2,1,0:T(2,128)S(1)} %copy-done.8), custom_call_target="tpu_custom_call" | custom-call | flops 2147483648 | bytes 6291456 | tf_op jit(solution)/shard_map/inverse_modes/pallas_call | solution.py:163
  92.2 0.0 all-gather.3.cloned.1.call-done
  92.2 7.0 %fusion.14 = bf16[1,8,32768]{2,1,0:T(8,128)(2,1)} fusion(f32[8,32768]{1,0:T(8,128)S(1)} %inverse_modes.1, bf16[8,128]{1,0:T(8,128)(2,1)S(1)} %copy-done, bf16[1,128,32768]{2,1,0:T(8,128)(2,1)} %all-gather.3.cloned.1.call-done, f32[8]{0:T(128)S(1)} %copy-done.9), kind=kOutput, calls=%fused_computation.22 | convolution fusion | flops 84672512 | bytes 9963552 | tf_op jit(solution)/shard_map/dot_general | solution.py:255
  (15 shorter events, 0.1 us)
Async XLA Ops:
  6.5 85.7 %copy-start = (bf16[8,128]{1,0:T(8,128)(2,1)S(1)}, bf16[8,128]{1,0:T(8,128)(2,1)}, u32[]{:S(2)}) copy-start(bf16[8,128]{1,0:T(8,128)(2,1)} %param.10) | copy-start | bytes 6148
  6.5 51.8 %copy-start.2 = (bf16[4,2,128,128]{3,2,1,0:T(8,128)(2,1)S(1)}, bf16[4,2,128,128]{3,2,1,0:T(8,128)(2,1)}, u32[]{:S(2)}) copy-start(bf16[4,2,128,128]{3,2,1,0:T(8,128)(2,1)} %weight_ref.1) | copy-start | bytes 786436
  6.5 85.6 %all-gather.3.cloned.1.call-start = ((), (), s32[]{:S(2)}) async-start(), calls=%async_computation.4 | async-start | bytes 8912896 | tf_op jit(solution)/shard_map/all_gather | solution.py:237
  7.3 1.0 copy-start.1
  8.3 2.2 %copy-start.4 = (bf16[512,4096]{1,0:T(8,128)(2,1)S(1)}, bf16[512,4096]{1,0:T(8,128)(2,1)}, u32[]{:S(2)}) copy-start(bf16[512,4096]{1,0:T(8,128)(2,1)} %constant.90.clone.table_ref) | copy-start | bytes 12582916
  10.5 1.2 %copy-start.5 = (f32[2,64,2048]{2,1,0:T(8,128)S(1)}, f32[2,64,2048]{2,1,0:T(8,128)}, u32[]{:S(2)}) copy-start(f32[2,64,2048]{2,1,0:T(8,128)} %constant.91.clone.block_ref) | copy-start | bytes 3145732
  11.7 1.0 copy-start.7
  12.8 68.2 %copy-start.6 = (f32[2,64,2048]{2,1,0:T(8,128)S(1)}, f32[2,64,2048]{2,1,0:T(8,128)}, u32[]{:S(2)}) copy-start(f32[2,64,2048]{2,1,0:T(8,128)} %constant.91.clone.block_ref) | copy-start | bytes 3145732
  12.8 68.2 %copy-start.8 = (f32[32,2,2048]{2,1,0:T(2,128)S(1)}, f32[32,2,2048]{2,1,0:T(2,128)}, u32[]{:S(2)}) copy-start(f32[32,2,2048]{2,1,0:T(2,128)} %constant.92.clone.start_ref) | copy-start | bytes 1572868
  12.8 79.4 %copy-start.9 = (f32[8]{0:T(128)S(1)}, f32[8]{0:T(128)}, u32[]{:S(2)}) copy-start(f32[8]{0:T(128)} %param.11) | copy-start | bytes 100
  18.1 19.3 %all-to-all-start = ((bf16[32,8,128]{2,1,0:T(8,128)(2,1)}), bf16[32,8,128]{2,1,0:T(8,128)(2,1)S(1)}, u32[]{:S(2)}, u32[]{:S(2)}) async-start(bf16[32,8,128]{2,1,0:T(8,128)(2,1)} %forward_modes.1), calls=%async_computation | async-start | bytes 131072 | tf_op jit(solution)/shard_map/all_to_all | solution.py:240
  38.1 20.1 %all-to-all-start.1 = ((bf16[16,8,128]{2,1,0:T(8,128)(2,1)}), bf16[16,8,128]{2,1,0:T(8,128)(2,1)S(1)}, u32[]{:S(2)}, u32[]{:S(2)}) async-start(bf16[16,8,128]{2,1,0:T(8,128)(2,1)} %broadcast_in_dim.14), calls=%async_computation.1 | async-start | bytes 65536 | tf_op jit(solution)/shard_map/all_to_all | solution.py:243
  81.0 2.2 %copy-start.3 = (bf16[4096,512]{1,0:T(8,128)(2,1)S(1)}, bf16[4096,512]{1,0:T(8,128)(2,1)}, u32[]{:S(2)}) copy-start(bf16[4096,512]{1,0:T(8,128)(2,1)} %constant.93.clone.table_ref) | copy-start | bytes 12582916
Sparse Core Ops, SparseCore 0:
  9.5 66.6 all-gather.2

commit v2 on v1

v2 whole, which is shorter than its diff:
```python
import math

import jax
import jax.numpy as jnp
import numpy as np
from jax import lax
from jax.experimental import pallas as pl
from jax.experimental.pallas import tpu as pltpu
from jax.sharding import Mesh
from jax.sharding import PartitionSpec as P

MODES = 2048
INNER = 512
CHUNK = 256
LOW = 8
LANES = 128
OWN = 32


def mode_order(tm_count, depth, cores):
    share = MODES // (tm_count * depth * cores)
    modes = np.arange(MODES, dtype=np.int64).reshape(tm_count, depth, cores, share)
    return modes.transpose(0, 2, 1, 3).reshape(-1)


def tables(steps_all, time_dev, modes):
    tm_count = steps_all // time_dev
    blocks = time_dev // INNER

    def turn(positions):
        angle = positions[:, None] * modes[None, :] % steps_all * (2.0 * math.pi / steps_all)
        return np.cos(angle), np.sin(angle)

    inner_cos, inner_sin = turn(np.arange(INNER, dtype=np.int64))
    split = lambda a: a.reshape(INNER, MODES // CHUNK, CHUNK)
    forward = np.stack([split(inner_cos), split(inner_sin)], axis=2).reshape(INNER, 2 * MODES)
    inverse = np.stack([split(inner_cos), -split(inner_sin)], axis=2).reshape(INNER, 2 * MODES).T
    low = np.stack(turn(np.arange(LOW, dtype=np.int64) * INNER))
    high = np.stack(turn(np.arange(blocks // LOW, dtype=np.int64) * (INNER * LOW)))
    start = np.stack(turn(np.arange(tm_count, dtype=np.int64) * time_dev), axis=1)
    return (
        np.ascontiguousarray(forward).astype(jnp.bfloat16),
        np.ascontiguousarray(inverse).astype(jnp.bfloat16),
        low.astype(np.float32),
        high.astype(np.float32),
        start.astype(np.float32),
    )


def column_select(depth, cores, chan_dev):
    pick = np.zeros((cores, LANES, LANES), np.float32)
    for core in range(cores):
        for z in range(depth):
            for ch in range(chan_dev):
                pick[core, (z * cores + core) * chan_dev + ch, 64 + z * chan_dev + ch] = 1.0
    return pick.astype(jnp.bfloat16)


def lane_ids(rows):
    return lax.broadcasted_iota(jnp.int32, (rows, LANES), 1)


def transpose_kernel(w_ref, out_ref):
    for m in range(w_ref.shape[0]):
        for part in range(w_ref.shape[1]):
            out_ref[m, part] = w_ref[m, part].astype(jnp.float32).T.astype(out_ref.dtype)


def transpose_weights(weight):
    return pl.pallas_call(
        transpose_kernel,
        in_specs=[pl.BlockSpec(memory_space=pltpu.VMEM)],
        out_specs=pl.BlockSpec(memory_space=pltpu.VMEM),
        out_shape=jax.ShapeDtypeStruct(weight.shape, weight.dtype),
        name="transpose_weights",
    )(weight)


def forward_kernel(
    where_ref, x_ref, skip_ref, pick_ref, table_ref, low_ref, high_ref, start_ref, out_ref, rows_ref, picked_ref
):
    chan_dev = x_ref.shape[0]
    highs = high_ref.shape[1]
    span = LOW * chan_dev

    @pl.when(pl.program_id(0) == 0)
    def _():
        for pair in range(highs * LOW // 2):
            first = x_ref[:, pl.ds(2 * pair * INNER, INNER)].astype(jnp.float32)
            second = x_ref[:, pl.ds((2 * pair + 1) * INNER, INNER)].astype(jnp.float32)
            rows_ref[pl.ds(16 * pair, 16), :] = jnp.concatenate([first, second], axis=0).astype(
                jnp.bfloat16
            )
        for core in range(2):
            picked_ref[core] = jnp.dot(
                skip_ref[...], pick_ref[core], preferred_element_type=jnp.float32
            )

    cos_s = start_ref[0, 0:1, :]
    sin_s = start_ref[0, 1:2, :]
    high_cos = high_ref[0] * cos_s - high_ref[1] * sin_s
    high_sin = high_ref[0] * sin_s + high_ref[1] * cos_s
    real = jnp.zeros((chan_dev, CHUNK), jnp.float32)
    imag = jnp.zeros((chan_dev, CHUNK), jnp.float32)
    product = jnp.dot(rows_ref[...], table_ref[...], preferred_element_type=jnp.float32)
    for h in range(highs):
        part_real = jnp.zeros((chan_dev, CHUNK), jnp.float32)
        part_imag = jnp.zeros((chan_dev, CHUNK), jnp.float32)
        for b in range(LOW):
            row = h * span + b * chan_dev
            by_cos = product[row : row + chan_dev, :CHUNK]
            by_sin = product[row : row + chan_dev, CHUNK:]
            cos_b = low_ref[0, b : b + 1, :]
            sin_b = low_ref[1, b : b + 1, :]
            part_real = part_real + (by_cos * cos_b - by_sin * sin_b)
            part_imag = part_imag + (by_cos * sin_b + by_sin * cos_b)
        cos_h = high_cos[h : h + 1]
        sin_h = high_sin[h : h + 1]
        real = real + (part_real * cos_h - part_imag * sin_h)
        imag = imag - (part_real * sin_h + part_imag * cos_h)
    lane = lane_ids(chan_dev)
    for tile in range(CHUNK // LANES):
        re = real[:, LANES * tile : LANES * (tile + 1)]
        im = imag[:, LANES * tile : LANES * (tile + 1)]
        for q in range(LANES // OWN):
            re_q = pltpu.roll(re, (LANES - OWN * q) % LANES, 1) if q else re
            im_q = pltpu.roll(im, (OWN - OWN * q) % LANES, 1) if q != 1 else im
            own = jnp.where(lane < OWN, re_q, im_q)
            own = jnp.where(lane < 2 * OWN, own, picked_ref[q % 2])
            out_ref[4 * tile + q] = own.astype(out_ref.dtype)


def forward(where, x, skip_weight, pick, table, low, high, start):
    chan_dev, time_dev = x.shape
    chunks = MODES // CHUNK
    owners = MODES // OWN
    whole = lambda a: pl.BlockSpec(a.shape, lambda i, w: (0,) * a.ndim)
    return pl.pallas_call(
        forward_kernel,
        grid_spec=pltpu.PrefetchScalarGridSpec(
            num_scalar_prefetch=1,
            grid=(chunks,),
            in_specs=[
                whole(x),
                whole(skip_weight),
                whole(pick),
                pl.BlockSpec((INNER, 2 * CHUNK), lambda i, w: (0, i)),
                pl.BlockSpec((2, LOW, CHUNK), lambda i, w: (0, 0, i)),
                pl.BlockSpec((2, high.shape[1], CHUNK), lambda i, w: (0, 0, i)),
                pl.BlockSpec((1, 2, CHUNK), lambda i, w: (w[0], 0, i)),
            ],
            out_specs=pl.BlockSpec((owners // chunks, chan_dev, LANES), lambda i, w: (i, 0, 0)),
            scratch_shapes=[
                pltpu.VMEM((time_dev // INNER * chan_dev, INNER), jnp.bfloat16),
                pltpu.VMEM((2, chan_dev, LANES), jnp.float32),
            ],
        ),
        out_shape=jax.ShapeDtypeStruct((owners, chan_dev, LANES), jnp.bfloat16),
        cost_estimate=pl.CostEstimate(
            flops=4 * chan_dev * time_dev * MODES, bytes_accessed=6 << 20, transcendentals=0
        ),
        name="forward_modes",
    )(where, x, skip_weight, pick, table, low, high, start)


def sum_kernel(arrived_ref, spec_ref, skip_ref):
    owners = arrived_ref.shape[0]
    lane = lane_ids(arrived_ref.shape[1])
    sums, skips = [], []
    for core in range(2):
        total = arrived_ref[core].astype(jnp.float32)
        skips.append(pltpu.roll(total, 64, 1))
        for sender in range(2 + core, owners, 2):
            total = total + arrived_ref[sender].astype(jnp.float32)
        sums.append(total)
    both = jnp.where(lane < 64, sums[0], pltpu.roll(sums[1], 64, 1)).astype(spec_ref.dtype)
    for z in range(spec_ref.shape[0]):
        spec_ref[z] = both
    skip_ref[...] = jnp.concatenate(skips, axis=0).astype(skip_ref.dtype)


def sum_spectra(arrived, depth):
    _, chan_dev, _ = arrived.shape
    return pl.pallas_call(
        sum_kernel,
        in_specs=[pl.BlockSpec(memory_space=pltpu.VMEM)],
        out_specs=[pl.BlockSpec(memory_space=pltpu.VMEM)] * 2,
        out_shape=[
            jax.ShapeDtypeStruct((depth, chan_dev, LANES), jnp.bfloat16),
            jax.ShapeDtypeStruct((2 * chan_dev, LANES), jnp.bfloat16),
        ],
        compiler_params=pltpu.CompilerParams(vmem_limit_bytes=8 << 20),
        name="sum_spectra",
    )(arrived)


def mix_kernel(where_ref, spec_ref, weight_ref, out_ref, held_ref, sem, *, steps_all):
    depth, share, _, outs, _ = held_ref.shape
    copy = pltpu.make_async_copy(
        weight_ref.at[:, :, :, pl.ds(pl.multiple_of(where_ref[0] * outs, outs), outs), :], held_ref, sem
    )
    copy.start()
    rows = []
    for z in range(depth):
        both = spec_ref[z].astype(jnp.float32)
        rows += [both, pltpu.roll(both, 64, 1)]
    spec = jnp.concatenate(rows, axis=0).astype(jnp.bfloat16)
    lane = lane_ids(outs)
    copy.wait()
    by_real = jnp.zeros((outs, LANES), jnp.float32)
    by_imag = jnp.zeros((outs, LANES), jnp.float32)
    for z in range(depth):
        held = held_ref[z].reshape(share * 2 * outs, LANES)
        product = jnp.dot(held, spec, preferred_element_type=jnp.float32)
        for m in range(share):
            here = lane % OWN == z * share + m
            row = 2 * m * outs
            by_real = jnp.where(here, product[row : row + outs], by_real)
            by_imag = jnp.where(here, product[row + outs : row + 2 * outs], by_imag)
    mixed = by_real + jnp.where(
        lane < OWN, -pltpu.roll(by_imag, LANES - OWN, 1), pltpu.roll(by_imag, OWN, 1)
    )
    zero_mode = (lane % OWN == 0) & (where_ref[1] == 0)
    mixed = mixed * jnp.where(zero_mode, 1.0 / steps_all, 2.0 / steps_all)
    half = outs // 2
    for core in range(2):
        part = mixed[core * half : (core + 1) * half].astype(out_ref.dtype)
        for p in range(out_ref.shape[0] // 2):
            out_ref[2 * p + core] = part


def mix(where, spec, weight, owners, steps_all):
    depth, chan_dev, _ = spec.shape
    share = weight.shape[1]
    return pl.pallas_call(
        lambda *refs: mix_kernel(*refs, steps_all=steps_all),
        in_specs=[
            pl.BlockSpec(memory_space=pltpu.SMEM),
            pl.BlockSpec(memory_space=pltpu.VMEM),
            pl.BlockSpec(memory_space=pltpu.HBM),
        ],
        out_specs=pl.BlockSpec(memory_space=pltpu.VMEM),
        scratch_shapes=[
            pltpu.VMEM((depth, share, 2, 2 * chan_dev, LANES), jnp.bfloat16),
            pltpu.SemaphoreType.DMA,
        ],
        out_shape=jax.ShapeDtypeStruct((owners, chan_dev, LANES), jnp.bfloat16),
        compiler_params=pltpu.CompilerParams(vmem_limit_bytes=8 << 20),
        name="mix_modes",
    )(where, spec, weight)


def skip_kernel(core_ref, weight_ref, x_ref, own_ref, other_ref):
    inputs, width = x_ref.shape
    quarter = width // 4
    weight = weight_ref[...].astype(jnp.float32)
    low = lane_ids(16) < 64
    first = jnp.where(low, weight, 0.0)
    second = pltpu.roll(first, 64, 1)
    none = jnp.zeros_like(first)
    stacked = jnp.concatenate(
        [
            jnp.concatenate([first, none], axis=1),
            jnp.concatenate([second, none], axis=1),
            jnp.concatenate([none, first], axis=1),
            jnp.concatenate([none, second], axis=1),
        ],
        axis=0,
    ).astype(jnp.bfloat16)
    x = jnp.concatenate([x_ref[:, q * quarter : (q + 1) * quarter] for q in range(4)], axis=0)
    product = jnp.dot(stacked, x, preferred_element_type=jnp.float32)
    is_first = core_ref[0] == 0
    for q in range(4):
        core0 = product[16 * q : 16 * q + 8]
        core1 = product[16 * q + 8 : 16 * q + 16]
        own_ref[:, q * quarter : (q + 1) * quarter] = jnp.where(is_first, core0, core1)
        other_ref[:, q * quarter : (q + 1) * quarter] = jnp.where(is_first, core1, core0).astype(
            other_ref.dtype
        )


def skip_parts(core, weight, x):
    inputs, time_dev = x.shape
    width = 4096
    return pl.pallas_call(
        skip_kernel,
        grid=(time_dev // width,),
        in_specs=[
            pl.BlockSpec(memory_space=pltpu.SMEM),
            pl.BlockSpec(weight.shape, lambda i: (0, 0)),
            pl.BlockSpec((inputs, width), lambda i: (0, i)),
        ],
        out_specs=[pl.BlockSpec((8, width), lambda i: (0, i))] * 2,
        out_shape=[
            jax.ShapeDtypeStruct((8, time_dev), jnp.float32),
            jax.ShapeDtypeStruct((8, time_dev), jnp.bfloat16),
        ],
        cost_estimate=pl.CostEstimate(
            flops=2 * 16 * inputs * time_dev, bytes_accessed=6 << 20, transcendentals=0
        ),
        name="skip_parts",
    )(core, weight, x)


def inverse_kernel(
    where_ref,
    mixed_ref,
    table_ref,
    low_ref,
    high_ref,
    start_ref,
    own_ref,
    other_ref,
    bias_ref,
    out_ref,
    turned_ref,
    sum_ref,
):
    chan_dev = own_ref.shape[0]
    highs = high_ref.shape[1]
    span = LOW * chan_dev
    step = pl.program_id(0)
    lane = lane_ids(chan_dev)
    reals, imags = [], []
    for tile in range(CHUNK // LANES):
        re = im = None
        for q in range(LANES // OWN):
            block = mixed_ref[4 * tile + q].astype(jnp.float32)
            re_q = pltpu.roll(block, OWN * q, 1) if q else block
            im_q = pltpu.roll(block, (OWN * q - OWN) % LANES, 1) if q != 1 else block
            re = re_q if q == 0 else jnp.where(lane // OWN == q, re_q, re)
            im = im_q if q == 0 else jnp.where(lane // OWN == q, im_q, im)
        reals.append(re)
        imags.append(im)
    real = jnp.concatenate(reals, axis=1)
    imag = jnp.concatenate(imags, axis=1)
    cos_s = start_ref[0, 0:1, :]
    sin_s = start_ref[0, 1:2, :]
    high_cos = high_ref[0] * cos_s - high_ref[1] * sin_s
    high_sin = high_ref[0] * sin_s + high_ref[1] * cos_s
    for h in range(highs):
        cos_h = high_cos[h : h + 1]
        sin_h = high_sin[h : h + 1]
        real_h = real * cos_h - imag * sin_h
        imag_h = real * sin_h + imag * cos_h
        for pair in range(LOW // 2):
            parts = []
            for b in (2 * pair, 2 * pair + 1):
                cos_b = low_ref[0, b : b + 1, :]
                sin_b = low_ref[1, b : b + 1, :]
                parts.append(
                    jnp.concatenate(
                        [real_h * cos_b - imag_h * sin_b, real_h * sin_b + imag_h * cos_b], axis=1
                    )
                )
            turned_ref[pl.ds(h * span + 2 * pair * chan_dev, 2 * chan_dev), :] = jnp.concatenate(
                parts, axis=0
            ).astype(jnp.bfloat16)
    product = jnp.dot(turned_ref[...], table_ref[...], preferred_element_type=jnp.float32)

    @pl.when(step == 0)
    def _():
        sum_ref[...] = product

    @pl.when(step > 0)
    def _():
        sum_ref[...] += product

    @pl.when(step == pl.num_programs(0) - 1)
    def _():
        bias = bias_ref[...][:, :1]
        for b in range(highs * LOW):
            cols = pl.ds(b * INNER, INNER)
            total = sum_ref[pl.ds(b * chan_dev, chan_dev), :] + (
                own_ref[:, cols] + other_ref[:, cols].astype(jnp.float32)
            )
            total = total + bias
            gelu = 0.5 * total * (1.0 + lax.erf(total * math.sqrt(0.5)))
            out_ref[:, cols] = gelu.astype(out_ref.dtype)


def inverse(where, mixed, table, low, high, start, own, other, bias):
    owners, chan_dev, _ = mixed.shape
    time_dev = own.shape[1]
    chunks = MODES // CHUNK
    rows = time_dev // INNER * chan_dev
    whole = lambda a: pl.BlockSpec(a.shape, lambda i, w: (0,) * a.ndim)
    return pl.pallas_call(
        inverse_kernel,
        grid_spec=pltpu.PrefetchScalarGridSpec(
            num_scalar_prefetch=1,
            grid=(chunks,),
            in_specs=[
                pl.BlockSpec((owners // chunks, chan_dev, LANES), lambda i, w: (i, 0, 0)),
                pl.BlockSpec((2 * CHUNK, INNER), lambda i, w: (i, 0)),
                pl.BlockSpec((2, LOW, CHUNK), lambda i, w: (0, 0, i)),
                pl.BlockSpec((2, high.shape[1], CHUNK), lambda i, w: (0, 0, i)),
                pl.BlockSpec((1, 2, CHUNK), lambda i, w: (w[0], 0, i)),
                whole(own),
                whole(other),
                whole(bias),
            ],
            out_specs=pl.BlockSpec((chan_dev, time_dev), lambda i, w: (0, 0)),
            scratch_shapes=[
                pltpu.VMEM((rows, 2 * CHUNK), jnp.bfloat16),
                pltpu.VMEM((rows, INNER), jnp.float32),
            ],
        ),
        out_shape=jax.ShapeDtypeStruct((chan_dev, time_dev), jnp.bfloat16),
        cost_estimate=pl.CostEstimate(
            flops=4 * chan_dev * time_dev * MODES, bytes_accessed=6 << 20, transcendentals=0
        ),
        name="inverse_modes",
    )(where, mixed, table, low, high, start, own, other, bias)


def shards(records, spectral_weight, skip_weight, skip_bias):
    groups, chan_dev, time_dev = records.shape
    tm_count = lax.axis_size(("y", "x"))
    depth = lax.axis_size("z")
    cores = lax.axis_size("core")
    steps_all = time_dev * tm_count
    modes = mode_order(tm_count, depth, cores)
    forward_table, inverse_table, low, high, start = tables(steps_all, time_dev, modes)
    pick = column_select(depth, cores, chan_dev)
    time_index = lax.axis_index(("y", "x")).astype(jnp.int32)
    core_index = lax.axis_index("core").astype(jnp.int32)
    z_index = lax.axis_index("z").astype(jnp.int32)
    x = records.reshape(chan_dev, time_dev)

    turned, x_late = lax.optimization_barrier((transpose_weights(spectral_weight), x))
    weights = lax.all_gather(turned, "z", axis=0, tiled=False)
    gathered = lax.all_gather(x_late, "z", axis=0, tiled=True)

    where = time_index.reshape(1)
    partial = forward(where, x, skip_weight, pick, forward_table, low, high, start)
    arrived = lax.all_to_all(partial, ("y", "x", "core"), 0, 0, tiled=True)
    spectrum, skip_rows = sum_spectra(arrived, depth)
    spectrum = lax.all_to_all(spectrum, "z", 0, 0, tiled=True)
    mix_where = jnp.stack([z_index, time_index * cores + core_index])
    mixed = mix(mix_where, spectrum, weights, tm_count * cores, steps_all)
    skip_rows, mixed = lax.optimization_barrier((skip_rows, mixed))
    mixed = lax.all_to_all(mixed, ("y", "x", "core"), 0, 0, tiled=True)

    own, other = skip_parts(core_index.reshape(1), skip_rows, gathered)
    other = lax.ppermute(other, "core", [(0, 1), (1, 0)])
    bias = jnp.broadcast_to(skip_bias[:, None], (chan_dev, LANES))
    out = inverse(where, mixed, inverse_table, low, high, start, own, other, bias)
    return out.reshape(groups, chan_dev, time_dev)


def solution(mesh):
    fine = Mesh(mesh.devices.reshape(8, 4, 8, 2), ("y", "x", "z", "core"))
    return jax.shard_map(
        shards,
        mesh=fine,
        in_specs=(
            P(None, ("z", "core"), ("y", "x")),
            P(("y", "x", "z", "core"), None, None, None),
            P(("z", "core"), None),
            P(("z", "core")),
        ),
        out_specs=P(None, ("z", "core"), ("y", "x")),
        check_vma=False,
    )
```

time: 107 us -> 166 us (1.55)
  waiting for transfers between devices: 17.2 us -> 75.5 us
  Pallas kernels: 14.7 us -> 27.7 us
  matrix products: 6.97 us -> 0 us
  local copies, waits for them, and re-layouts: 8.4 us -> 2.98 us
    all_gather x1 -> x2, waiting for transfers between devices: 0.02 us -> 57.1 us  [the longest x1 57.1 us: shards(): gathered = lax.all_gather(x_late, 'z', axis=0, tiled=True)]
    pallas_call x1 -> x4, Pallas kernels: 0.37 us -> 10.2 us  [the longest x1 6.69 us: skip_parts(): pl.pallas_call(skip_kernel, grid=(time_dev // width,), in_specs=[pl.Block...]
    dot_general x1 -> x0, matrix products: 6.97 us -> none  [shards(): skip = jnp.dot(skip_weight, gathered, preferred_element_type=jnp.float32)]
    unnamed x20 -> x8, local copies, waits for them, and re-layouts: 7.7 us -> 2.26 us
    pallas_call x1, Pallas kernels: 5.36 us -> 8.24 us  [forward(): pl.pallas_call(forward_kernel, grid_spec=pltpu.PrefetchScalarGridSpec(num...]
    ppermute x0 -> x1, starting transfers between devices: none -> 2.57 us  [shards(): other = lax.ppermute(other, 'core', [(0, 1), (1, 0)])]
    all_to_all x2 -> x1, blocking collectives: 22.3 us -> 20.8 us  [shards(): mixed = lax.all_to_all(mixed, ('y', 'x', 'core'), 0, 0, tiled=True)]
  transfers between devices with their start and end apart: 3 -> 5, of which waited for: 2 -> 3; matrix products, arithmetic and copies ran while one was open for 1% -> 0% of each run, Pallas kernels for 14% -> 6%
where the time goes in v2:
time: 166 us; the launch traced here: 165 us
  waiting for transfers between devices  75.5 us (45%)
  Pallas kernels  27.7 us (17%)
  starting transfers between devices  24.4 us (15%)
  blocking collectives  20.8 us (13%)
  between operations  13.5 us (8%)
  local copies, waits for them, and re-layouts  2.98 us (2%)
    all_gather x1, waiting for transfers between devices, shards(): gathered = lax.all_gather(x_late, 'z', axis=0, tiled=True)  57.1 us
    all_to_all x1, blocking collectives, shards(): mixed = lax.all_to_all(mixed, ('y', 'x', 'core'), 0, 0, tiled=True)  20.8 us
    all_to_all x1, starting transfers between devices, shards(): arrived = lax.all_to_all(partial, ('y', 'x', 'core'), 0, 0, tiled=True)  11.8 us
    all_to_all x1, waiting for transfers between devices, shards(): arrived = lax.all_to_all(partial, ('y', 'x', 'core'), 0, 0, tiled=True)  11.1 us
    all_to_all x1, starting transfers between devices, shards(): spectrum = lax.all_to_all(spectrum, 'z', 0, 0, tiled=True)  10 us
    pallas_call x1, Pallas kernels, inverse(): pl.pallas_call(inverse_kernel, grid_spec=pltpu.PrefetchScalarGridSpec(num...  9.3 us
    pallas_call x1, Pallas kernels, forward(): pl.pallas_call(forward_kernel, grid_spec=pltpu.PrefetchScalarGridSpec(num...  8.24 us
    pallas_call x1, Pallas kernels, skip_parts(): pl.pallas_call(skip_kernel, grid=(time_dev // width,), in_specs=[pl.Block...  6.69 us
  transfers between devices with their start and end apart: 5, of which 3 were waited for; matrix products, arithmetic and copies ran while one was open for 0% of the time, Pallas kernels for 6%

profile of v2, /device:TPU:1, one launch (start us, length us, event | category | flops | bytes accessed | tf_op | source)
XLA Modules:
  0.0 164.9 jit_solution(17663232115735455634)
XLA Ops:
  6.5 0.0 all-gather.6.cloned.1.call-start
  6.5 1.8 %transpose_weights.1 = bf16[4,2,128,128]{3,2,1,0:T(8,128)(2,1)} custom-call(bf16[4,2,128,128]{3,2,1,0:T(8,128)(2,1)} %w_ref.1), custom_call_target="tpu_custom_call" | custom-call | tf_op jit(solution)/shard_map/transpose_weights/pallas_call | solution.py:70
  8.3 0.0 all-gather.6.cloned.1.call-update
  8.4 0.0 all-gather.4.cloned.1.call-start
  8.4 0.7 all-gather.4.cloned.1.call-update
  9.1 8.2 %forward_modes.1 = bf16[64,8,128]{2,1,0:T(8,128)(2,1)} custom-call(s32[1]{0:T(128)} %bitcast.where_ref, bf16[8,32768]{1,0:T(8,128)(2,1)} %bitcast.9, bf16[8,128]{1,0:T(8,128)(2,1)} %skip_ref.1, bf16[2,128,128]{2,1,0:T(8,128)(2,1)} %constant.34.clone.pick_ref, bf16[512,4096]{1,0:T(8,128)(2,1)} %constant.35.clone.table_ref, ...), custom_call_target="tpu_custom_call" | custom-call | flops 2147483648 | bytes 6291456 | tf_op jit(solution)/shard_map/forward_modes/pallas_call | solution.py:138
  17.4 11.8 %all-to-all-start = ((bf16[64,8,128]{2,1,0:T(8,128)(2,1)}), bf16[64,8,128]{2,1,0:T(8,128)(2,1)S(1)}, u32[]{:S(2)}, u32[]{:S(2)}) async-start(bf16[64,8,128]{2,1,0:T(8,128)(2,1)} %forward_modes.1), calls=%async_computation | async-start | bytes 262144 | tf_op jit(solution)/shard_map/all_to_all | solution.py:437
  29.1 11.1 %all-to-all-done.arrived_ref = bf16[64,8,128]{2,1,0:T(8,128)(2,1)S(1)} async-done(((bf16[64,8,128]{2,1,0:T(8,128)(2,1)}), bf16[64,8,128]{2,1,0:T(8,128)(2,1)S(1)}, u32[]{:S(2)}, u32[]{:S(2)}) %all-to-all-start) | async-done | bytes 131104 | tf_op jit(solution)/shard_map/all_to_all | solution.py:437
  40.2 0.7 sum_spectra.1
  40.9 0.6 copy-done.1
  41.5 10.0 %all-to-all-start.1 = ((bf16[8,8,128]{2,1,0:T(8,128)(2,1)}), bf16[8,8,128]{2,1,0:T(8,128)(2,1)S(1)}, u32[]{:S(2)}, u32[]{:S(2)}) async-start(bf16[8,8,128]{2,1,0:T(8,128)(2,1)} %get-tuple-element.14), calls=%async_computation.1 | async-start | bytes 32768 | tf_op jit(solution)/shard_map/all_to_all | solution.py:439
  51.6 0.1 pad_add_fusion.refs_0_
  51.6 6.6 %all-to-all-done.1.refs_1_ = bf16[8,8,128]{2,1,0:T(8,128)(2,1)S(1)} async-done(((bf16[8,8,128]{2,1,0:T(8,128)(2,1)}), bf16[8,8,128]{2,1,0:T(8,128)(2,1)S(1)}, u32[]{:S(2)}, u32[]{:S(2)}) %all-to-all-start.1) | async-done | bytes 16416 | tf_op jit(solution)/shard_map/all_to_all | solution.py:439
  58.2 1.6 copy-done
  59.8 1.0 mix_modes.1
  60.8 57.1 %all-gather.4.cloned.1.call-done.x_ref = bf16[64,32768]{1,0:T(8,128)(2,1)} async-done(((bf16[8,32768]{1,0:T(8,128)(2,1)}), bf16[64,32768]{1,0:T(8,128)(2,1)}) %all-gather.4.cloned.1.call-update) | async-done | bytes 4194320 | tf_op jit(solution)/shard_map/all_gather | solution.py:433
  117.9 6.7 %skip_parts.1 = (f32[8,32768]{1,0:T(8,128)}, bf16[8,32768]{1,0:T(8,128)(2,1)}) custom-call(s32[1]{0:T(128)} %bitcast.5.core_ref, bf16[16,128]{1,0:T(8,128)(2,1)} %copy-done.1, bf16[64,32768]{1,0:T(8,128)(2,1)} %all-gather.4.cloned.1.call-done.x_ref), custom_call_target="tpu_custom_call" | custom-call | flops 67108864 | bytes 6291456 | tf_op jit(solution)/shard_map/skip_parts/pallas_call | solution.py:285
  124.6 2.6 %collective-permute-start = (bf16[8,32768]{1,0:T(8,128)(2,1)}, bf16[8,32768]{1,0:T(8,128)(2,1)S(1)}, u32[]{:S(2)}, u32[]{:S(2)}) collective-permute-start(bf16[8,32768]{1,0:T(8,128)(2,1)} %get-tuple-element.20), channel_id=1, source_target_pairs={{0,1},{1,0},{2,3},{3,2},{4,5},{5,4},{6,7},{7,6},{8,9},{9,8},{10,11... | collective-permute-start | bytes 1572872 | tf_op jit(solution)/shard_map/ppermute | solution.py:446
  127.2 20.8 %all_to_all.15.mixed_ref = bf16[64,8,128]{2,1,0:T(8,128)(2,1)} all-to-all(bf16[64,8,128]{2,1,0:T(8,128)(2,1)S(1)} %mix_modes.1), channel_id=1, replica_groups=mesh['y'=8,'x'=4,'z'=8,'core'=2] {'y','x','core'}, dimensions={0} | all-to-all | bytes 262144 | tf_op jit(solution)/shard_map/all_to_all | solution.py:443
  148.0 0.0 collective-permute-done.other_ref
  148.0 0.0 copy-done.2
  148.0 0.7 broadcast_in_dim.2.bias_ref
  148.7 0.1 copy-done.3
  148.8 9.3 %inverse_modes.1 = bf16[8,32768]{1,0:T(8,128)(2,1)} custom-call(s32[1]{0:T(128)} %bitcast.where_ref, bf16[64,8,128]{2,1,0:T(8,128)(2,1)} %all_to_all.15.mixed_ref, bf16[4096,512]{1,0:T(8,128)(2,1)} %constant.39.clone.table_ref, f32[2,8,2048]{2,1,0:T(8,128)} %constant.36.clone.low_ref, f32[2,8,2048]{2,1,0:T(8,128)} %constant.37.clone.high_ref, ...), custom_call_target="tpu_custom_call" | custom-call | flops 2147483648 | bytes 6291456 | tf_op jit(solution)/shard_map/inverse_modes/pallas_call | solution.py:388
  (5 shorter events, 0.0 us)
Async XLA Ops:
  6.5 51.7 %all-gather.6.cloned.1.call-start = ((), (), s32[]{:S(2)}) async-start(), calls=%async_computation.4 | async-start | bytes 2359296 | tf_op jit(solution)/shard_map/all_gather | solution.py:432
  8.4 109.5 %all-gather.4.cloned.1.call-start = ((), (), s32[]{:S(2)}) async-start(), calls=%async_computation.3 | async-start | bytes 4718592 | tf_op jit(solution)/shard_map/all_gather | solution.py:433
  17.4 130.7 %copy-start.2 = (f32[8]{0:T(128)S(1)}, f32[8]{0:T(128)}, u32[]{:S(2)}) copy-start(f32[8]{0:T(128)} %param.13) | copy-start | bytes 100
  17.4 22.9 %all-to-all-start = ((bf16[64,8,128]{2,1,0:T(8,128)(2,1)}), bf16[64,8,128]{2,1,0:T(8,128)(2,1)S(1)}, u32[]{:S(2)}, u32[]{:S(2)}) async-start(bf16[64,8,128]{2,1,0:T(8,128)(2,1)} %forward_modes.1), calls=%async_computation | async-start | bytes 262144 | tf_op jit(solution)/shard_map/all_to_all | solution.py:437
  40.9 0.6 copy-start.1
  41.5 16.7 %all-to-all-start.1 = ((bf16[8,8,128]{2,1,0:T(8,128)(2,1)}), bf16[8,8,128]{2,1,0:T(8,128)(2,1)S(1)}, u32[]{:S(2)}, u32[]{:S(2)}) async-start(bf16[8,8,128]{2,1,0:T(8,128)(2,1)} %get-tuple-element.14), calls=%async_computation.1 | async-start | bytes 32768 | tf_op jit(solution)/shard_map/all_to_all | solution.py:439
  58.2 1.6 copy-start
  124.6 23.4 %collective-permute-start = (bf16[8,32768]{1,0:T(8,128)(2,1)}, bf16[8,32768]{1,0:T(8,128)(2,1)S(1)}, u32[]{:S(2)}, u32[]{:S(2)}) collective-permute-start(bf16[8,32768]{1,0:T(8,128)(2,1)} %get-tuple-element.20), channel_id=1, source_target_pairs={{0,1},{1,0},{2,3},{3,2},{4,5},{5,4},{6,7},{7,6},{8,9},{9,8},{10,11... | collective-permute-start | bytes 1572872 | tf_op jit(solution)/shard_map/ppermute | solution.py:446
  148.0 0.8 copy-start.3
Sparse Core Ops, SparseCore 0:
  9.4 46.1 all-gather.5
  57.7 60.1 all-gather.3

commit v3 on v0

v3 whole, which is shorter than its diff:
```python
import math

import jax
import jax.numpy as jnp
import numpy as np
from jax import lax
from jax.experimental import pallas as pl
from jax.experimental.pallas import tpu as pltpu
from jax.sharding import PartitionSpec as P

MODES = 2048
INNER = 512
CHUNK = 256
CHUNKS = MODES // CHUNK
LOW = 8
LANES = 128
HALF = 64
VMEM_LIMIT = 52 << 20


def tables(steps_all, time_dev):
    tm_count = steps_all // time_dev
    blocks = time_dev // INNER
    modes = np.arange(MODES, dtype=np.int64)

    def turn(positions):
        angle = positions[:, None] * modes[None, :] % steps_all * (2.0 * math.pi / steps_all)
        return np.cos(angle), np.sin(angle)

    inner_cos, inner_sin = turn(np.arange(INNER, dtype=np.int64))
    split = lambda a: a.reshape(INNER, CHUNKS, CHUNK).transpose(1, 0, 2)
    forward = np.concatenate([split(inner_cos), split(inner_sin)], axis=2)
    inverse = np.concatenate([split(inner_cos), -split(inner_sin)], axis=2).transpose(0, 2, 1)
    low = np.stack(turn(np.arange(LOW, dtype=np.int64) * INNER))
    high = np.stack(turn(np.arange(blocks // LOW, dtype=np.int64) * (INNER * LOW)))
    start = np.stack(turn(np.arange(tm_count, dtype=np.int64) * time_dev), axis=1)
    return (
        np.ascontiguousarray(forward).astype(jnp.bfloat16),
        np.ascontiguousarray(inverse).astype(jnp.bfloat16),
        low.astype(np.float32),
        high.astype(np.float32),
        start.astype(np.float32),
    )


def lane_ids(rows):
    return lax.broadcasted_iota(jnp.int32, (rows, LANES), 1)


def start_copies(pairs, sems):
    copies = [pltpu.make_async_copy(src, dst, sems.at[n]) for n, (src, dst) in enumerate(pairs)]
    for copy in copies:
        copy.start()
    return copies


def high_turns(high, start):
    cos_s, sin_s = start[0:1], start[1:2]
    return high[0] * cos_s - high[1] * sin_s, high[0] * sin_s + high[1] * cos_s


def forward_kernel(
    where_ref, x_hbm, table_hbm, low_hbm, high_hbm, start_hbm, out_ref,
    x_ref, table_ref, low_ref, high_ref, start_ref, rows_ref, product_ref, sems,
):
    chan_dev = x_ref.shape[0]
    highs = high_ref.shape[1]
    span = LOW * chan_dev
    time_dev = x_ref.shape[1]
    pieces = 4
    piece = time_dev // pieces
    pairs = [
        (x_hbm.at[:, pl.ds(n * piece, piece)], x_ref.at[:, pl.ds(n * piece, piece)])
        for n in range(pieces)
    ]
    pairs += [(table_hbm.at[0], table_ref.at[0])]
    pairs += [(low_hbm, low_ref), (high_hbm, high_ref), (start_hbm.at[where_ref[0]], start_ref)]
    pairs += [(table_hbm.at[n], table_ref.at[n]) for n in range(1, CHUNKS)]
    copies = start_copies(pairs, sems)
    for n in range(pieces):
        copies[n].wait()
        for pair in range(n * piece // INNER // 2, (n + 1) * piece // INNER // 2):
            first = x_ref[:, pl.ds(2 * pair * INNER, INNER)].astype(jnp.float32)
            second = x_ref[:, pl.ds((2 * pair + 1) * INNER, INNER)].astype(jnp.float32)
            rows_ref[pl.ds(16 * pair, 16), :] = jnp.concatenate([first, second], axis=0).astype(
                jnp.bfloat16
            )
    lane = lane_ids(chan_dev)

    def multiply(n):
        copies[pieces if n == 0 else pieces + 3 + n].wait()
        product_ref[n % 2] = jnp.dot(
            rows_ref[...], table_ref[n], preferred_element_type=jnp.float32
        )

    multiply(0)
    for copy in copies[pieces + 1 : pieces + 4]:
        copy.wait()
    for n in range(CHUNKS):
        if n + 1 < CHUNKS:
            multiply(n + 1)
        chunk = pl.ds(n * CHUNK, CHUNK)
        high_cos, high_sin = high_turns(high_ref[:, :, chunk], start_ref[:, chunk])
        for tile in range(CHUNK // LANES):
            cols = pl.ds(tile * LANES, LANES)
            sin_cols = pl.ds(CHUNK + tile * LANES, LANES)
            lanes = pl.ds(n * CHUNK + tile * LANES, LANES)
            low_cos = [low_ref[0, pl.ds(b, 1), lanes] for b in range(LOW)]
            low_sin = [low_ref[1, pl.ds(b, 1), lanes] for b in range(LOW)]
            real = imag = None
            for h in range(highs):
                part_real = part_imag = None
                for b in range(LOW):
                    rows = pl.ds(h * span + b * chan_dev, chan_dev)
                    by_cos = product_ref[n % 2, rows, cols]
                    by_sin = product_ref[n % 2, rows, sin_cols]
                    re = by_cos * low_cos[b] - by_sin * low_sin[b]
                    im = by_cos * low_sin[b] + by_sin * low_cos[b]
                    part_real = re if b == 0 else part_real + re
                    part_imag = im if b == 0 else part_imag + im
                cos_h = high_cos[h : h + 1, tile * LANES : (tile + 1) * LANES]
                sin_h = high_sin[h : h + 1, tile * LANES : (tile + 1) * LANES]
                re = part_real * cos_h - part_imag * sin_h
                im = part_real * sin_h + part_imag * cos_h
                real = re if h == 0 else real + re
                imag = im if h == 0 else imag + im
            imag = -imag
            owner = (n * CHUNK + tile * LANES) // HALF
            out_ref[owner] = jnp.where(lane < HALF, real, pltpu.roll(imag, HALF, 1)).astype(
                out_ref.dtype
            )
            out_ref[owner + 1] = jnp.where(lane < HALF, pltpu.roll(real, HALF, 1), imag).astype(
                out_ref.dtype
            )


def forward(where, x, table, low, high, start):
    chan_dev, time_dev = x.shape
    hbm = pl.BlockSpec(memory_space=pltpu.HBM)
    return pl.pallas_call(
        forward_kernel,
        in_specs=[pl.BlockSpec(memory_space=pltpu.SMEM)] + [hbm] * 5,
        out_specs=pl.BlockSpec(memory_space=pltpu.VMEM),
        scratch_shapes=[
            pltpu.VMEM(x.shape, x.dtype),
            pltpu.VMEM(table.shape, table.dtype),
            pltpu.VMEM(low.shape, low.dtype),
            pltpu.VMEM(high.shape, high.dtype),
            pltpu.VMEM(start.shape[1:], start.dtype),
            pltpu.VMEM((time_dev // INNER * chan_dev, INNER), jnp.bfloat16),
            pltpu.VMEM((2, time_dev // INNER * chan_dev, 2 * CHUNK), jnp.float32),
            pltpu.SemaphoreType.DMA((CHUNKS + 7,)),
        ],
        out_shape=jax.ShapeDtypeStruct((MODES // HALF, chan_dev, LANES), jnp.bfloat16),
        cost_estimate=pl.CostEstimate(
            flops=4 * chan_dev * time_dev * MODES, bytes_accessed=6 << 20, transcendentals=0
        ),
        name="forward_modes",
    )(where, x, table, low, high, start)


def inverse_kernel(
    where_ref, mixed_ref, table_hbm, low_hbm, high_hbm, start_hbm, out_ref,
    table_ref, low_ref, high_ref, start_ref, turned_ref, sum_ref, sems,
):
    chan_dev = mixed_ref.shape[1]
    highs = high_ref.shape[1]
    span = LOW * chan_dev
    pairs = [(low_hbm, low_ref), (high_hbm, high_ref), (start_hbm.at[where_ref[0]], start_ref)]
    pairs += [(table_hbm.at[n], table_ref.at[n]) for n in range(CHUNKS)]
    copies = start_copies(pairs, sems)
    lane = lane_ids(chan_dev)
    for copy in copies[:3]:
        copy.wait()

    def turn(n):
        chunk = pl.ds(n * CHUNK, CHUNK)
        high_cos, high_sin = high_turns(high_ref[:, :, chunk], start_ref[:, chunk])
        for tile in range(CHUNK // LANES):
            lanes = pl.ds(n * CHUNK + tile * LANES, LANES)
            owner = (n * CHUNK + tile * LANES) // HALF
            even = mixed_ref[owner].astype(jnp.float32)
            odd = mixed_ref[owner + 1].astype(jnp.float32)
            real = jnp.where(lane < HALF, even, pltpu.roll(odd, HALF, 1))
            imag = jnp.where(lane < HALF, pltpu.roll(even, HALF, 1), odd)
            low_cos = [low_ref[0, pl.ds(b, 1), lanes] for b in range(LOW)]
            low_sin = [low_ref[1, pl.ds(b, 1), lanes] for b in range(LOW)]
            for h in range(highs):
                cos_h = high_cos[h : h + 1, tile * LANES : (tile + 1) * LANES]
                sin_h = high_sin[h : h + 1, tile * LANES : (tile + 1) * LANES]
                real_h = real * cos_h - imag * sin_h
                imag_h = real * sin_h + imag * cos_h
                for b in range(0, LOW, 2):
                    rows = pl.ds(h * span + b * chan_dev, 2 * chan_dev)
                    re = [real_h * low_cos[c] - imag_h * low_sin[c] for c in (b, b + 1)]
                    im = [real_h * low_sin[c] + imag_h * low_cos[c] for c in (b, b + 1)]
                    turned_ref[n % 2, rows, pl.ds(tile * LANES, LANES)] = jnp.concatenate(
                        re, axis=0
                    ).astype(jnp.bfloat16)
                    turned_ref[n % 2, rows, pl.ds(CHUNK + tile * LANES, LANES)] = jnp.concatenate(
                        im, axis=0
                    ).astype(jnp.bfloat16)

    turn(0)
    for n in range(CHUNKS):
        copies[3 + n].wait()
        product = jnp.dot(turned_ref[n % 2], table_ref[n], preferred_element_type=jnp.float32)
        if n == 0:
            sum_ref[...] = product
        elif n + 1 < CHUNKS:
            sum_ref[...] += product
        else:
            for b in range(highs * LOW):
                rows = slice(b * chan_dev, (b + 1) * chan_dev)
                out_ref[:, pl.ds(b * INNER, INNER)] = sum_ref[rows, :] + product[rows, :]
        if n + 1 < CHUNKS:
            turn(n + 1)


def inverse(where, mixed, table, low, high, start, time_dev):
    owners, chan_dev, _ = mixed.shape
    rows = time_dev // INNER * chan_dev
    hbm = pl.BlockSpec(memory_space=pltpu.HBM)
    return pl.pallas_call(
        inverse_kernel,
        in_specs=[pl.BlockSpec(memory_space=pltpu.SMEM), pl.BlockSpec(memory_space=pltpu.VMEM)]
        + [hbm] * 4,
        out_specs=pl.BlockSpec(memory_space=pltpu.VMEM),
        scratch_shapes=[
            pltpu.VMEM(table.shape, table.dtype),
            pltpu.VMEM(low.shape, low.dtype),
            pltpu.VMEM(high.shape, high.dtype),
            pltpu.VMEM(start.shape[1:], start.dtype),
            pltpu.VMEM((2, rows, 2 * CHUNK), jnp.bfloat16),
            pltpu.VMEM((rows, INNER), jnp.float32),
            pltpu.SemaphoreType.DMA((CHUNKS + 3,)),
        ],
        out_shape=jax.ShapeDtypeStruct((chan_dev, time_dev), jnp.float32),
        compiler_params=pltpu.CompilerParams(vmem_limit_bytes=VMEM_LIMIT),
        cost_estimate=pl.CostEstimate(
            flops=4 * chan_dev * time_dev * MODES, bytes_accessed=6 << 20, transcendentals=0
        ),
        name="inverse_modes",
    )(where, mixed, table, low, high, start)


def sum_kernel(arrived_ref, out_ref):
    total = arrived_ref[0].astype(jnp.float32)
    for sender in range(1, arrived_ref.shape[0]):
        total = total + arrived_ref[sender].astype(jnp.float32)
    total = total.astype(out_ref.dtype)
    for receiver in range(out_ref.shape[0]):
        out_ref[receiver] = total


def sum_and_copy(arrived, copies):
    return pl.pallas_call(
        sum_kernel,
        in_specs=[pl.BlockSpec(memory_space=pltpu.VMEM)],
        out_specs=pl.BlockSpec(memory_space=pltpu.VMEM),
        out_shape=jax.ShapeDtypeStruct((copies, *arrived.shape[1:]), jnp.bfloat16),
        compiler_params=pltpu.CompilerParams(vmem_limit_bytes=4 << 20),
        name="sum_and_copy",
    )(arrived)


def mix_kernel(where_ref, spec_ref, weight_ref, out_ref, turned_ref, mixed_ref, *, steps_all):
    chan = where_ref[0]
    spec = jnp.concatenate([spec_ref[c].astype(jnp.float32) for c in range(spec_ref.shape[0])], axis=0)
    turned_ref[...] = spec.T
    mixed_ref[...] = jnp.zeros_like(mixed_ref)
    block_modes = weight_ref.shape[0]
    for m in range(block_modes):
        mode = chan * block_modes + m
        re_row = turned_ref[pl.ds(mode, 1), :]
        im_row = turned_ref[pl.ds(HALF + mode, 1), :]
        both = jnp.concatenate([re_row, im_row, jnp.zeros((6, LANES), jnp.float32)], axis=0).astype(
            jnp.bfloat16
        )
        by_real = jnp.dot(both, weight_ref[m, 0], preferred_element_type=jnp.float32)
        by_imag = jnp.dot(both, weight_ref[m, 1], preferred_element_type=jnp.float32)
        scale = jnp.where(where_ref[1] * HALF + mode == 0, 1.0 / steps_all, 2.0 / steps_all)
        mixed_ref[pl.ds(mode, 1), :] = (by_real[0:1] - by_imag[1:2]) * scale
        mixed_ref[pl.ds(HALF + mode, 1), :] = (by_imag[0:1] + by_real[1:2]) * scale
    mixed = mixed_ref[...].T.astype(out_ref.dtype)
    rows = out_ref.shape[1]
    for c in range(out_ref.shape[0]):
        out_ref[c] = mixed[c * rows : (c + 1) * rows]


def mix(where, spec, weight, steps_all):
    return pl.pallas_call(
        lambda *refs: mix_kernel(*refs, steps_all=steps_all),
        in_specs=[
            pl.BlockSpec(memory_space=pltpu.SMEM),
            pl.BlockSpec(memory_space=pltpu.VMEM),
            pl.BlockSpec(memory_space=pltpu.VMEM),
        ],
        out_specs=pl.BlockSpec(memory_space=pltpu.VMEM),
        scratch_shapes=[pltpu.VMEM((128, LANES), jnp.float32), pltpu.VMEM((128, LANES), jnp.float32)],
        out_shape=jax.ShapeDtypeStruct(spec.shape, jnp.bfloat16),
        compiler_params=pltpu.CompilerParams(vmem_limit_bytes=4 << 20),
        name="mix_modes",
    )(where, spec, weight)


def output_kernel(weight_ref, bias_ref, spectral_ref, x_hbm, out_ref, x_ref, sems):
    chan_dev, time_dev = out_ref.shape
    parts = x_ref.shape[0]
    width = time_dev // parts
    half = width // 2
    copies = start_copies(
        [(x_hbm.at[:, pl.ds(n * width, width)], x_ref.at[n]) for n in range(parts)], sems
    )
    weight = weight_ref[...].astype(jnp.float32)
    none = jnp.zeros_like(weight)
    stacked = jnp.concatenate(
        [jnp.concatenate([weight, none], axis=1), jnp.concatenate([none, weight], axis=1)], axis=0
    ).astype(jnp.bfloat16)
    bias = bias_ref[...]
    for n in range(parts):
        copies[n].wait()
        x = jnp.concatenate([x_ref[n, :, :half], x_ref[n, :, half:]], axis=0)
        skip = jnp.dot(stacked, x, preferred_element_type=jnp.float32)
        for side in range(2):
            cols = pl.ds(n * width + side * half, half)
            total = spectral_ref[:, cols] + skip[side * chan_dev : (side + 1) * chan_dev] + bias
            gelu = 0.5 * total * (1.0 + lax.erf(total * math.sqrt(0.5)))
            out_ref[:, cols] = gelu.astype(out_ref.dtype)


def output(weight, bias, spectral, x):
    chan_dev, time_dev = spectral.shape
    parts = 16
    vmem = pl.BlockSpec(memory_space=pltpu.VMEM)
    return pl.pallas_call(
        output_kernel,
        in_specs=[vmem, vmem, vmem, pl.BlockSpec(memory_space=pltpu.HBM)],
        out_specs=vmem,
        scratch_shapes=[
            pltpu.VMEM((parts, x.shape[0], time_dev // parts), x.dtype),
            pltpu.SemaphoreType.DMA((parts,)),
        ],
        out_shape=jax.ShapeDtypeStruct((chan_dev, time_dev), jnp.bfloat16),
        compiler_params=pltpu.CompilerParams(vmem_limit_bytes=VMEM_LIMIT),
        cost_estimate=pl.CostEstimate(
            flops=2 * 2 * chan_dev * x.shape[0] * time_dev, bytes_accessed=10 << 20, transcendentals=0
        ),
        name="skip_and_output",
    )(weight, bias, spectral, x)


def shards(records, spectral_weight, skip_weight, skip_bias):
    groups, chan_dev, time_dev = records.shape
    tm_count = lax.axis_size("tm")
    chan_count = lax.axis_size("chan")
    steps_all = time_dev * tm_count
    forward_table, inverse_table, low, high, start = tables(steps_all, time_dev)
    time_index = lax.axis_index("tm").astype(jnp.int32)
    chan_index = lax.axis_index("chan").astype(jnp.int32)
    where = time_index.reshape(1)
    x = records.reshape(chan_dev, time_dev)

    gathered = lax.all_gather(x, "chan", axis=0, tiled=True)

    partial = forward(where, x, forward_table, low, high, start)
    arrived = lax.all_to_all(partial, "tm", 0, 0, tiled=True)
    spectrum = sum_and_copy(arrived, chan_count)
    spectrum = lax.all_to_all(spectrum, "chan", 0, 0, tiled=True)
    mixed = mix(jnp.stack([chan_index, time_index]), spectrum, spectral_weight, steps_all)
    mixed = lax.all_to_all(mixed, "chan", 0, 0, tiled=True)
    mixed = sum_and_copy(mixed, tm_count)
    mixed = lax.all_to_all(mixed, "tm", 0, 0, tiled=True)
    spectral = inverse(where, mixed, inverse_table, low, high, start, time_dev)

    out = output(skip_weight, skip_bias[:, None], spectral, gathered)
    return out.reshape(groups, chan_dev, time_dev)


def solution(mesh):
    return jax.shard_map(
        shards,
        mesh=mesh,
        in_specs=(
            P(None, "chan", "tm"),
            P(("tm", "chan"), None, None, None),
            P("chan", None),
            P("chan"),
        ),
        out_specs=P(None, "chan", "tm"),
        check_vma=False,
    )
```

time: 414 us -> 96 us (0.23); the launches traced: 407 us -> 95.7 us
  waiting for transfers between devices: 231 us -> 26.1 us
  local copies, waits for them, and re-layouts: 31.6 us -> 0.12 us
  blocking collectives: 40.7 us -> 10.4 us
  other arithmetic: 28 us -> 0.07 us
  matrix products: 27.9 us -> 0 us
  Pallas kernels: 0 us -> 18.7 us
  loops' own time: 16 us -> 0 us
  starting transfers between devices: 17 us -> 26.8 us
    unnamed x3 -> x1, waiting for transfers between devices: 219 us -> 0.71 us
    all_gather x1 -> x0, blocking collectives: 40.7 us -> none  [shards(): all_modes = lax.all_gather(mixed, 'tm', axis=3, tiled=True)]
    dot_general x29 -> x0, matrix products: 27.9 us -> none  [the longest x1 7.18 us: shards(): jnp.einsum('oi,bit->bot', skip_weight, lax.all_gather(records, 'chan', ax...]
    pallas_call x0 -> x6, Pallas kernels: none -> 18.7 us  [the longest x1 6.47 us: forward(): pl.pallas_call(forward_kernel, in_specs=[pl.BlockSpec(memory_space=pltpu....]
    dynamic_slice x24 -> x0, local copies, waits for them, and re-layouts: 16.6 us -> none  [the longest x16 9.84 us: shards(): lax.scan(forward_turn, (zero_modes, zero_modes), turn_ids)]
    another operation x2 -> x0, loops' own time: 16 us -> none  [the longest x1 10.4 us: shards(): lax.scan(forward_turn, (zero_modes, zero_modes), turn_ids)]
    all_to_all x2 -> x3, waiting for transfers between devices: 11.7 us -> 25.3 us  [the longest x1 8.9 us: shards(): mixed = lax.all_to_all(mixed, 'tm', 0, 0, tiled=True)]
    all_to_all x0 -> x1, blocking collectives: none -> 10.4 us  [shards(): mixed = lax.all_to_all(mixed, 'chan', 0, 0, tiled=True)]
  transfers between devices with their start and end apart: 4 -> 4, of which waited for: 3 -> 3; matrix products, arithmetic and copies ran while one was open for 9% -> 0% of each run, Pallas kernels for 0% -> 14%
where the time goes in v3:
time: 96 us; the launch traced here: 95.7 us
  starting transfers between devices  26.8 us (28%)
  waiting for transfers between devices  26.1 us (27%)
  Pallas kernels  18.7 us (19%)
  between operations  13.5 us (14%)
  blocking collectives  10.4 us (11%)
    all_to_all x1, starting transfers between devices, shards(): spectrum = lax.all_to_all(spectrum, 'chan', 0, 0, tiled=True)  12.4 us
    all_to_all x1, starting transfers between devices, shards(): arrived = lax.all_to_all(partial, 'tm', 0, 0, tiled=True)  10.5 us
    all_to_all x1, blocking collectives, shards(): mixed = lax.all_to_all(mixed, 'chan', 0, 0, tiled=True)  10.4 us
    all_to_all x1, waiting for transfers between devices, shards(): mixed = lax.all_to_all(mixed, 'tm', 0, 0, tiled=True)  8.9 us
    all_to_all x1, waiting for transfers between devices, shards(): arrived = lax.all_to_all(partial, 'tm', 0, 0, tiled=True)  8.82 us
    all_to_all x1, waiting for transfers between devices, shards(): spectrum = lax.all_to_all(spectrum, 'chan', 0, 0, tiled=True)  7.6 us
    pallas_call x1, Pallas kernels, forward(): pl.pallas_call(forward_kernel, in_specs=[pl.BlockSpec(memory_space=pltpu....  6.47 us
    pallas_call x1, Pallas kernels, output(): pl.pallas_call(output_kernel, in_specs=[vmem, vmem, vmem, pl.BlockSpec(me...  5.18 us
  transfers between devices with their start and end apart: 4, of which 3 were waited for; matrix products, arithmetic and copies ran while one was open for 0% of the time, Pallas kernels for 14%

profile of v3, /device:TPU:1, one launch (start us, length us, event | category | flops | bytes accessed | tf_op | source)
XLA Modules:
  0.0 95.7 jit_solution(16677445848220824575)
XLA Ops:
  6.5 0.7 all-gather.3.cloned.1.call-update
  7.3 0.0 copy-start.2
  7.3 0.0 copy-start.3
  7.3 0.0 copy-start.4
  7.3 6.5 %forward_modes.1 = bf16[32,8,128]{2,1,0:T(8,128)(2,1)} custom-call(s32[1]{0:T(128)} %bitcast.1.where_ref, bf16[8,32768]{1,0:T(8,128)(2,1)} %bitcast.7, bf16[8,512,512]{2,1,0:T(8,128)(2,1)} %constant.19.clone.table_hbm, f32[2,8,2048]{2,1,0:T(8,128)} %constant.20.clone.low_hbm, f32[2,8,2048]{2,1,0:T(8,128)} %constant.21.clone.high_hbm, ...), custom_call_target="tpu_custom_call" | custom-call | flops 2147483648 | bytes 6291456 | tf_op jit(solution)/shard_map/forward_modes/pallas_call | solution.py:140
  13.8 10.5 %all-to-all-start = ((bf16[32,8,128]{2,1,0:T(8,128)(2,1)}), bf16[32,8,128]{2,1,0:T(8,128)(2,1)S(1)}, u32[]{:S(2)}, u32[]{:S(2)}) async-start(bf16[32,8,128]{2,1,0:T(8,128)(2,1)} %forward_modes.1), calls=%async_computation | async-start | bytes 131072 | tf_op jit(solution)/shard_map/all_to_all | solution.py:367
  24.3 8.8 %all-to-all-done.arrived_ref = bf16[32,8,128]{2,1,0:T(8,128)(2,1)S(1)} async-done(((bf16[32,8,128]{2,1,0:T(8,128)(2,1)}), bf16[32,8,128]{2,1,0:T(8,128)(2,1)S(1)}, u32[]{:S(2)}, u32[]{:S(2)}) %all-to-all-start) | async-done | bytes 65568 | tf_op jit(solution)/shard_map/all_to_all | solution.py:367
  33.1 0.7 sum_and_copy.2
  33.8 12.4 %all-to-all-start.1 = ((bf16[16,8,128]{2,1,0:T(8,128)(2,1)}), bf16[16,8,128]{2,1,0:T(8,128)(2,1)S(1)}, u32[]{:S(2)}, u32[]{:S(2)}) async-start(bf16[16,8,128]{2,1,0:T(8,128)(2,1)} %sum_and_copy.2), calls=%async_computation.1 | async-start | bytes 65536 | tf_op jit(solution)/shard_map/all_to_all | solution.py:369
  46.2 0.1 pad_add_fusion.refs_0_
  46.3 7.6 %all-to-all-done.1.refs_1_ = bf16[16,8,128]{2,1,0:T(8,128)(2,1)S(1)} async-done(((bf16[16,8,128]{2,1,0:T(8,128)(2,1)}), bf16[16,8,128]{2,1,0:T(8,128)(2,1)S(1)}, u32[]{:S(2)}, u32[]{:S(2)}) %all-to-all-start.1) | async-done | bytes 32800 | tf_op jit(solution)/shard_map/all_to_all | solution.py:369
  53.9 0.0 copy-done
  53.9 0.9 mix_modes.1
  54.8 0.0 copy-start.1
  54.8 10.4 %all_to_all.20.arrived_ref = bf16[16,8,128]{2,1,0:T(8,128)(2,1)S(1)} all-to-all(bf16[16,8,128]{2,1,0:T(8,128)(2,1)S(1)} %mix_modes.1), channel_id=1, replica_groups=mesh['tm'=32,'chan'=16] {'chan'}, dimensions={0} | all-to-all | bytes 65536 | tf_op jit(solution)/shard_map/all_to_all | solution.py:371
  65.3 0.7 sum_and_copy.3
  65.9 3.9 %all-to-all-start.3 = ((bf16[32,8,128]{2,1,0:T(8,128)(2,1)}), bf16[32,8,128]{2,1,0:T(8,128)(2,1)S(1)}, u32[]{:S(2)}, u32[]{:S(2)}) async-start(bf16[32,8,128]{2,1,0:T(8,128)(2,1)} %sum_and_copy.3), calls=%async_computation.3 | async-start | bytes 131072 | tf_op jit(solution)/shard_map/all_to_all | solution.py:373
  69.8 0.1 copy.10.bias_ref
  69.9 8.9 %all-to-all-done.3.mixed_ref = bf16[32,8,128]{2,1,0:T(8,128)(2,1)S(1)} async-done(((bf16[32,8,128]{2,1,0:T(8,128)(2,1)}), bf16[32,8,128]{2,1,0:T(8,128)(2,1)S(1)}, u32[]{:S(2)}, u32[]{:S(2)}) %all-to-all-start.3) | async-done | bytes 65568 | tf_op jit(solution)/shard_map/all_to_all | solution.py:373
  78.8 0.0 copy-done.2
  78.8 0.0 copy-done.4
  78.8 4.8 %inverse_modes.1.spectral_ref = f32[8,32768]{1,0:T(8,128)S(1)} custom-call(s32[1]{0:T(128)} %bitcast.1.where_ref, bf16[32,8,128]{2,1,0:T(8,128)(2,1)S(1)} %all-to-all-done.3.mixed_ref, bf16[8,512,512]{2,1,0:T(8,128)(2,1)} %constant.23.clone.table_hbm, f32[2,8,2048]{2,1,0:T(8,128)S(1)} %copy-done.4, f32[2,8,2048]{2,1,0:T(8,128)S(1)} %copy-done.3, ...), custom_call_target="tpu_custom_call" | custom-call | flops 2147483648 | bytes 6291456 | tf_op jit(solution)/shard_map/inverse_modes/pallas_call | solution.py:224
  83.6 0.0 all-gather.3.cloned.1.call-done
  83.7 5.2 %skip_and_output.1 = bf16[8,32768]{1,0:T(8,128)(2,1)} custom-call(bf16[8,128]{1,0:T(8,128)(2,1)S(1)} %copy-done.1, f32[8,1]{1,0:T(8,128)S(1)} %copy.10.bias_ref, f32[8,32768]{1,0:T(8,128)S(1)} %inverse_modes.1.spectral_ref, bf16[128,32768]{1,0:T(8,128)(2,1)} %bitcast.6), custom_call_target="tpu_custom_call" | custom-call | flops 134217728 | bytes 10485760 | tf_op jit(solution)/shard_map/skip_and_output/pallas_call | solution.py:336
  (6 shorter events, 0.0 us)
Async XLA Ops:
  6.5 77.1 %all-gather.3.cloned.1.call-start = ((), (), s32[]{:S(2)}) async-start(), calls=%async_computation.4 | async-start | bytes 8912896 | tf_op jit(solution)/shard_map/all_gather | solution.py:364
  7.3 46.6 %copy-start = (bf16[4,2,128,128]{3,2,1,0:T(8,128)(2,1)S(1)}, bf16[4,2,128,128]{3,2,1,0:T(8,128)(2,1)}, u32[]{:S(2)}) copy-start(bf16[4,2,128,128]{3,2,1,0:T(8,128)(2,1)} %refs_2_.1) | copy-start | bytes 786436
  7.3 62.5 %copy-start.5 = (f32[8]{0:T(128)S(1)}, f32[8]{0:T(128)}, u32[]{:S(2)}) copy-start(f32[8]{0:T(128)} %param.12) | copy-start | bytes 100
  7.3 71.5 %copy-start.2 = (f32[32,2,2048]{2,1,0:T(2,128)S(1)}, f32[32,2,2048]{2,1,0:T(2,128)}, u32[]{:S(2)}) copy-start(f32[32,2,2048]{2,1,0:T(2,128)} %constant.22.clone.start_hbm) | copy-start | bytes 1572868
  7.3 71.5 %copy-start.3 = (f32[2,8,2048]{2,1,0:T(8,128)S(1)}, f32[2,8,2048]{2,1,0:T(8,128)}, u32[]{:S(2)}) copy-start(f32[2,8,2048]{2,1,0:T(8,128)} %constant.21.clone.high_hbm) | copy-start | bytes 393220
  7.3 71.5 %copy-start.4 = (f32[2,8,2048]{2,1,0:T(8,128)S(1)}, f32[2,8,2048]{2,1,0:T(8,128)}, u32[]{:S(2)}) copy-start(f32[2,8,2048]{2,1,0:T(8,128)} %constant.20.clone.low_hbm) | copy-start | bytes 393220
  13.8 19.3 %all-to-all-start = ((bf16[32,8,128]{2,1,0:T(8,128)(2,1)}), bf16[32,8,128]{2,1,0:T(8,128)(2,1)S(1)}, u32[]{:S(2)}, u32[]{:S(2)}) async-start(bf16[32,8,128]{2,1,0:T(8,128)(2,1)} %forward_modes.1), calls=%async_computation | async-start | bytes 131072 | tf_op jit(solution)/shard_map/all_to_all | solution.py:367
  33.8 20.1 %all-to-all-start.1 = ((bf16[16,8,128]{2,1,0:T(8,128)(2,1)}), bf16[16,8,128]{2,1,0:T(8,128)(2,1)S(1)}, u32[]{:S(2)}, u32[]{:S(2)}) async-start(bf16[16,8,128]{2,1,0:T(8,128)(2,1)} %sum_and_copy.2), calls=%async_computation.1 | async-start | bytes 65536 | tf_op jit(solution)/shard_map/all_to_all | solution.py:369
  54.8 28.8 %copy-start.1 = (bf16[8,128]{1,0:T(8,128)(2,1)S(1)}, bf16[8,128]{1,0:T(8,128)(2,1)}, u32[]{:S(2)}) copy-start(bf16[8,128]{1,0:T(8,128)(2,1)} %weight_ref.1) | copy-start | bytes 6148
  65.9 12.9 %all-to-all-start.3 = ((bf16[32,8,128]{2,1,0:T(8,128)(2,1)}), bf16[32,8,128]{2,1,0:T(8,128)(2,1)S(1)}, u32[]{:S(2)}, u32[]{:S(2)}) async-start(bf16[32,8,128]{2,1,0:T(8,128)(2,1)} %sum_and_copy.3), calls=%async_computation.3 | async-start | bytes 131072 | tf_op jit(solution)/shard_map/all_to_all | solution.py:373
Sparse Core Ops, SparseCore 0:
  9.5 66.6 all-gather.2

commit v4 on v3

v4 whole, which is shorter than its diff:
```python
import math

import jax
import jax.numpy as jnp
import numpy as np
from jax import lax
from jax.experimental import pallas as pl
from jax.experimental.pallas import tpu as pltpu
from jax.sharding import PartitionSpec as P

MODES = 2048
INNER = 512
SIDE = INNER // 2
CHUNK = 256
SPAN = 512
LOW = 8
LANES = 128
HALF = 64
VMEM_LIMIT = 52 << 20


def tables(steps_all, time_dev):
    tm_count = steps_all // time_dev
    blocks = time_dev // INNER
    modes = np.arange(MODES, dtype=np.int64)

    def turn(half_steps):
        angle = half_steps[:, None] * modes[None, :] % (2 * steps_all) * (math.pi / steps_all)
        return np.cos(angle), np.sin(angle)

    inner_cos, inner_sin = turn(2 * np.arange(SIDE, dtype=np.int64) + 1)

    def split(a, width):
        return a.reshape(SIDE, MODES // width, width).transpose(1, 0, 2)

    forward = np.concatenate([split(inner_cos, CHUNK), split(inner_sin, CHUNK)], axis=2)
    inverse = np.concatenate([split(inner_cos, SPAN), split(inner_sin, SPAN)], axis=2)
    inverse = inverse.transpose(0, 2, 1)
    low = np.stack(turn(np.arange(LOW, dtype=np.int64) * (2 * INNER) + INNER - 1))
    high = np.stack(turn(np.arange(blocks // LOW, dtype=np.int64) * (2 * INNER * LOW)))
    start = np.stack(turn(np.arange(tm_count, dtype=np.int64) * (2 * time_dev)), axis=1)
    return (
        np.ascontiguousarray(forward).astype(jnp.bfloat16),
        np.ascontiguousarray(inverse).astype(jnp.bfloat16),
        low.astype(np.float32),
        high.astype(np.float32),
        start.astype(np.float32),
    )


def lane_ids(rows):
    return lax.broadcasted_iota(jnp.int32, (rows, LANES), 1)


def mirror_matrix():
    row = lax.broadcasted_iota(jnp.int32, (SIDE, SIDE), 0)
    col = lax.broadcasted_iota(jnp.int32, (SIDE, SIDE), 1)
    return jnp.where(row + col == SIDE - 1, 1.0, 0.0).astype(jnp.bfloat16)


def start_copies(pairs, sems):
    copies = [pltpu.make_async_copy(src, dst, sems.at[n]) for n, (src, dst) in enumerate(pairs)]
    for copy in copies:
        copy.start()
    return copies


def high_turns(high, start):
    cos_s, sin_s = start[0:1], start[1:2]
    return high[0] * cos_s - high[1] * sin_s, high[0] * sin_s + high[1] * cos_s


def forward_kernel(
    where_ref, x_hbm, table_hbm, low_hbm, high_hbm, start_hbm, out_ref,
    x_ref, table_ref, low_ref, high_ref, start_ref, sum_ref, diff_ref, product_ref, sems,
):
    chan_dev, time_dev = x_ref.shape
    highs = high_ref.shape[1]
    span = LOW * chan_dev
    chunks = MODES // CHUNK
    pieces = 1
    piece = time_dev // pieces
    pairs = [
        (x_hbm.at[:, pl.ds(n * piece, piece)], x_ref.at[:, pl.ds(n * piece, piece)])
        for n in range(pieces)
    ]
    pairs += [(table_hbm.at[0], table_ref.at[0])]
    pairs += [(low_hbm, low_ref), (high_hbm, high_ref), (start_hbm.at[where_ref[0]], start_ref)]
    pairs += [(table_hbm.at[n], table_ref.at[n]) for n in range(1, chunks)]
    copies = start_copies(pairs, sems)
    mirror = mirror_matrix()
    piece_rows = piece // INNER * chan_dev
    for n in range(pieces):
        copies[n].wait()
        sides = []
        for side in range(2):
            sides.append(
                jnp.concatenate(
                    [
                        x_ref[:, pl.ds(n * piece + b * INNER + side * SIDE, SIDE)].astype(jnp.float32)
                        for b in range(piece // INNER)
                    ],
                    axis=0,
                )
            )
        before = jnp.dot(sides[0].astype(jnp.bfloat16), mirror, preferred_element_type=jnp.float32)
        rows = pl.ds(n * piece_rows, piece_rows)
        sum_ref[rows, :] = (sides[1] + before).astype(jnp.bfloat16)
        diff_ref[rows, :] = (sides[1] - before).astype(jnp.bfloat16)
    lane = lane_ids(chan_dev)

    def multiply(n):
        copies[pieces if n == 0 else pieces + 3 + n].wait()
        product_ref[n % 2, :, :CHUNK] = jnp.dot(
            sum_ref[...], table_ref[n, :, :CHUNK], preferred_element_type=jnp.float32
        )
        product_ref[n % 2, :, CHUNK:] = jnp.dot(
            diff_ref[...], table_ref[n, :, CHUNK:], preferred_element_type=jnp.float32
        )

    multiply(0)
    for copy in copies[pieces + 1 : pieces + 4]:
        copy.wait()
    for n in range(chunks):
        if n + 1 < chunks:
            multiply(n + 1)
        chunk = pl.ds(n * CHUNK, CHUNK)
        high_cos, high_sin = high_turns(high_ref[:, :, chunk], start_ref[:, chunk])
        for tile in range(CHUNK // LANES):
            cols = pl.ds(tile * LANES, LANES)
            sin_cols = pl.ds(CHUNK + tile * LANES, LANES)
            lanes = pl.ds(n * CHUNK + tile * LANES, LANES)
            low_cos = [low_ref[0, pl.ds(b, 1), lanes] for b in range(LOW)]
            low_sin = [low_ref[1, pl.ds(b, 1), lanes] for b in range(LOW)]
            real = imag = None
            for h in range(highs):
                part_real = part_imag = None
                for b in range(LOW):
                    rows = pl.ds(h * span + b * chan_dev, chan_dev)
                    by_cos = product_ref[n % 2, rows, cols]
                    by_sin = product_ref[n % 2, rows, sin_cols]
                    re = by_cos * low_cos[b] - by_sin * low_sin[b]
                    im = by_cos * low_sin[b] + by_sin * low_cos[b]
                    part_real = re if b == 0 else part_real + re
                    part_imag = im if b == 0 else part_imag + im
                cos_h = high_cos[h : h + 1, tile * LANES : (tile + 1) * LANES]
                sin_h = high_sin[h : h + 1, tile * LANES : (tile + 1) * LANES]
                re = part_real * cos_h - part_imag * sin_h
                im = part_real * sin_h + part_imag * cos_h
                real = re if h == 0 else real + re
                imag = im if h == 0 else imag + im
            imag = -imag
            owner = (n * CHUNK + tile * LANES) // HALF
            out_ref[owner] = jnp.where(lane < HALF, real, pltpu.roll(imag, HALF, 1)).astype(
                out_ref.dtype
            )
            out_ref[owner + 1] = jnp.where(lane < HALF, pltpu.roll(real, HALF, 1), imag).astype(
                out_ref.dtype
            )


def forward(where, x, table, low, high, start):
    chan_dev, time_dev = x.shape
    rows = time_dev // INNER * chan_dev
    hbm = pl.BlockSpec(memory_space=pltpu.HBM)
    return pl.pallas_call(
        forward_kernel,
        in_specs=[pl.BlockSpec(memory_space=pltpu.SMEM)] + [hbm] * 5,
        out_specs=pl.BlockSpec(memory_space=pltpu.VMEM),
        scratch_shapes=[
            pltpu.VMEM(x.shape, x.dtype),
            pltpu.VMEM(table.shape, table.dtype),
            pltpu.VMEM(low.shape, low.dtype),
            pltpu.VMEM(high.shape, high.dtype),
            pltpu.VMEM(start.shape[1:], start.dtype),
            pltpu.VMEM((rows, SIDE), jnp.bfloat16),
            pltpu.VMEM((rows, SIDE), jnp.bfloat16),
            pltpu.VMEM((2, rows, 2 * CHUNK), jnp.float32),
            pltpu.SemaphoreType.DMA((MODES // CHUNK + 4,)),
        ],
        out_shape=jax.ShapeDtypeStruct((MODES // HALF, chan_dev, LANES), jnp.bfloat16),
        cost_estimate=pl.CostEstimate(
            flops=2 * chan_dev * time_dev * MODES, bytes_accessed=4 << 20, transcendentals=0
        ),
        name="forward_modes",
    )(where, x, table, low, high, start)


def inverse_kernel(
    where_ref, mixed_ref, table_hbm, low_hbm, high_hbm, start_hbm, out_ref,
    table_ref, low_ref, high_ref, start_ref, turned_ref, even_ref, odd_ref, sems,
):
    chan_dev = mixed_ref.shape[1]
    highs = high_ref.shape[1]
    span = LOW * chan_dev
    chunks = MODES // SPAN
    pairs = [(low_hbm, low_ref), (high_hbm, high_ref), (start_hbm.at[where_ref[0]], start_ref)]
    pairs += [(table_hbm.at[n], table_ref.at[n]) for n in range(chunks)]
    copies = start_copies(pairs, sems)
    lane = lane_ids(chan_dev)
    for copy in copies[:3]:
        copy.wait()

    def turn(n):
        chunk = pl.ds(n * SPAN, SPAN)
        high_cos, high_sin = high_turns(high_ref[:, :, chunk], start_ref[:, chunk])
        for tile in range(SPAN // LANES):
            lanes = pl.ds(n * SPAN + tile * LANES, LANES)
            owner = (n * SPAN + tile * LANES) // HALF
            first = mixed_ref[owner].astype(jnp.float32)
            second = mixed_ref[owner + 1].astype(jnp.float32)
            real = jnp.where(lane < HALF, first, pltpu.roll(second, HALF, 1))
            imag = jnp.where(lane < HALF, pltpu.roll(first, HALF, 1), second)
            low_cos = [low_ref[0, pl.ds(b, 1), lanes] for b in range(LOW)]
            low_sin = [low_ref[1, pl.ds(b, 1), lanes] for b in range(LOW)]
            for h in range(highs):
                cos_h = high_cos[h : h + 1, tile * LANES : (tile + 1) * LANES]
                sin_h = high_sin[h : h + 1, tile * LANES : (tile + 1) * LANES]
                real_h = real * cos_h - imag * sin_h
                imag_h = real * sin_h + imag * cos_h
                for b in range(0, LOW, 2):
                    rows = pl.ds(h * span + b * chan_dev, 2 * chan_dev)
                    re = [real_h * low_cos[c] - imag_h * low_sin[c] for c in (b, b + 1)]
                    im = [real_h * low_sin[c] + imag_h * low_cos[c] for c in (b, b + 1)]
                    turned_ref[n % 2, rows, pl.ds(tile * LANES, LANES)] = jnp.concatenate(
                        re, axis=0
                    ).astype(jnp.bfloat16)
                    turned_ref[n % 2, rows, pl.ds(SPAN + tile * LANES, LANES)] = jnp.concatenate(
                        im, axis=0
                    ).astype(jnp.bfloat16)

    turn(0)
    for n in range(chunks):
        copies[3 + n].wait()
        even = jnp.dot(
            turned_ref[n % 2, :, :SPAN], table_ref[n, :SPAN, :], preferred_element_type=jnp.float32
        )
        odd = jnp.dot(
            turned_ref[n % 2, :, SPAN:], table_ref[n, SPAN:, :], preferred_element_type=jnp.float32
        )
        if n == 0:
            even_ref[...] = even
            odd_ref[...] = odd
        elif n + 1 < chunks:
            even_ref[...] += even
            odd_ref[...] += odd
        if n + 1 < chunks:
            turn(n + 1)
    even = even_ref[...] + even
    odd = odd_ref[...] + odd
    after = even - odd
    mirrored = even + odd
    mirror = mirror_matrix()
    upper = mirrored.astype(jnp.bfloat16)
    lower = (mirrored - upper.astype(jnp.float32)).astype(jnp.bfloat16)
    before = jnp.dot(upper, mirror, preferred_element_type=jnp.float32)
    before = before + jnp.dot(lower, mirror, preferred_element_type=jnp.float32)
    for b in range(highs * LOW):
        rows = slice(b * chan_dev, (b + 1) * chan_dev)
        out_ref[:, pl.ds(b * INNER, SIDE)] = before[rows]
        out_ref[:, pl.ds(b * INNER + SIDE, SIDE)] = after[rows]


def inverse(where, mixed, table, low, high, start, time_dev):
    owners, chan_dev, _ = mixed.shape
    rows = time_dev // INNER * chan_dev
    hbm = pl.BlockSpec(memory_space=pltpu.HBM)
    return pl.pallas_call(
        inverse_kernel,
        in_specs=[pl.BlockSpec(memory_space=pltpu.SMEM), pl.BlockSpec(memory_space=pltpu.VMEM)]
        + [hbm] * 4,
        out_specs=pl.BlockSpec(memory_space=pltpu.VMEM),
        scratch_shapes=[
            pltpu.VMEM(table.shape, table.dtype),
            pltpu.VMEM(low.shape, low.dtype),
            pltpu.VMEM(high.shape, high.dtype),
            pltpu.VMEM(start.shape[1:], start.dtype),
            pltpu.VMEM((2, rows, 2 * SPAN), jnp.bfloat16),
            pltpu.VMEM((rows, SIDE), jnp.float32),
            pltpu.VMEM((rows, SIDE), jnp.float32),
            pltpu.SemaphoreType.DMA((MODES // SPAN + 3,)),
        ],
        out_shape=jax.ShapeDtypeStruct((chan_dev, time_dev), jnp.float32),
        compiler_params=pltpu.CompilerParams(vmem_limit_bytes=VMEM_LIMIT),
        cost_estimate=pl.CostEstimate(
            flops=2 * chan_dev * time_dev * MODES, bytes_accessed=4 << 20, transcendentals=0
        ),
        name="inverse_modes",
    )(where, mixed, table, low, high, start)


def mix_kernel(where_ref, spec_ref, weight_ref, out_ref, turned_ref, mixed_ref, *, steps_all):
    turned_ref[...] = spec_ref[...].astype(jnp.float32).T
    mixed_ref[...] = jnp.zeros_like(mixed_ref)
    block_modes = weight_ref.shape[0]
    for m in range(block_modes):
        mode = where_ref[1] * block_modes + m
        re_row = turned_ref[pl.ds(mode, 1), :]
        im_row = turned_ref[pl.ds(HALF + mode, 1), :]
        both = jnp.concatenate([re_row, im_row, jnp.zeros((6, LANES), jnp.float32)], axis=0).astype(
            jnp.bfloat16
        )
        by_real = jnp.dot(both, weight_ref[m, 0], preferred_element_type=jnp.float32)
        by_imag = jnp.dot(both, weight_ref[m, 1], preferred_element_type=jnp.float32)
        scale = jnp.where(where_ref[0] * HALF + mode == 0, 1.0 / steps_all, 2.0 / steps_all)
        mixed_ref[pl.ds(mode, 1), :] = (by_real[0:1] - by_imag[1:2]) * scale
        mixed_ref[pl.ds(HALF + mode, 1), :] = (by_imag[0:1] + by_real[1:2]) * scale
    out_ref[...] = mixed_ref[...].T.astype(out_ref.dtype)


def mix(where, spec, weight, steps_all):
    return pl.pallas_call(
        lambda *refs: mix_kernel(*refs, steps_all=steps_all),
        in_specs=[
            pl.BlockSpec(memory_space=pltpu.SMEM),
            pl.BlockSpec(memory_space=pltpu.VMEM),
            pl.BlockSpec(memory_space=pltpu.VMEM),
        ],
        out_specs=pl.BlockSpec(memory_space=pltpu.VMEM),
        scratch_shapes=[pltpu.VMEM((128, LANES), jnp.float32), pltpu.VMEM((128, LANES), jnp.float32)],
        out_shape=jax.ShapeDtypeStruct(spec.shape, jnp.bfloat16),
        compiler_params=pltpu.CompilerParams(vmem_limit_bytes=4 << 20),
        name="mix_modes",
    )(where, spec, weight)


def output_kernel(weight_ref, bias_ref, spectral_ref, x_hbm, out_hbm, x_ref, out_ref, sems, out_sems):
    chan_dev, time_dev = out_ref.shape
    parts = x_ref.shape[0]
    width = time_dev // parts
    half = width // 2
    copies = start_copies(
        [(x_hbm.at[:, pl.ds(n * width, width)], x_ref.at[n]) for n in range(parts)], sems
    )
    weight = weight_ref[...].astype(jnp.float32)
    none = jnp.zeros_like(weight)
    stacked = jnp.concatenate(
        [jnp.concatenate([weight, none], axis=1), jnp.concatenate([none, weight], axis=1)], axis=0
    ).astype(jnp.bfloat16)
    row = lax.broadcasted_iota(jnp.int32, (chan_dev, 1), 0)
    bias = jnp.zeros((chan_dev, 1), jnp.float32)
    for c in range(chan_dev):
        bias = jnp.where(row == c, bias_ref[c], bias)
    results = []
    for n in range(parts):
        copies[n].wait()
        x = jnp.concatenate([x_ref[n, :, :half], x_ref[n, :, half:]], axis=0)
        skip = jnp.dot(stacked, x, preferred_element_type=jnp.float32)
        for side in range(2):
            cols = pl.ds(n * width + side * half, half)
            total = spectral_ref[:, cols] + skip[side * chan_dev : (side + 1) * chan_dev] + bias
            gelu = 0.5 * total * (1.0 + lax.erf(total * math.sqrt(0.5)))
            out_ref[:, cols] = gelu.astype(out_ref.dtype)
        cols = pl.ds(n * width, width)
        result = pltpu.make_async_copy(out_ref.at[:, cols], out_hbm.at[:, cols], out_sems.at[n])
        result.start()
        results.append(result)
    for result in results:
        result.wait()


def output(weight, bias, spectral, x):
    chan_dev, time_dev = spectral.shape
    parts = 8
    vmem = pl.BlockSpec(memory_space=pltpu.VMEM)
    hbm = pl.BlockSpec(memory_space=pltpu.HBM)
    return pl.pallas_call(
        output_kernel,
        in_specs=[vmem, pl.BlockSpec(memory_space=pltpu.SMEM), vmem, hbm],
        out_specs=hbm,
        scratch_shapes=[
            pltpu.VMEM((parts, x.shape[0], time_dev // parts), x.dtype),
            pltpu.VMEM((chan_dev, time_dev), jnp.bfloat16),
            pltpu.SemaphoreType.DMA((parts,)),
            pltpu.SemaphoreType.DMA((parts,)),
        ],
        out_shape=jax.ShapeDtypeStruct((chan_dev, time_dev), jnp.bfloat16),
        compiler_params=pltpu.CompilerParams(vmem_limit_bytes=VMEM_LIMIT),
        cost_estimate=pl.CostEstimate(
            flops=2 * 2 * chan_dev * x.shape[0] * time_dev, bytes_accessed=10 << 20, transcendentals=0
        ),
        name="skip_and_output",
    )(weight, bias, spectral, x)


def sum_and_copy(arrived, copies):
    total = jnp.sum(arrived.astype(jnp.float32), axis=0).astype(jnp.bfloat16)
    return jnp.broadcast_to(total[None], (copies, *total.shape))


def shards(records, spectral_weight, skip_weight, skip_bias):
    groups, chan_dev, time_dev = records.shape
    tm_count = lax.axis_size("tm")
    chan_count = lax.axis_size("chan")
    steps_all = time_dev * tm_count
    forward_table, inverse_table, low, high, start = tables(steps_all, time_dev)
    where = jnp.stack([lax.axis_index("tm"), lax.axis_index("chan")]).astype(jnp.int32)
    x = records.reshape(chan_dev, time_dev)

    gathered = lax.all_gather(x, "chan", axis=0, tiled=True)

    partial = forward(where, x, forward_table, low, high, start)
    arrived = lax.all_to_all(partial, "tm", 0, 0, tiled=True)
    spectrum = sum_and_copy(arrived, chan_count)
    spectrum = lax.all_to_all(spectrum, "chan", 0, 0, tiled=True)
    mixed = mix(where, spectrum.reshape(-1, LANES), spectral_weight, steps_all)
    mixed = lax.all_to_all(mixed.reshape(spectrum.shape), "chan", 0, 0, tiled=True)
    mixed = sum_and_copy(mixed, tm_count)
    mixed = lax.all_to_all(mixed, "tm", 0, 0, tiled=True)
    spectral = inverse(where, mixed, inverse_table, low, high, start, time_dev)

    out = output(skip_weight, skip_bias, spectral, gathered)
    return out.reshape(groups, chan_dev, time_dev)


def solution(mesh):
    return jax.shard_map(
        shards,
        mesh=mesh,
        in_specs=(
            P(None, "chan", "tm"),
            P(("tm", "chan"), None, None, None),
            P("chan", None),
            P("chan"),
        ),
        out_specs=P(None, "chan", "tm"),
        check_vma=False,
    )
```

time: 96 us -> 93.8 us (0.977)
  blocking collectives: 10.4 us -> 61.9 us
  starting transfers between devices: 26.8 us -> 0.01 us
  waiting for transfers between devices: 26.1 us -> 0.73 us
  Pallas kernels: 18.7 us -> 16.6 us
    all_to_all x1 -> x4, blocking collectives: 10.4 us -> 61.9 us  [the longest x1 19.9 us: shards(): spectrum = lax.all_to_all(spectrum, 'chan', 0, 0, tiled=True)]
    all_to_all x3 -> x0, starting transfers between devices: 26.8 us -> none  [the longest x1 12.4 us: shards(): spectrum = lax.all_to_all(spectrum, 'chan', 0, 0, tiled=True)]
    all_to_all x3 -> x0, waiting for transfers between devices: 25.3 us -> none  [the longest x1 8.9 us: shards(): mixed = lax.all_to_all(mixed, 'tm', 0, 0, tiled=True)]
    pallas_call x3 -> x1, Pallas kernels: 6.48 us -> 5.07 us  [output(): pl.pallas_call(output_kernel, in_specs=[vmem, pl.BlockSpec(memory_space=p...]
  transfers between devices with their start and end apart: 4 -> 1, of which waited for: 3 -> 0; matrix products, arithmetic and copies ran while one was open for 0% -> 1% of each run, Pallas kernels for 14% -> 12%
where the time goes in v4:
time: 93.8 us; the launch traced here: 93.5 us
  blocking collectives  61.9 us (66%)
  Pallas kernels  16.6 us (18%)
  between operations  13.5 us (14%)
    all_to_all x1, blocking collectives, shards(): spectrum = lax.all_to_all(spectrum, 'chan', 0, 0, tiled=True)  19.9 us
    all_to_all x1, blocking collectives, shards(): arrived = lax.all_to_all(partial, 'tm', 0, 0, tiled=True)  19.4 us
    all_to_all x1, blocking collectives, shards(): mixed = lax.all_to_all(mixed, 'tm', 0, 0, tiled=True)  12.3 us
    all_to_all x1, blocking collectives, shards(): lax.all_to_all(mixed.reshape(spectrum.shape), 'chan', 0, 0, tiled=True)  10.4 us
    pallas_call x1, Pallas kernels, forward(): pl.pallas_call(forward_kernel, in_specs=[pl.BlockSpec(memory_space=pltpu....  6.01 us
    pallas_call x1, Pallas kernels, output(): pl.pallas_call(output_kernel, in_specs=[vmem, pl.BlockSpec(memory_space=p...  5.07 us
    pallas_call x1, Pallas kernels, inverse(): pl.pallas_call(inverse_kernel, in_specs=[pl.BlockSpec(memory_space=pltpu....  4.58 us
  transfers between devices with their start and end apart: 1, of which 0 were waited for; matrix products, arithmetic and copies ran while one was open for 1% of the time, Pallas kernels for 12%

profile of v4, /device:TPU:1, one launch (start us, length us, event | category | flops | bytes accessed | tf_op | source)
XLA Modules:
  0.0 93.5 jit_solution(5197901917372215594)
XLA Ops:
  6.5 0.0 all-gather.3.cloned.1.call-start
  6.5 0.7 all-gather.3.cloned.1.call-update
  7.3 0.6 pad_add_fusion.where_ref.refs_0_
  7.9 0.0 copy-start.1
  7.9 0.0 copy-start.4
  7.9 0.0 copy-start
  7.9 0.0 copy-start.3
  7.9 6.0 %forward_modes.1 = bf16[32,8,128]{2,1,0:T(8,128)(2,1)} custom-call(s32[2]{0:T(128)} %pad_add_fusion.where_ref.refs_0_, bf16[8,32768]{1,0:T(8,128)(2,1)} %bitcast.10, bf16[8,256,512]{2,1,0:T(8,128)(2,1)} %constant.23.clone.table_hbm, f32[2,8,2048]{2,1,0:T(8,128)} %constant.24.clone.low_hbm, f32[2,8,2048]{2,1,0:T(8,128)} %constant.25.clone.high_hbm, ...), custom_call_target="tpu_custom_call" | custom-call | flops 1073741824 | bytes 4194304 | tf_op jit(solution)/shard_map/forward_modes/pallas_call | solution.py:166
  13.9 19.4 %all_to_all.20 = bf16[32,8,128]{2,1,0:T(8,128)(2,1)S(1)} all-to-all(bf16[32,8,128]{2,1,0:T(8,128)(2,1)} %forward_modes.1), channel_id=1, replica_groups=mesh['tm'=32,'chan'=16] {'tm'}, dimensions={0} | all-to-all | bytes 131072 | tf_op jit(solution)/shard_map/all_to_all | solution.py:403
  33.4 19.9 %all_to_all.21 = bf16[16,8,128]{2,1,0:T(8,128)(2,1)S(1)} all-to-all(bf16[16,8,128]{2,1,0:T(8,128)(2,1)S(1)} %broadcast_in_dim.4), channel_id=1, replica_groups=mesh['tm'=32,'chan'=16] {'chan'}, dimensions={0} | all-to-all | bytes 65536 | tf_op jit(solution)/shard_map/all_to_all | solution.py:405
  53.2 0.0 copy-done.1
  53.2 0.0 copy-done.4
  53.2 0.9 mix_modes.1
  54.2 10.4 %all_to_all.22 = bf16[16,8,128]{2,1,0:T(8,128)(2,1)S(1)} all-to-all(bf16[16,8,128]{2,1,0:T(8,128)(2,1)S(1)} %bitcast.8), channel_id=1, replica_groups=mesh['tm'=32,'chan'=16] {'chan'}, dimensions={0} | all-to-all | bytes 65536 | tf_op jit(solution)/shard_map/all_to_all | solution.py:407
  64.6 0.0 copy-start.6
  64.7 12.3 %all_to_all.23.mixed_ref = bf16[32,8,128]{2,1,0:T(8,128)(2,1)S(1)} all-to-all(bf16[32,8,128]{2,1,0:T(8,128)(2,1)S(1)} %broadcast_in_dim.5), channel_id=1, replica_groups=mesh['tm'=32,'chan'=16] {'tm'}, dimensions={0} | all-to-all | bytes 131072 | tf_op jit(solution)/shard_map/all_to_all | solution.py:409
  76.9 0.0 copy-done
  76.9 0.0 copy-done.2
  76.9 0.0 copy-done.3
  76.9 4.6 %inverse_modes.1.spectral_ref = f32[8,32768]{1,0:T(8,128)S(1)} custom-call(s32[2]{0:T(128)S(1)} %copy-done.4, bf16[32,8,128]{2,1,0:T(8,128)(2,1)S(1)} %all_to_all.23.mixed_ref, bf16[4,1024,256]{2,1,0:T(8,128)(2,1)} %constant.27.clone.table_hbm, f32[2,8,2048]{2,1,0:T(8,128)S(1)} %copy-done.3, f32[2,8,2048]{2,1,0:T(8,128)S(1)} %copy-done.2, ...), custom_call_target="tpu_custom_call" | custom-call | flops 1073741824 | bytes 4194304 | tf_op jit(solution)/shard_map/inverse_modes/pallas_call | solution.py:268
  81.5 0.0 all-gather.3.cloned.1.call-done
  81.5 0.0 copy-done.5
  81.5 0.0 copy-done.6
  81.6 5.1 %skip_and_output.1 = bf16[8,32768]{1,0:T(8,128)(2,1)} custom-call(bf16[8,128]{1,0:T(8,128)(2,1)S(1)} %copy-done.5, f32[8]{0:T(128)S(1)} %copy-done.6, f32[8,32768]{1,0:T(8,128)S(1)} %inverse_modes.1.spectral_ref, bf16[128,32768]{1,0:T(8,128)(2,1)} %bitcast.9), custom_call_target="tpu_custom_call" | custom-call | flops 134217728 | bytes 10485760 | tf_op jit(solution)/shard_map/skip_and_output/pallas_call | solution.py:367
  (6 shorter events, 0.1 us)
Async XLA Ops:
  6.5 75.0 %all-gather.3.cloned.1.call-start = ((), (), s32[]{:S(2)}) async-start(), calls=%async_computation.4 | async-start | bytes 8912896 | tf_op jit(solution)/shard_map/all_gather | solution.py:400
  7.9 45.3 %copy-start.1 = (bf16[4,2,128,128]{3,2,1,0:T(8,128)(2,1)S(1)}, bf16[4,2,128,128]{3,2,1,0:T(8,128)(2,1)}, u32[]{:S(2)}) copy-start(bf16[4,2,128,128]{3,2,1,0:T(8,128)(2,1)} %refs_2_.1) | copy-start | bytes 786436
  7.9 45.3 %copy-start.4 = (s32[2]{0:T(128)S(1)}, s32[2]{0:T(128)}, u32[]{:S(2)}) copy-start(s32[2]{0:T(128)} %pad_add_fusion.where_ref.refs_0_) | copy-start | bytes 28
  7.9 69.0 %copy-start = (f32[32,2,2048]{2,1,0:T(2,128)S(1)}, f32[32,2,2048]{2,1,0:T(2,128)}, u32[]{:S(2)}) copy-start(f32[32,2,2048]{2,1,0:T(2,128)} %constant.26.clone.start_hbm) | copy-start | bytes 1572868
  7.9 69.0 %copy-start.2 = (f32[2,8,2048]{2,1,0:T(8,128)S(1)}, f32[2,8,2048]{2,1,0:T(8,128)}, u32[]{:S(2)}) copy-start(f32[2,8,2048]{2,1,0:T(8,128)} %constant.25.clone.high_hbm) | copy-start | bytes 393220
  7.9 69.0 %copy-start.3 = (f32[2,8,2048]{2,1,0:T(8,128)S(1)}, f32[2,8,2048]{2,1,0:T(8,128)}, u32[]{:S(2)}) copy-start(f32[2,8,2048]{2,1,0:T(8,128)} %constant.24.clone.low_hbm) | copy-start | bytes 393220
  64.6 16.9 %copy-start.5 = (bf16[8,128]{1,0:T(8,128)(2,1)S(1)}, bf16[8,128]{1,0:T(8,128)(2,1)}, u32[]{:S(2)}) copy-start(bf16[8,128]{1,0:T(8,128)(2,1)} %weight_ref.1) | copy-start | bytes 6148
  64.6 16.9 %copy-start.6 = (f32[8]{0:T(128)S(1)}, f32[8]{0:T(128)}, u32[]{:S(2)}) copy-start(f32[8]{0:T(128)} %bias_ref.1) | copy-start | bytes 100
Sparse Core Ops, SparseCore 0:
  9.5 66.6 all-gather.2

commit v5 on v4

--- a/solution.py
+++ b/solution.py
@@ -9,9 +9,9 @@
 from jax.sharding import PartitionSpec as P
 
 MODES = 2048
-INNER = 512
+INNER = 1024
 SIDE = INNER // 2
-CHUNK = 256
+CHUNK = 512
 SPAN = 512
 LOW = 8
 LANES = 128
@@ -71,7 +71,7 @@
 
 
 def forward_kernel(
-    where_ref, x_hbm, table_hbm, low_hbm, high_hbm, start_hbm, out_ref,
+    x_hbm, table_hbm, low_hbm, high_hbm, start_hbm, out_ref,
     x_ref, table_ref, low_ref, high_ref, start_ref, sum_ref, diff_ref, product_ref, sems,
 ):
     chan_dev, time_dev = x_ref.shape
@@ -85,7 +85,7 @@
         for n in range(pieces)
     ]
     pairs += [(table_hbm.at[0], table_ref.at[0])]
-    pairs += [(low_hbm, low_ref), (high_hbm, high_ref), (start_hbm.at[where_ref[0]], start_ref)]
+    pairs += [(low_hbm, low_ref), (high_hbm, high_ref), (start_hbm.at[lax.axis_index("tm")], start_ref)]
     pairs += [(table_hbm.at[n], table_ref.at[n]) for n in range(1, chunks)]
     copies = start_copies(pairs, sems)
     mirror = mirror_matrix()
@@ -159,13 +159,13 @@
             )
 
 
-def forward(where, x, table, low, high, start):
+def forward(x, table, low, high, start):
     chan_dev, time_dev = x.shape
     rows = time_dev // INNER * chan_dev
     hbm = pl.BlockSpec(memory_space=pltpu.HBM)
     return pl.pallas_call(
         forward_kernel,
-        in_specs=[pl.BlockSpec(memory_space=pltpu.SMEM)] + [hbm] * 5,
+        in_specs=[hbm] * 5,
         out_specs=pl.BlockSpec(memory_space=pltpu.VMEM),
         scratch_shapes=[
             pltpu.VMEM(x.shape, x.dtype),
@@ -183,18 +183,18 @@
             flops=2 * chan_dev * time_dev * MODES, bytes_accessed=4 << 20, transcendentals=0
         ),
         name="forward_modes",
-    )(where, x, table, low, high, start)
+    )(x, table, low, high, start)
 
 
 def inverse_kernel(
-    where_ref, mixed_ref, table_hbm, low_hbm, high_hbm, start_hbm, out_ref,
+    mixed_ref, table_hbm, low_hbm, high_hbm, start_hbm, out_ref,
     table_ref, low_ref, high_ref, start_ref, turned_ref, even_ref, odd_ref, sems,
 ):
     chan_dev = mixed_ref.shape[1]
     highs = high_ref.shape[1]
     span = LOW * chan_dev
     chunks = MODES // SPAN
-    pairs = [(low_hbm, low_ref), (high_hbm, high_ref), (start_hbm.at[where_ref[0]], start_ref)]
+    pairs = [(low_hbm, low_ref), (high_hbm, high_ref), (start_hbm.at[lax.axis_index("tm")], start_ref)]
     pairs += [(table_hbm.at[n], table_ref.at[n]) for n in range(chunks)]
     copies = start_copies(pairs, sems)
     lane = lane_ids(chan_dev)
@@ -261,14 +261,13 @@
         out_ref[:, pl.ds(b * INNER + SIDE, SIDE)] = after[rows]
 
 
-def inverse(where, mixed, table, low, high, start, time_dev):
+def inverse(mixed, table, low, high, start, time_dev):
     owners, chan_dev, _ = mixed.shape
     rows = time_dev // INNER * chan_dev
     hbm = pl.BlockSpec(memory_space=pltpu.HBM)
     return pl.pallas_call(
         inverse_kernel,
-        in_specs=[pl.BlockSpec(memory_space=pltpu.SMEM), pl.BlockSpec(memory_space=pltpu.VMEM)]
-        + [hbm] * 4,
+        in_specs=[pl.BlockSpec(memory_space=pltpu.VMEM)] + [hbm] * 4,
         out_specs=pl.BlockSpec(memory_space=pltpu.VMEM),
         scratch_shapes=[
             pltpu.VMEM(table.shape, table.dtype),
@@ -286,15 +285,17 @@
             flops=2 * chan_dev * time_dev * MODES, bytes_accessed=4 << 20, transcendentals=0
         ),
         name="inverse_modes",
-    )(where, mixed, table, low, high, start)
-
-
-def mix_kernel(where_ref, spec_ref, weight_ref, out_ref, turned_ref, mixed_ref, *, steps_all):
+    )(mixed, table, low, high, start)
+
+
+def mix_kernel(spec_ref, weight_ref, out_ref, turned_ref, mixed_ref, *, steps_all):
+    time_index = lax.axis_index("tm")
+    chan_index = lax.axis_index("chan")
     turned_ref[...] = spec_ref[...].astype(jnp.float32).T
     mixed_ref[...] = jnp.zeros_like(mixed_ref)
     block_modes = weight_ref.shape[0]
     for m in range(block_modes):
-        mode = where_ref[1] * block_modes + m
+        mode = chan_index * block_modes + m
         re_row = turned_ref[pl.ds(mode, 1), :]
         im_row = turned_ref[pl.ds(HALF + mode, 1), :]
         both = jnp.concatenate([re_row, im_row, jnp.zeros((6, LANES), jnp.float32)], axis=0).astype(
@@ -302,26 +303,22 @@
         )
         by_real = jnp.dot(both, weight_ref[m, 0], preferred_element_type=jnp.float32)
         by_imag = jnp.dot(both, weight_ref[m, 1], preferred_element_type=jnp.float32)
-        scale = jnp.where(where_ref[0] * HALF + mode == 0, 1.0 / steps_all, 2.0 / steps_all)
+        scale = jnp.where(time_index * HALF + mode == 0, 1.0 / steps_all, 2.0 / steps_all)
         mixed_ref[pl.ds(mode, 1), :] = (by_real[0:1] - by_imag[1:2]) * scale
         mixed_ref[pl.ds(HALF + mode, 1), :] = (by_imag[0:1] + by_real[1:2]) * scale
     out_ref[...] = mixed_ref[...].T.astype(out_ref.dtype)
 
 
-def mix(where, spec, weight, steps_all):
+def mix(spec, weight, steps_all):
     return pl.pallas_call(
         lambda *refs: mix_kernel(*refs, steps_all=steps_all),
-        in_specs=[
-            pl.BlockSpec(memory_space=pltpu.SMEM),
-            pl.BlockSpec(memory_space=pltpu.VMEM),
-            pl.BlockSpec(memory_space=pltpu.VMEM),
-        ],
+        in_specs=[pl.BlockSpec(memory_space=pltpu.VMEM)] * 2,
         out_specs=pl.BlockSpec(memory_space=pltpu.VMEM),
         scratch_shapes=[pltpu.VMEM((128, LANES), jnp.float32), pltpu.VMEM((128, LANES), jnp.float32)],
         out_shape=jax.ShapeDtypeStruct(spec.shape, jnp.bfloat16),
         compiler_params=pltpu.CompilerParams(vmem_limit_bytes=4 << 20),
         name="mix_modes",
-    )(where, spec, weight)
+    )(spec, weight)
 
 
 def output_kernel(weight_ref, bias_ref, spectral_ref, x_hbm, out_hbm, x_ref, out_ref, sems, out_sems):
@@ -394,20 +391,19 @@
     chan_count = lax.axis_size("chan")
     steps_all = time_dev * tm_count
     forward_table, inverse_table, low, high, start = tables(steps_all, time_dev)
-    where = jnp.stack([lax.axis_index("tm"), lax.axis_index("chan")]).astype(jnp.int32)
     x = records.reshape(chan_dev, time_dev)
 
     gathered = lax.all_gather(x, "chan", axis=0, tiled=True)
 
-    partial = forward(where, x, forward_table, low, high, start)
+    partial = forward(x, forward_table, low, high, start)
     arrived = lax.all_to_all(partial, "tm", 0, 0, tiled=True)
     spectrum = sum_and_copy(arrived, chan_count)
     spectrum = lax.all_to_all(spectrum, "chan", 0, 0, tiled=True)
-    mixed = mix(where, spectrum.reshape(-1, LANES), spectral_weight, steps_all)
+    mixed = mix(spectrum.reshape(-1, LANES), spectral_weight, steps_all)
     mixed = lax.all_to_all(mixed.reshape(spectrum.shape), "chan", 0, 0, tiled=True)
     mixed = sum_and_copy(mixed, tm_count)
     mixed = lax.all_to_all(mixed, "tm", 0, 0, tiled=True)
-    spectral = inverse(where, mixed, inverse_table, low, high, start, time_dev)
+    spectral = inverse(mixed, inverse_table, low, high, start, time_dev)
 
     out = output(skip_weight, skip_bias, spectral, gathered)
     return out.reshape(groups, chan_dev, time_dev)

time: 93.8 us -> 89.6 us (0.955)
  Pallas kernels: 16.6 us -> 13.5 us
    pallas_call x1, Pallas kernels: 6.01 us -> 4.39 us  [forward(): pl.pallas_call(forward_kernel, in_specs=[hbm] * 5, out_specs=pl.BlockSpec...]
  transfers between devices with their start and end apart: 1 -> 1, of which waited for: 0 -> 0; matrix products, arithmetic and copies ran while one was open for 1% -> 0% of each run, Pallas kernels for 12% -> 9%
where the time goes in v5:
time: 89.6 us; the launch traced here: 89.4 us
  blocking collectives  61.5 us (69%)
  Pallas kernels  13.5 us (15%)
  between operations  13.5 us (15%)
    all_to_all x1, blocking collectives, shards(): spectrum = lax.all_to_all(spectrum, 'chan', 0, 0, tiled=True)  19.9 us
    all_to_all x1, blocking collectives, shards(): arrived = lax.all_to_all(partial, 'tm', 0, 0, tiled=True)  19.3 us
    all_to_all x1, blocking collectives, shards(): mixed = lax.all_to_all(mixed, 'tm', 0, 0, tiled=True)  11.8 us
    all_to_all x1, blocking collectives, shards(): lax.all_to_all(mixed.reshape(spectrum.shape), 'chan', 0, 0, tiled=True)  10.4 us
    pallas_call x1, Pallas kernels, output(): pl.pallas_call(output_kernel, in_specs=[vmem, pl.BlockSpec(memory_space=p...  5.07 us
    pallas_call x1, Pallas kernels, forward(): pl.pallas_call(forward_kernel, in_specs=[hbm] * 5, out_specs=pl.BlockSpec...  4.39 us
    pallas_call x1, Pallas kernels, inverse(): pl.pallas_call(inverse_kernel, in_specs=[pl.BlockSpec(memory_space=pltpu....  3.69 us
  transfers between devices with their start and end apart: 1, of which 0 were waited for; matrix products, arithmetic and copies ran while one was open for 0% of the time, Pallas kernels for 9%

profile of v5, /device:TPU:1, one launch (start us, length us, event | category | flops | bytes accessed | tf_op | source)
XLA Modules:
  0.0 89.4 jit_solution(9819453989806030059)
XLA Ops:
  6.5 0.0 copy-start
  6.5 0.0 copy-start.2
  6.5 0.0 copy-start.1
  6.5 0.0 copy-start.3
  6.5 0.0 all-gather.3.cloned.1.call-start
  6.6 0.7 all-gather.3.cloned.1.call-update
  7.3 4.4 %forward_modes.1 = bf16[32,8,128]{2,1,0:T(8,128)(2,1)} custom-call(bf16[8,32768]{1,0:T(8,128)(2,1)} %bitcast.8, bf16[4,512,1024]{2,1,0:T(8,128)(2,1)} %constant.14.clone.table_hbm, f32[2,8,2048]{2,1,0:T(8,128)} %constant.15.clone.low_hbm, f32[2,4,2048]{2,1,0:T(4,128)} %constant.16.clone.high_hbm, f32[32,2,2048]{2,1,0:T(2,128)} %constant.17.clone.start_hbm), custom_call_target="tpu_custom_call" | custom-call | flops 1073741824 | bytes 4194304 | tf_op jit(solution)/shard_map/forward_modes/pallas_call | solution.py:166
  11.7 0.0 copy-start.4
  11.7 0.0 copy-start.5
  11.7 19.3 %all_to_all.20 = bf16[32,8,128]{2,1,0:T(8,128)(2,1)S(1)} all-to-all(bf16[32,8,128]{2,1,0:T(8,128)(2,1)} %forward_modes.1), channel_id=1, replica_groups=mesh['tm'=32,'chan'=16] {'tm'}, dimensions={0} | all-to-all | bytes 131072 | tf_op jit(solution)/shard_map/all_to_all | solution.py:399
  31.1 19.9 %all_to_all.21 = bf16[16,8,128]{2,1,0:T(8,128)(2,1)S(1)} all-to-all(bf16[16,8,128]{2,1,0:T(8,128)(2,1)S(1)} %broadcast_in_dim.4), channel_id=1, replica_groups=mesh['tm'=32,'chan'=16] {'chan'}, dimensions={0} | all-to-all | bytes 65536 | tf_op jit(solution)/shard_map/all_to_all | solution.py:401
  51.0 0.0 copy-done.3
  51.0 0.4 mix_modes.1
  51.3 10.4 %all_to_all.22 = bf16[16,8,128]{2,1,0:T(8,128)(2,1)S(1)} all-to-all(bf16[16,8,128]{2,1,0:T(8,128)(2,1)S(1)} %bitcast.6), channel_id=1, replica_groups=mesh['tm'=32,'chan'=16] {'chan'}, dimensions={0} | all-to-all | bytes 65536 | tf_op jit(solution)/shard_map/all_to_all | solution.py:403
  61.8 11.8 %all_to_all.23.mixed_ref = bf16[32,8,128]{2,1,0:T(8,128)(2,1)S(1)} all-to-all(bf16[32,8,128]{2,1,0:T(8,128)(2,1)S(1)} %broadcast_in_dim.5), channel_id=1, replica_groups=mesh['tm'=32,'chan'=16] {'tm'}, dimensions={0} | all-to-all | bytes 131072 | tf_op jit(solution)/shard_map/all_to_all | solution.py:405
  73.7 0.0 copy-done
  73.7 0.0 copy-done.2
  73.7 0.0 copy-done.1
  73.7 3.7 %inverse_modes.1.spectral_ref = f32[8,32768]{1,0:T(8,128)S(1)} custom-call(bf16[32,8,128]{2,1,0:T(8,128)(2,1)S(1)} %all_to_all.23.mixed_ref, bf16[4,1024,512]{2,1,0:T(8,128)(2,1)} %constant.18.clone.table_hbm, f32[2,8,2048]{2,1,0:T(8,128)S(1)} %copy-done.1, f32[2,4,2048]{2,1,0:T(4,128)S(1)} %copy-done.2, f32[32,2,2048]{2,1,0:T(2,128)S(1)} %copy-done), custom_call_target="tpu_custom_call" | custom-call | flops 1073741824 | bytes 4194304 | tf_op jit(solution)/shard_map/inverse_modes/pallas_call | solution.py:268
  77.4 0.0 all-gather.3.cloned.1.call-done
  77.4 0.0 copy-done.4
  77.4 0.0 copy-done.5
  77.4 5.1 %skip_and_output.1 = bf16[8,32768]{1,0:T(8,128)(2,1)} custom-call(bf16[8,128]{1,0:T(8,128)(2,1)S(1)} %copy-done.4, f32[8]{0:T(128)S(1)} %copy-done.5, f32[8,32768]{1,0:T(8,128)S(1)} %inverse_modes.1.spectral_ref, bf16[128,32768]{1,0:T(8,128)(2,1)} %bitcast.7), custom_call_target="tpu_custom_call" | custom-call | flops 134217728 | bytes 10485760 | tf_op jit(solution)/shard_map/skip_and_output/pallas_call | solution.py:364
  (4 shorter events, 0.1 us)
Async XLA Ops:
  6.5 67.1 %copy-start = (f32[32,2,2048]{2,1,0:T(2,128)S(1)}, f32[32,2,2048]{2,1,0:T(2,128)}, u32[]{:S(2)}) copy-start(f32[32,2,2048]{2,1,0:T(2,128)} %constant.17.clone.start_hbm) | copy-start | bytes 1572868
  6.5 67.1 %copy-start.2 = (f32[2,4,2048]{2,1,0:T(4,128)S(1)}, f32[2,4,2048]{2,1,0:T(4,128)}, u32[]{:S(2)}) copy-start(f32[2,4,2048]{2,1,0:T(4,128)} %constant.16.clone.high_hbm) | copy-start | bytes 196612
  6.5 67.1 %copy-start.1 = (f32[2,8,2048]{2,1,0:T(8,128)S(1)}, f32[2,8,2048]{2,1,0:T(8,128)}, u32[]{:S(2)}) copy-start(f32[2,8,2048]{2,1,0:T(8,128)} %constant.15.clone.low_hbm) | copy-start | bytes 393220
  6.5 44.4 %copy-start.3 = (bf16[4,2,128,128]{3,2,1,0:T(8,128)(2,1)S(1)}, bf16[4,2,128,128]{3,2,1,0:T(8,128)(2,1)}, u32[]{:S(2)}) copy-start(bf16[4,2,128,128]{3,2,1,0:T(8,128)(2,1)} %refs_1_.1) | copy-start | bytes 786436
  6.5 70.9 %all-gather.3.cloned.1.call-start = ((), (), s32[]{:S(2)}) async-start(), calls=%async_computation.4 | async-start | bytes 8912896 | tf_op jit(solution)/shard_map/all_gather | solution.py:396
  11.7 65.7 %copy-start.4 = (bf16[8,128]{1,0:T(8,128)(2,1)S(1)}, bf16[8,128]{1,0:T(8,128)(2,1)}, u32[]{:S(2)}) copy-start(bf16[8,128]{1,0:T(8,128)(2,1)} %weight_ref.1) | copy-start | bytes 6148
  11.7 65.7 %copy-start.5 = (f32[8]{0:T(128)S(1)}, f32[8]{0:T(128)}, u32[]{:S(2)}) copy-start(f32[8]{0:T(128)} %bias_ref.1) | copy-start | bytes 100
Sparse Core Ops, SparseCore 0:
  9.5 66.6 all-gather.2

commit v6 on v5

--- a/solution.py
+++ b/solution.py
@@ -11,9 +11,10 @@
 MODES = 2048
 INNER = 1024
 SIDE = INNER // 2
+MIRROR = 256
 CHUNK = 512
 SPAN = 512
-LOW = 8
+LOW = 16
 LANES = 128
 HALF = 64
 VMEM_LIMIT = 52 << 20
@@ -53,9 +54,9 @@
 
 
 def mirror_matrix():
-    row = lax.broadcasted_iota(jnp.int32, (SIDE, SIDE), 0)
-    col = lax.broadcasted_iota(jnp.int32, (SIDE, SIDE), 1)
-    return jnp.where(row + col == SIDE - 1, 1.0, 0.0).astype(jnp.bfloat16)
+    row = lax.broadcasted_iota(jnp.int32, (MIRROR, MIRROR), 0)
+    col = lax.broadcasted_iota(jnp.int32, (MIRROR, MIRROR), 1)
+    return jnp.where(row + col == MIRROR - 1, 1.0, 0.0).astype(jnp.bfloat16)
 
 
 def start_copies(pairs, sems):
@@ -103,7 +104,18 @@
                     axis=0,
                 )
             )
-        before = jnp.dot(sides[0].astype(jnp.bfloat16), mirror, preferred_element_type=jnp.float32)
+        first = sides[0].astype(jnp.bfloat16)
+        before = jnp.concatenate(
+            [
+                jnp.dot(
+                    first[:, m * MIRROR : (m + 1) * MIRROR],
+                    mirror,
+                    preferred_element_type=jnp.float32,
+                )
+                for m in reversed(range(SIDE // MIRROR))
+            ],
+            axis=1,
+        )
         rows = pl.ds(n * piece_rows, piece_rows)
         sum_ref[rows, :] = (sides[1] + before).astype(jnp.bfloat16)
         diff_ref[rows, :] = (sides[1] - before).astype(jnp.bfloat16)
@@ -253,8 +265,12 @@
     mirror = mirror_matrix()
     upper = mirrored.astype(jnp.bfloat16)
     lower = (mirrored - upper.astype(jnp.float32)).astype(jnp.bfloat16)
-    before = jnp.dot(upper, mirror, preferred_element_type=jnp.float32)
-    before = before + jnp.dot(lower, mirror, preferred_element_type=jnp.float32)
+    pieces = []
+    for n in reversed(range(SIDE // MIRROR)):
+        cols = slice(n * MIRROR, (n + 1) * MIRROR)
+        piece = jnp.dot(upper[:, cols], mirror, preferred_element_type=jnp.float32)
+        pieces.append(piece + jnp.dot(lower[:, cols], mirror, preferred_element_type=jnp.float32))
+    before = jnp.concatenate(pieces, axis=1)
     for b in range(highs * LOW):
         rows = slice(b * chan_dev, (b + 1) * chan_dev)
         out_ref[:, pl.ds(b * INNER, SIDE)] = before[rows]
@@ -334,10 +350,10 @@
     stacked = jnp.concatenate(
         [jnp.concatenate([weight, none], axis=1), jnp.concatenate([none, weight], axis=1)], axis=0
     ).astype(jnp.bfloat16)
-    row = lax.broadcasted_iota(jnp.int32, (chan_dev, 1), 0)
-    bias = jnp.zeros((chan_dev, 1), jnp.float32)
-    for c in range(chan_dev):
-        bias = jnp.where(row == c, bias_ref[c], bias)
+    diagonal = lax.broadcasted_iota(jnp.int32, (chan_dev, chan_dev), 0) == lax.broadcasted_iota(
+        jnp.int32, (chan_dev, chan_dev), 1
+    )
+    bias = jnp.sum(jnp.where(diagonal, bias_ref[...], 0.0), axis=1, keepdims=True)
     results = []
     for n in range(parts):
         copies[n].wait()
@@ -363,7 +379,7 @@
     hbm = pl.BlockSpec(memory_space=pltpu.HBM)
     return pl.pallas_call(
         output_kernel,
-        in_specs=[vmem, pl.BlockSpec(memory_space=pltpu.SMEM), vmem, hbm],
+        in_specs=[vmem, vmem, vmem, hbm],
         out_specs=hbm,
         scratch_shapes=[
             pltpu.VMEM((parts, x.shape[0], time_dev // parts), x.dtype),
@@ -405,7 +421,7 @@
     mixed = lax.all_to_all(mixed, "tm", 0, 0, tiled=True)
     spectral = inverse(mixed, inverse_table, low, high, start, time_dev)
 
-    out = output(skip_weight, skip_bias, spectral, gathered)
+    out = output(skip_weight, skip_bias[None, :], spectral, gathered)
     return out.reshape(groups, chan_dev, time_dev)
 
 

time: 89.6 us -> 88.7 us (0.990)
  Pallas kernels: 13.5 us -> 12.6 us
where the time goes in v6:
time: 88.7 us; the launch traced here: 88.4 us
  blocking collectives  61.5 us (69%)
  between operations  13.5 us (15%)
  Pallas kernels  12.6 us (14%)
    all_to_all x1, blocking collectives, shards(): spectrum = lax.all_to_all(spectrum, 'chan', 0, 0, tiled=True)  19.9 us
    all_to_all x1, blocking collectives, shards(): arrived = lax.all_to_all(partial, 'tm', 0, 0, tiled=True)  19.3 us
    all_to_all x1, blocking collectives, shards(): mixed = lax.all_to_all(mixed, 'tm', 0, 0, tiled=True)  11.8 us
    all_to_all x1, blocking collectives, shards(): lax.all_to_all(mixed.reshape(spectrum.shape), 'chan', 0, 0, tiled=True)  10.4 us
    pallas_call x1, Pallas kernels, output(): pl.pallas_call(output_kernel, in_specs=[vmem, vmem, vmem, hbm], out_specs...  4.53 us
    pallas_call x1, Pallas kernels, forward(): pl.pallas_call(forward_kernel, in_specs=[hbm] * 5, out_specs=pl.BlockSpec...  4.35 us
    pallas_call x1, Pallas kernels, inverse(): pl.pallas_call(inverse_kernel, in_specs=[pl.BlockSpec(memory_space=pltpu....  3.32 us
  transfers between devices with their start and end apart: 1, of which 0 were waited for; matrix products, arithmetic and copies ran while one was open for 0% of the time, Pallas kernels for 9%

profile of v6, /device:TPU:1, one launch (start us, length us, event | category | flops | bytes accessed | tf_op | source)
XLA Modules:
  0.0 88.4 jit_solution(4504648047948067603)
XLA Ops:
  6.5 0.0 copy-start
  6.5 0.0 copy-start.3
  6.5 0.0 copy-start.1
  6.5 0.0 copy-start.2
  6.5 0.0 all-gather.3.cloned.1.call-start
  6.6 0.7 all-gather.3.cloned.1.call-update
  7.3 4.4 %forward_modes.1 = bf16[32,8,128]{2,1,0:T(8,128)(2,1)} custom-call(bf16[8,32768]{1,0:T(8,128)(2,1)} %bitcast.10, bf16[4,512,1024]{2,1,0:T(8,128)(2,1)} %constant.14.clone.table_hbm, f32[2,16,2048]{2,1,0:T(8,128)} %constant.15.clone.low_hbm, f32[2,2,2048]{2,1,0:T(2,128)} %constant.16.clone.high_hbm, f32[32,2,2048]{2,1,0:T(2,128)} %constant.17.clone.start_hbm), custom_call_target="tpu_custom_call" | custom-call | flops 1073741824 | bytes 4194304 | tf_op jit(solution)/shard_map/forward_modes/pallas_call | solution.py:178
  11.6 0.0 copy-start.4
  11.6 0.0 copy-start.5
  11.7 19.3 %all_to_all.20 = bf16[32,8,128]{2,1,0:T(8,128)(2,1)S(1)} all-to-all(bf16[32,8,128]{2,1,0:T(8,128)(2,1)} %forward_modes.1), channel_id=1, replica_groups=mesh['tm'=32,'chan'=16] {'tm'}, dimensions={0} | all-to-all | bytes 131072 | tf_op jit(solution)/shard_map/all_to_all | solution.py:415
  31.0 19.9 %all_to_all.21 = bf16[16,8,128]{2,1,0:T(8,128)(2,1)S(1)} all-to-all(bf16[16,8,128]{2,1,0:T(8,128)(2,1)S(1)} %broadcast_in_dim.7), channel_id=1, replica_groups=mesh['tm'=32,'chan'=16] {'chan'}, dimensions={0} | all-to-all | bytes 65536 | tf_op jit(solution)/shard_map/all_to_all | solution.py:417
  50.9 0.0 copy-done.2
  50.9 0.4 mix_modes.1
  51.3 10.4 %all_to_all.22 = bf16[16,8,128]{2,1,0:T(8,128)(2,1)S(1)} all-to-all(bf16[16,8,128]{2,1,0:T(8,128)(2,1)S(1)} %bitcast.7), channel_id=1, replica_groups=mesh['tm'=32,'chan'=16] {'chan'}, dimensions={0} | all-to-all | bytes 65536 | tf_op jit(solution)/shard_map/all_to_all | solution.py:419
  61.8 11.8 %all_to_all.23.mixed_ref = bf16[32,8,128]{2,1,0:T(8,128)(2,1)S(1)} all-to-all(bf16[32,8,128]{2,1,0:T(8,128)(2,1)S(1)} %broadcast_in_dim.8), channel_id=1, replica_groups=mesh['tm'=32,'chan'=16] {'tm'}, dimensions={0} | all-to-all | bytes 131072 | tf_op jit(solution)/shard_map/all_to_all | solution.py:421
  73.6 0.0 copy-done
  73.6 0.0 copy-done.3
  73.6 0.0 copy-done.1
  73.6 3.3 %inverse_modes.1.spectral_ref = f32[8,32768]{1,0:T(8,128)S(1)} custom-call(bf16[32,8,128]{2,1,0:T(8,128)(2,1)S(1)} %all_to_all.23.mixed_ref, bf16[4,1024,512]{2,1,0:T(8,128)(2,1)} %constant.18.clone.table_hbm, f32[2,16,2048]{2,1,0:T(8,128)S(1)} %copy-done.1, f32[2,2,2048]{2,1,0:T(2,128)S(1)} %copy-done.3, f32[32,2,2048]{2,1,0:T(2,128)S(1)} %copy-done), custom_call_target="tpu_custom_call" | custom-call | flops 1073741824 | bytes 4194304 | tf_op jit(solution)/shard_map/inverse_modes/pallas_call | solution.py:284
  76.9 0.0 all-gather.3.cloned.1.call-done
  77.0 0.0 copy-done.4
  77.0 0.0 copy-done.5
  77.0 4.5 %skip_and_output.1 = bf16[8,32768]{1,0:T(8,128)(2,1)} custom-call(bf16[8,128]{1,0:T(8,128)(2,1)S(1)} %copy-done.4, f32[1,8]{1,0:T(1,128)S(1)} %bitcast.8, f32[8,32768]{1,0:T(8,128)S(1)} %inverse_modes.1.spectral_ref, bf16[128,32768]{1,0:T(8,128)(2,1)} %bitcast.9), custom_call_target="tpu_custom_call" | custom-call | flops 134217728 | bytes 10485760 | tf_op jit(solution)/shard_map/skip_and_output/pallas_call | solution.py:380
  (4 shorter events, 0.1 us)
Async XLA Ops:
  6.5 67.1 %copy-start = (f32[32,2,2048]{2,1,0:T(2,128)S(1)}, f32[32,2,2048]{2,1,0:T(2,128)}, u32[]{:S(2)}) copy-start(f32[32,2,2048]{2,1,0:T(2,128)} %constant.17.clone.start_hbm) | copy-start | bytes 1572868
  6.5 67.1 %copy-start.3 = (f32[2,2,2048]{2,1,0:T(2,128)S(1)}, f32[2,2,2048]{2,1,0:T(2,128)}, u32[]{:S(2)}) copy-start(f32[2,2,2048]{2,1,0:T(2,128)} %constant.16.clone.high_hbm) | copy-start | bytes 98308
  6.5 67.1 %copy-start.1 = (f32[2,16,2048]{2,1,0:T(8,128)S(1)}, f32[2,16,2048]{2,1,0:T(8,128)}, u32[]{:S(2)}) copy-start(f32[2,16,2048]{2,1,0:T(8,128)} %constant.15.clone.low_hbm) | copy-start | bytes 786436
  6.5 44.4 %copy-start.2 = (bf16[4,2,128,128]{3,2,1,0:T(8,128)(2,1)S(1)}, bf16[4,2,128,128]{3,2,1,0:T(8,128)(2,1)}, u32[]{:S(2)}) copy-start(bf16[4,2,128,128]{3,2,1,0:T(8,128)(2,1)} %refs_1_.1) | copy-start | bytes 786436
  6.5 70.4 %all-gather.3.cloned.1.call-start = ((), (), s32[]{:S(2)}) async-start(), calls=%async_computation.4 | async-start | bytes 8912896 | tf_op jit(solution)/shard_map/all_gather | solution.py:412
  11.6 65.3 %copy-start.4 = (bf16[8,128]{1,0:T(8,128)(2,1)S(1)}, bf16[8,128]{1,0:T(8,128)(2,1)}, u32[]{:S(2)}) copy-start(bf16[8,128]{1,0:T(8,128)(2,1)} %weight_ref.1) | copy-start | bytes 6148
  11.6 65.3 %copy-start.5 = (f32[8]{0:T(128)S(1)}, f32[8]{0:T(128)}, u32[]{:S(2)}) copy-start(f32[8]{0:T(128)} %param.12) | copy-start | bytes 100
Sparse Core Ops, SparseCore 0:
  9.5 66.6 all-gather.2

commit v7 on v6

v7 whole, which is shorter than its diff:
```python
import math

import jax
import jax.numpy as jnp
import numpy as np
from jax import lax
from jax.experimental import pallas as pl
from jax.experimental.pallas import tpu as pltpu
from jax.sharding import PartitionSpec as P

MODES = 2048
INNER = 2048
SIDE = INNER // 2
MIRROR = 256
BAND = MODES // 2
CHUNK = 256
LOW = 16
LANES = 128
HALF = 64
VMEM_LIMIT = 52 << 20


def tables(steps_all, time_dev):
    tm_count = steps_all // time_dev
    blocks = time_dev // INNER
    pair = np.arange(BAND, dtype=np.int64)
    modes = np.concatenate([BAND + pair, BAND - 1 - pair])
    inner = 2 * np.arange(SIDE, dtype=np.int64) + 1

    def turn(half_steps, half_modes):
        angle = half_steps[:, None] * half_modes[None, :] % (4 * steps_all)
        return np.cos(angle * (math.pi / (2 * steps_all))), np.sin(angle * (math.pi / (2 * steps_all)))

    inner_cos, inner_sin = turn(inner, 2 * pair + 1)
    split = lambda a: a.reshape(SIDE, BAND // CHUNK, CHUNK).transpose(1, 0, 2)
    forward = np.concatenate([split(inner_cos), split(inner_sin)], axis=2)
    carrier = np.stack(turn(inner, np.array([2 * BAND - 1])))[:, :, 0]
    low = np.stack(turn(np.arange(LOW, dtype=np.int64) * (2 * INNER) + INNER - 1, 2 * modes))
    high = np.stack(turn(np.arange(blocks // LOW, dtype=np.int64) * (2 * INNER * LOW), 2 * modes))
    start = np.stack(turn(np.arange(tm_count, dtype=np.int64) * (2 * time_dev), 2 * modes), axis=1)
    return (
        np.ascontiguousarray(forward).astype(jnp.bfloat16),
        np.ascontiguousarray(forward.transpose(0, 2, 1)).astype(jnp.bfloat16),
        carrier.astype(np.float32),
        low.astype(np.float32),
        high.astype(np.float32),
        start.astype(np.float32),
    )


def lane_ids(rows):
    return lax.broadcasted_iota(jnp.int32, (rows, LANES), 1)


def mirror_matrix():
    row = lax.broadcasted_iota(jnp.int32, (MIRROR, MIRROR), 0)
    col = lax.broadcasted_iota(jnp.int32, (MIRROR, MIRROR), 1)
    return jnp.where(row + col == MIRROR - 1, 1.0, 0.0).astype(jnp.bfloat16)


def start_copies(pairs, sems):
    copies = [pltpu.make_async_copy(src, dst, sems.at[n]) for n, (src, dst) in enumerate(pairs)]
    for copy in copies:
        copy.start()
    return copies


def high_turns(high, start):
    cos_s, sin_s = start[0:1], start[1:2]
    return high[0] * cos_s - high[1] * sin_s, high[0] * sin_s + high[1] * cos_s


def owners_of(pairs_from, upper):
    count = pairs_from // HALF
    if upper:
        return BAND // HALF + count, BAND // HALF + count + 1
    return BAND // HALF - 1 - count, BAND // HALF - 2 - count


def forward_kernel(
    x_hbm, table_hbm, carrier_hbm, low_hbm, high_hbm, start_hbm, out_ref,
    x_ref, table_ref, carrier_ref, low_ref, high_ref, start_ref, even_ref, odd_ref, product_ref, sems,
):
    chan_dev, time_dev = x_ref.shape
    highs = high_ref.shape[1]
    rows_all = time_dev // INNER * chan_dev
    span = LOW * chan_dev
    chunks = BAND // CHUNK
    pairs = [(x_hbm, x_ref), (carrier_hbm, carrier_ref), (table_hbm.at[0], table_ref.at[0])]
    pairs += [(low_hbm, low_ref), (high_hbm, high_ref), (start_hbm.at[lax.axis_index("tm")], start_ref)]
    pairs += [(table_hbm.at[n], table_ref.at[n]) for n in range(1, chunks)]
    copies = start_copies(pairs, sems)
    mirror = mirror_matrix()
    copies[0].wait()
    copies[1].wait()
    sides = []
    for side in range(2):
        sides.append(
            jnp.concatenate(
                [
                    x_ref[:, pl.ds(b * INNER + side * SIDE, SIDE)].astype(jnp.float32)
                    for b in range(time_dev // INNER)
                ],
                axis=0,
            )
        )
    first = sides[0].astype(jnp.bfloat16)
    before = jnp.concatenate(
        [
            jnp.dot(
                first[:, m * MIRROR : (m + 1) * MIRROR], mirror, preferred_element_type=jnp.float32
            )
            for m in reversed(range(SIDE // MIRROR))
        ],
        axis=1,
    )
    total = sides[1] + before
    change = sides[1] - before
    carrier_cos = carrier_ref[0:1, :]
    carrier_sin = carrier_ref[1:2, :]
    even_ref[:rows_all, :] = (total * carrier_cos).astype(jnp.bfloat16)
    even_ref[rows_all:, :] = (change * carrier_sin).astype(jnp.bfloat16)
    odd_ref[:rows_all, :] = (change * carrier_cos).astype(jnp.bfloat16)
    odd_ref[rows_all:, :] = (total * carrier_sin).astype(jnp.bfloat16)
    lane = lane_ids(chan_dev)

    def multiply(n):
        copies[2 if n == 0 else 5 + n].wait()
        product_ref[n % 2, :, :CHUNK] = jnp.dot(
            even_ref[...], table_ref[n, :, :CHUNK], preferred_element_type=jnp.float32
        )
        product_ref[n % 2, :, CHUNK:] = jnp.dot(
            odd_ref[...], table_ref[n, :, CHUNK:], preferred_element_type=jnp.float32
        )

    multiply(0)
    for copy in copies[3:6]:
        copy.wait()
    for n in range(chunks):
        if n + 1 < chunks:
            multiply(n + 1)
        for tile in range(CHUNK // LANES):
            cols = pl.ds(tile * LANES, LANES)
            sin_cols = pl.ds(CHUNK + tile * LANES, LANES)
            begin = n * CHUNK + tile * LANES
            lanes = (pl.ds(begin, LANES), pl.ds(BAND + begin, LANES))
            high_turn = [high_turns(high_ref[:, :, part], start_ref[:, part]) for part in lanes]
            real, imag = [None, None], [None, None]
            for h in range(highs):
                part_real, part_imag = [None, None], [None, None]
                for b in range(LOW):
                    row = h * span + b * chan_dev
                    rows = pl.ds(row, chan_dev)
                    more = pl.ds(rows_all + row, chan_dev)
                    even_cos = product_ref[n % 2, rows, cols]
                    odd_cos = product_ref[n % 2, more, cols]
                    odd_sin = product_ref[n % 2, rows, sin_cols]
                    even_sin = product_ref[n % 2, more, sin_cols]
                    parts = (
                        (even_cos - even_sin, odd_cos + odd_sin),
                        (even_cos + even_sin, odd_cos - odd_sin),
                    )
                    for half, (by_cos, by_sin) in enumerate(parts):
                        cos_b = low_ref[0, pl.ds(b, 1), lanes[half]]
                        sin_b = low_ref[1, pl.ds(b, 1), lanes[half]]
                        re = by_cos * cos_b - by_sin * sin_b
                        im = by_cos * sin_b + by_sin * cos_b
                        part_real[half] = re if b == 0 else part_real[half] + re
                        part_imag[half] = im if b == 0 else part_imag[half] + im
                for half in range(2):
                    cos_h = high_turn[half][0][h : h + 1]
                    sin_h = high_turn[half][1][h : h + 1]
                    re = part_real[half] * cos_h - part_imag[half] * sin_h
                    im = part_real[half] * sin_h + part_imag[half] * cos_h
                    real[half] = re if h == 0 else real[half] + re
                    imag[half] = im if h == 0 else imag[half] + im
            for half in range(2):
                re, im = real[half], -imag[half]
                one, two = owners_of(begin, half == 0)
                out_ref[one] = jnp.where(lane < HALF, re, pltpu.roll(im, HALF, 1)).astype(
                    out_ref.dtype
                )
                out_ref[two] = jnp.where(lane < HALF, pltpu.roll(re, HALF, 1), im).astype(
                    out_ref.dtype
                )


def forward(x, table, carrier, low, high, start):
    chan_dev, time_dev = x.shape
    rows = time_dev // INNER * chan_dev
    hbm = pl.BlockSpec(memory_space=pltpu.HBM)
    return pl.pallas_call(
        forward_kernel,
        in_specs=[hbm] * 6,
        out_specs=pl.BlockSpec(memory_space=pltpu.VMEM),
        scratch_shapes=[
            pltpu.VMEM(x.shape, x.dtype),
            pltpu.VMEM(table.shape, table.dtype),
            pltpu.VMEM(carrier.shape, carrier.dtype),
            pltpu.VMEM(low.shape, low.dtype),
            pltpu.VMEM(high.shape, high.dtype),
            pltpu.VMEM(start.shape[1:], start.dtype),
            pltpu.VMEM((2 * rows, SIDE), jnp.bfloat16),
            pltpu.VMEM((2 * rows, SIDE), jnp.bfloat16),
            pltpu.VMEM((2, 2 * rows, 2 * CHUNK), jnp.float32),
            pltpu.SemaphoreType.DMA((BAND // CHUNK + 5,)),
        ],
        out_shape=jax.ShapeDtypeStruct((MODES // HALF, chan_dev, LANES), jnp.bfloat16),
        cost_estimate=pl.CostEstimate(
            flops=2 * chan_dev * time_dev * MODES, bytes_accessed=4 << 20, transcendentals=0
        ),
        name="forward_modes",
    )(x, table, carrier, low, high, start)


def inverse_kernel(
    mixed_ref, table_hbm, carrier_ref, low_ref, high_ref, starts_ref, out_ref,
    table_ref, even_ref, odd_ref, cos_ref, sin_ref, sems,
):
    chan_dev, time_dev = out_ref.shape
    highs = high_ref.shape[1]
    rows_all = time_dev // INNER * chan_dev
    span = LOW * chan_dev
    chunks = BAND // CHUNK
    copies = start_copies([(table_hbm.at[n], table_ref.at[n]) for n in range(chunks)], sems)
    time_index = lax.axis_index("tm")
    lane = lane_ids(chan_dev)

    def turn(n):
        for tile in range(CHUNK // LANES):
            cols = pl.ds(tile * LANES, LANES)
            begin = n * CHUNK + tile * LANES
            lanes = (pl.ds(begin, LANES), pl.ds(BAND + begin, LANES))
            high_turn = [
                high_turns(high_ref[:, :, part], starts_ref[time_index, :, part]) for part in lanes
            ]
            modes = []
            for half in range(2):
                one, two = owners_of(begin, half == 0)
                first = mixed_ref[one].astype(jnp.float32)
                second = mixed_ref[two].astype(jnp.float32)
                modes.append(
                    (
                        jnp.where(lane < HALF, first, pltpu.roll(second, HALF, 1)),
                        jnp.where(lane < HALF, pltpu.roll(first, HALF, 1), second),
                    )
                )
            for h in range(highs):
                turned_h = []
                for half, (real, imag) in enumerate(modes):
                    cos_h = high_turn[half][0][h : h + 1]
                    sin_h = high_turn[half][1][h : h + 1]
                    turned_h.append((real * cos_h - imag * sin_h, real * sin_h + imag * cos_h))
                for b in range(0, LOW, 2):
                    row = h * span + b * chan_dev
                    rows = pl.ds(row, 2 * chan_dev)
                    more = pl.ds(rows_all + row, 2 * chan_dev)
                    parts = ([], [], [], [])
                    for c in (b, b + 1):
                        turned = []
                        for half, (real, imag) in enumerate(turned_h):
                            cos_b = low_ref[0, pl.ds(c, 1), lanes[half]]
                            sin_b = low_ref[1, pl.ds(c, 1), lanes[half]]
                            turned.append((real * cos_b - imag * sin_b, real * sin_b + imag * cos_b))
                        (up_re, up_im), (down_re, down_im) = turned
                        parts[0].append(up_re + down_re)
                        parts[1].append(up_im + down_im)
                        parts[2].append(up_re - down_re)
                        parts[3].append(up_im - down_im)
                    even_re, even_im, odd_re, odd_im = [
                        jnp.concatenate(part, axis=0).astype(jnp.bfloat16) for part in parts
                    ]
                    even_ref[n % 2, rows, cols] = even_re
                    even_ref[n % 2, more, cols] = even_im
                    odd_ref[n % 2, rows, cols] = odd_re
                    odd_ref[n % 2, more, cols] = odd_im

    turn(0)
    for n in range(chunks):
        copies[n].wait()
        by_cos = jnp.dot(
            even_ref[n % 2], table_ref[n, :CHUNK, :], preferred_element_type=jnp.float32
        )
        by_sin = jnp.dot(odd_ref[n % 2], table_ref[n, CHUNK:, :], preferred_element_type=jnp.float32)
        if n == 0:
            cos_ref[...] = by_cos
            sin_ref[...] = by_sin
        else:
            cos_ref[...] += by_cos
            sin_ref[...] += by_sin
        if n + 1 < chunks:
            turn(n + 1)
    even_re = cos_ref[:rows_all, :]
    even_im = cos_ref[rows_all:, :]
    odd_re = sin_ref[:rows_all, :]
    odd_im = sin_ref[rows_all:, :]
    carrier_cos = carrier_ref[0:1, :]
    carrier_sin = carrier_ref[1:2, :]
    after = carrier_cos * (even_re - odd_im) - carrier_sin * (even_im + odd_re)
    mirrored = carrier_cos * (even_re + odd_im) + carrier_sin * (even_im - odd_re)
    mirror = mirror_matrix()
    upper = mirrored.astype(jnp.bfloat16)
    lower = (mirrored - upper.astype(jnp.float32)).astype(jnp.bfloat16)
    pieces = []
    for n in reversed(range(SIDE // MIRROR)):
        cols = slice(n * MIRROR, (n + 1) * MIRROR)
        piece = jnp.dot(upper[:, cols], mirror, preferred_element_type=jnp.float32)
        pieces.append(piece + jnp.dot(lower[:, cols], mirror, preferred_element_type=jnp.float32))
    before = jnp.concatenate(pieces, axis=1)
    for b in range(highs * LOW):
        rows = slice(b * chan_dev, (b + 1) * chan_dev)
        out_ref[:, pl.ds(b * INNER, SIDE)] = before[rows]
        out_ref[:, pl.ds(b * INNER + SIDE, SIDE)] = after[rows]


def inverse(mixed, table, carrier, low, high, start, time_dev):
    owners, chan_dev, _ = mixed.shape
    rows = time_dev // INNER * chan_dev
    hbm = pl.BlockSpec(memory_space=pltpu.HBM)
    vmem = pl.BlockSpec(memory_space=pltpu.VMEM)
    return pl.pallas_call(
        inverse_kernel,
        in_specs=[vmem, hbm, vmem, vmem, vmem, vmem],
        out_specs=pl.BlockSpec(memory_space=pltpu.VMEM),
        scratch_shapes=[
            pltpu.VMEM(table.shape, table.dtype),
            pltpu.VMEM((2, 2 * rows, CHUNK), jnp.bfloat16),
            pltpu.VMEM((2, 2 * rows, CHUNK), jnp.bfloat16),
            pltpu.VMEM((2 * rows, SIDE), jnp.float32),
            pltpu.VMEM((2 * rows, SIDE), jnp.float32),
            pltpu.SemaphoreType.DMA((BAND // CHUNK,)),
        ],
        out_shape=jax.ShapeDtypeStruct((chan_dev, time_dev), jnp.float32),
        compiler_params=pltpu.CompilerParams(vmem_limit_bytes=VMEM_LIMIT),
        cost_estimate=pl.CostEstimate(
            flops=2 * chan_dev * time_dev * MODES, bytes_accessed=4 << 20, transcendentals=0
        ),
        name="inverse_modes",
    )(mixed, table, carrier, low, high, start)


def mix_kernel(spec_ref, weight_ref, out_ref, turned_ref, mixed_ref, *, steps_all):
    time_index = lax.axis_index("tm")
    chan_index = lax.axis_index("chan")
    turned_ref[...] = spec_ref[...].astype(jnp.float32).T
    mixed_ref[...] = jnp.zeros_like(mixed_ref)
    block_modes = weight_ref.shape[0]
    for m in range(block_modes):
        mode = chan_index * block_modes + m
        place = jnp.where(time_index * HALF < BAND, HALF - 1 - mode, mode)
        re_row = turned_ref[pl.ds(place, 1), :]
        im_row = turned_ref[pl.ds(HALF + place, 1), :]
        both = jnp.concatenate([re_row, im_row, jnp.zeros((6, LANES), jnp.float32)], axis=0).astype(
            jnp.bfloat16
        )
        by_real = jnp.dot(both, weight_ref[m, 0], preferred_element_type=jnp.float32)
        by_imag = jnp.dot(both, weight_ref[m, 1], preferred_element_type=jnp.float32)
        scale = jnp.where(time_index * HALF + mode == 0, 1.0 / steps_all, 2.0 / steps_all)
        mixed_ref[pl.ds(place, 1), :] = (by_real[0:1] - by_imag[1:2]) * scale
        mixed_ref[pl.ds(HALF + place, 1), :] = (by_imag[0:1] + by_real[1:2]) * scale
    out_ref[...] = mixed_ref[...].T.astype(out_ref.dtype)


def mix(spec, weight, steps_all):
    return pl.pallas_call(
        lambda *refs: mix_kernel(*refs, steps_all=steps_all),
        in_specs=[pl.BlockSpec(memory_space=pltpu.VMEM)] * 2,
        out_specs=pl.BlockSpec(memory_space=pltpu.VMEM),
        scratch_shapes=[pltpu.VMEM((128, LANES), jnp.float32), pltpu.VMEM((128, LANES), jnp.float32)],
        out_shape=jax.ShapeDtypeStruct(spec.shape, jnp.bfloat16),
        compiler_params=pltpu.CompilerParams(vmem_limit_bytes=4 << 20),
        name="mix_modes",
    )(spec, weight)


def output_kernel(weight_ref, bias_ref, spectral_ref, x_hbm, out_hbm, x_ref, out_ref, sems, out_sems):
    chan_dev, time_dev = out_ref.shape
    parts = x_ref.shape[0]
    width = time_dev // parts
    half = width // 2
    copies = start_copies(
        [(x_hbm.at[:, pl.ds(n * width, width)], x_ref.at[n]) for n in range(parts)], sems
    )
    weight = weight_ref[...].astype(jnp.float32)
    none = jnp.zeros_like(weight)
    stacked = jnp.concatenate(
        [jnp.concatenate([weight, none], axis=1), jnp.concatenate([none, weight], axis=1)], axis=0
    ).astype(jnp.bfloat16)
    diagonal = lax.broadcasted_iota(jnp.int32, (chan_dev, chan_dev), 0) == lax.broadcasted_iota(
        jnp.int32, (chan_dev, chan_dev), 1
    )
    bias = jnp.sum(jnp.where(diagonal, bias_ref[...], 0.0), axis=1, keepdims=True)
    results = []
    for n in range(parts):
        copies[n].wait()
        x = jnp.concatenate([x_ref[n, :, :half], x_ref[n, :, half:]], axis=0)
        skip = jnp.dot(stacked, x, preferred_element_type=jnp.float32)
        for side in range(2):
            cols = pl.ds(n * width + side * half, half)
            total = spectral_ref[:, cols] + skip[side * chan_dev : (side + 1) * chan_dev] + bias
            gelu = 0.5 * total * (1.0 + lax.erf(total * math.sqrt(0.5)))
            out_ref[:, cols] = gelu.astype(out_ref.dtype)
        cols = pl.ds(n * width, width)
        result = pltpu.make_async_copy(out_ref.at[:, cols], out_hbm.at[:, cols], out_sems.at[n])
        result.start()
        results.append(result)
    for result in results:
        result.wait()


def output(weight, bias, spectral, x):
    chan_dev, time_dev = spectral.shape
    parts = 8
    vmem = pl.BlockSpec(memory_space=pltpu.VMEM)
    hbm = pl.BlockSpec(memory_space=pltpu.HBM)
    return pl.pallas_call(
        output_kernel,
        in_specs=[vmem, vmem, vmem, hbm],
        out_specs=hbm,
        scratch_shapes=[
            pltpu.VMEM((parts, x.shape[0], time_dev // parts), x.dtype),
            pltpu.VMEM((chan_dev, time_dev), jnp.bfloat16),
            pltpu.SemaphoreType.DMA((parts,)),
            pltpu.SemaphoreType.DMA((parts,)),
        ],
        out_shape=jax.ShapeDtypeStruct((chan_dev, time_dev), jnp.bfloat16),
        compiler_params=pltpu.CompilerParams(vmem_limit_bytes=VMEM_LIMIT),
        cost_estimate=pl.CostEstimate(
            flops=2 * 2 * chan_dev * x.shape[0] * time_dev, bytes_accessed=10 << 20, transcendentals=0
        ),
        name="skip_and_output",
    )(weight, bias, spectral, x)


def sum_and_copy(arrived, copies):
    total = jnp.sum(arrived.astype(jnp.float32), axis=0).astype(jnp.bfloat16)
    return jnp.broadcast_to(total[None], (copies, *total.shape))


def shards(records, spectral_weight, skip_weight, skip_bias):
    groups, chan_dev, time_dev = records.shape
    tm_count = lax.axis_size("tm")
    chan_count = lax.axis_size("chan")
    steps_all = time_dev * tm_count
    forward_table, inverse_table, carrier, low, high, start = tables(steps_all, time_dev)
    x = records.reshape(chan_dev, time_dev)

    gathered = lax.all_gather(x, "chan", axis=0, tiled=True)

    partial = forward(x, forward_table, carrier, low, high, start)
    arrived = lax.all_to_all(partial, "tm", 0, 0, tiled=True)
    spectrum = sum_and_copy(arrived, chan_count)
    spectrum = lax.all_to_all(spectrum, "chan", 0, 0, tiled=True)
    mixed = mix(spectrum.reshape(-1, LANES), spectral_weight, steps_all)
    mixed = lax.all_to_all(mixed.reshape(spectrum.shape), "chan", 0, 0, tiled=True)
    mixed = sum_and_copy(mixed, tm_count)
    mixed = lax.all_to_all(mixed, "tm", 0, 0, tiled=True)
    spectral = inverse(mixed, inverse_table, carrier, low, high, start, time_dev)

    out = output(skip_weight, skip_bias[None, :], spectral, gathered)
    return out.reshape(groups, chan_dev, time_dev)


def solution(mesh):
    return jax.shard_map(
        shards,
        mesh=mesh,
        in_specs=(
            P(None, "chan", "tm"),
            P(("tm", "chan"), None, None, None),
            P("chan", None),
            P("chan"),
        ),
        out_specs=P(None, "chan", "tm"),
        check_vma=False,
    )
```

time: 88.7 us -> 88.3 us (level)
  no operation moved by 1% of the time
where the time goes in v7:
time: 88.3 us; the launch traced here: 88.1 us
  blocking collectives  61.5 us (70%)
  between operations  13.5 us (15%)
  Pallas kernels  12.2 us (14%)
    all_to_all x1, blocking collectives, shards(): spectrum = lax.all_to_all(spectrum, 'chan', 0, 0, tiled=True)  19.9 us
    all_to_all x1, blocking collectives, shards(): arrived = lax.all_to_all(partial, 'tm', 0, 0, tiled=True)  19.3 us
    all_to_all x1, blocking collectives, shards(): mixed = lax.all_to_all(mixed, 'tm', 0, 0, tiled=True)  11.8 us
    all_to_all x1, blocking collectives, shards(): lax.all_to_all(mixed.reshape(spectrum.shape), 'chan', 0, 0, tiled=True)  10.4 us
    pallas_call x1, Pallas kernels, output(): pl.pallas_call(output_kernel, in_specs=[vmem, vmem, vmem, hbm], out_specs...  4.53 us
    pallas_call x1, Pallas kernels, forward(): pl.pallas_call(forward_kernel, in_specs=[hbm] * 6, out_specs=pl.BlockSpec...  4.19 us
    pallas_call x1, Pallas kernels, inverse(): pl.pallas_call(inverse_kernel, in_specs=[vmem, hbm, vmem, vmem, vmem, vme...  3.12 us
  transfers between devices with their start and end apart: 1, of which 0 were waited for; matrix products, arithmetic and copies ran while one was open for 0% of the time, Pallas kernels for 9%

profile of v7, /device:TPU:1, one launch (start us, length us, event | category | flops | bytes accessed | tf_op | source)
XLA Modules:
  0.0 88.1 jit_solution(15704563303542529041)
XLA Ops:
  6.5 0.0 copy-start
  6.5 0.0 copy-start.3
  6.5 0.0 copy-start.4
  6.5 0.0 copy-start.2
  6.5 0.0 all-gather.3.cloned.1.call-start
  6.6 0.7 all-gather.3.cloned.1.call-update
  7.3 4.2 %forward_modes.1 = bf16[32,8,128]{2,1,0:T(8,128)(2,1)} custom-call(bf16[8,32768]{1,0:T(8,128)(2,1)} %bitcast.10, bf16[4,1024,512]{2,1,0:T(8,128)(2,1)} %constant.16.clone.table_hbm, f32[2,1024]{1,0:T(2,128)} %constant.17.clone.carrier_hbm.carrier_ref, f32[2,16,2048]{2,1,0:T(8,128)} %constant.18.clone.low_hbm.low_ref, ...), custom_call_target="tpu_custom_call" | custom-call | flops 1073741824 | bytes 4194304 | tf_op jit(solution)/shard_map/forward_modes/pallas_call | solution.py:192
  11.5 0.0 copy-start.5
  11.5 0.0 copy-start.6
  11.5 19.3 %all_to_all.20 = bf16[32,8,128]{2,1,0:T(8,128)(2,1)S(1)} all-to-all(bf16[32,8,128]{2,1,0:T(8,128)(2,1)} %forward_modes.1), channel_id=1, replica_groups=mesh['tm'=32,'chan'=16] {'tm'}, dimensions={0} | all-to-all | bytes 131072 | tf_op jit(solution)/shard_map/all_to_all | solution.py:451
  30.9 19.9 %all_to_all.21 = bf16[16,8,128]{2,1,0:T(8,128)(2,1)S(1)} all-to-all(bf16[16,8,128]{2,1,0:T(8,128)(2,1)S(1)} %broadcast_in_dim.7), channel_id=1, replica_groups=mesh['tm'=32,'chan'=16] {'chan'}, dimensions={0} | all-to-all | bytes 65536 | tf_op jit(solution)/shard_map/all_to_all | solution.py:453
  50.8 0.0 copy-done.2
  50.8 0.4 mix_modes.1
  51.2 10.4 %all_to_all.22 = bf16[16,8,128]{2,1,0:T(8,128)(2,1)S(1)} all-to-all(bf16[16,8,128]{2,1,0:T(8,128)(2,1)S(1)} %bitcast.7), channel_id=1, replica_groups=mesh['tm'=32,'chan'=16] {'chan'}, dimensions={0} | all-to-all | bytes 65536 | tf_op jit(solution)/shard_map/all_to_all | solution.py:455
  61.6 11.8 %all_to_all.23.mixed_ref = bf16[32,8,128]{2,1,0:T(8,128)(2,1)S(1)} all-to-all(bf16[32,8,128]{2,1,0:T(8,128)(2,1)S(1)} %broadcast_in_dim.8), channel_id=1, replica_groups=mesh['tm'=32,'chan'=16] {'tm'}, dimensions={0} | all-to-all | bytes 131072 | tf_op jit(solution)/shard_map/all_to_all | solution.py:457
  73.5 0.0 copy-done
  73.5 0.0 copy-done.3
  73.5 0.0 copy-done.1
  73.5 0.0 copy-done.4
  73.5 3.1 %inverse_modes.1.spectral_ref = f32[8,32768]{1,0:T(8,128)S(1)} custom-call(bf16[32,8,128]{2,1,0:T(8,128)(2,1)S(1)} %all_to_all.23.mixed_ref, bf16[4,512,1024]{2,1,0:T(8,128)(2,1)} %constant.21.clone.table_hbm, f32[2,1024]{1,0:T(2,128)S(1)} %copy-done.4, f32[2,16,2048]{2,1,0:T(8,128)S(1)} %copy-done.1, f32[2,1,2048]{2,1,0:T(1,128)S(1)} %copy-done.3, ...), custom_call_target="tpu_custom_call" | custom-call | flops 1073741824 | bytes 4194304 | tf_op jit(solution)/shard_map/inverse_modes/pallas_call | solution.py:321
  76.6 0.0 all-gather.3.cloned.1.call-done
  76.7 0.0 copy-done.5
  76.7 0.0 copy-done.6
  76.7 4.5 %skip_and_output.1 = bf16[8,32768]{1,0:T(8,128)(2,1)} custom-call(bf16[8,128]{1,0:T(8,128)(2,1)S(1)} %copy-done.5, f32[1,8]{1,0:T(1,128)S(1)} %bitcast.8, f32[8,32768]{1,0:T(8,128)S(1)} %inverse_modes.1.spectral_ref, bf16[128,32768]{1,0:T(8,128)(2,1)} %bitcast.9), custom_call_target="tpu_custom_call" | custom-call | flops 134217728 | bytes 10485760 | tf_op jit(solution)/shard_map/skip_and_output/pallas_call | solution.py:416
  (5 shorter events, 0.1 us)
Async XLA Ops:
  6.5 66.9 %copy-start = (f32[32,2,2048]{2,1,0:T(2,128)S(1)}, f32[32,2,2048]{2,1,0:T(2,128)}, u32[]{:S(2)}) copy-start(f32[32,2,2048]{2,1,0:T(2,128)} %constant.20.clone.start_hbm.starts_ref) | copy-start | bytes 1572868
  6.5 66.9 %copy-start.3 = (f32[2,1,2048]{2,1,0:T(1,128)S(1)}, f32[2,1,2048]{2,1,0:T(1,128)}, u32[]{:S(2)}) copy-start(f32[2,1,2048]{2,1,0:T(1,128)} %constant.19.clone.high_hbm.high_ref) | copy-start | bytes 49156
  6.5 66.9 %copy-start.1 = (f32[2,16,2048]{2,1,0:T(8,128)S(1)}, f32[2,16,2048]{2,1,0:T(8,128)}, u32[]{:S(2)}) copy-start(f32[2,16,2048]{2,1,0:T(8,128)} %constant.18.clone.low_hbm.low_ref) | copy-start | bytes 786436
  6.5 66.9 %copy-start.4 = (f32[2,1024]{1,0:T(2,128)S(1)}, f32[2,1024]{1,0:T(2,128)}, u32[]{:S(2)}) copy-start(f32[2,1024]{1,0:T(2,128)} %constant.17.clone.carrier_hbm.carrier_ref) | copy-start | bytes 24580
  6.5 44.2 %copy-start.2 = (bf16[4,2,128,128]{3,2,1,0:T(8,128)(2,1)S(1)}, bf16[4,2,128,128]{3,2,1,0:T(8,128)(2,1)}, u32[]{:S(2)}) copy-start(bf16[4,2,128,128]{3,2,1,0:T(8,128)(2,1)} %refs_1_.1) | copy-start | bytes 786436
  6.5 70.1 %all-gather.3.cloned.1.call-start = ((), (), s32[]{:S(2)}) async-start(), calls=%async_computation.4 | async-start | bytes 8912896 | tf_op jit(solution)/shard_map/all_gather | solution.py:448
  11.5 65.2 %copy-start.5 = (bf16[8,128]{1,0:T(8,128)(2,1)S(1)}, bf16[8,128]{1,0:T(8,128)(2,1)}, u32[]{:S(2)}) copy-start(bf16[8,128]{1,0:T(8,128)(2,1)} %weight_ref.1) | copy-start | bytes 6148
  11.5 65.2 %copy-start.6 = (f32[8]{0:T(128)S(1)}, f32[8]{0:T(128)}, u32[]{:S(2)}) copy-start(f32[8]{0:T(128)} %param.13) | copy-start | bytes 100
Sparse Core Ops, SparseCore 0:
  9.5 66.6 all-gather.2

commit v8 on v7

--- a/solution.py
+++ b/solution.py
@@ -14,7 +14,6 @@
 MIRROR = 256
 BAND = MODES // 2
 CHUNK = 256
-LOW = 16
 LANES = 128
 HALF = 64
 VMEM_LIMIT = 52 << 20
@@ -35,15 +34,13 @@
     split = lambda a: a.reshape(SIDE, BAND // CHUNK, CHUNK).transpose(1, 0, 2)
     forward = np.concatenate([split(inner_cos), split(inner_sin)], axis=2)
     carrier = np.stack(turn(inner, np.array([2 * BAND - 1])))[:, :, 0]
-    low = np.stack(turn(np.arange(LOW, dtype=np.int64) * (2 * INNER) + INNER - 1, 2 * modes))
-    high = np.stack(turn(np.arange(blocks // LOW, dtype=np.int64) * (2 * INNER * LOW), 2 * modes))
+    block = np.stack(turn(np.arange(blocks, dtype=np.int64) * (2 * INNER) + INNER - 1, 2 * modes))
     start = np.stack(turn(np.arange(tm_count, dtype=np.int64) * (2 * time_dev), 2 * modes), axis=1)
     return (
         np.ascontiguousarray(forward).astype(jnp.bfloat16),
         np.ascontiguousarray(forward.transpose(0, 2, 1)).astype(jnp.bfloat16),
         carrier.astype(np.float32),
-        low.astype(np.float32),
-        high.astype(np.float32),
+        block.astype(np.float32),
         start.astype(np.float32),
     )
 
@@ -65,11 +62,6 @@
     return copies
 
 
-def high_turns(high, start):
-    cos_s, sin_s = start[0:1], start[1:2]
-    return high[0] * cos_s - high[1] * sin_s, high[0] * sin_s + high[1] * cos_s
-
-
 def owners_of(pairs_from, upper):
     count = pairs_from // HALF
     if upper:
@@ -78,16 +70,15 @@
 
 
 def forward_kernel(
-    x_hbm, table_hbm, carrier_hbm, low_hbm, high_hbm, start_hbm, out_ref,
-    x_ref, table_ref, carrier_ref, low_ref, high_ref, start_ref, even_ref, odd_ref, product_ref, sems,
+    x_hbm, table_hbm, carrier_hbm, block_hbm, start_hbm, out_ref,
+    x_ref, table_ref, carrier_ref, block_ref, start_ref, even_ref, odd_ref, product_ref, sems,
 ):
     chan_dev, time_dev = x_ref.shape
-    highs = high_ref.shape[1]
+    blocks = block_ref.shape[1]
     rows_all = time_dev // INNER * chan_dev
-    span = LOW * chan_dev
     chunks = BAND // CHUNK
     pairs = [(x_hbm, x_ref), (carrier_hbm, carrier_ref), (table_hbm.at[0], table_ref.at[0])]
-    pairs += [(low_hbm, low_ref), (high_hbm, high_ref), (start_hbm.at[lax.axis_index("tm")], start_ref)]
+    pairs += [(block_hbm, block_ref), (start_hbm.at[lax.axis_index("tm")], start_ref)]
     pairs += [(table_hbm.at[n], table_ref.at[n]) for n in range(1, chunks)]
     copies = start_copies(pairs, sems)
     mirror = mirror_matrix()
@@ -125,7 +116,7 @@
     lane = lane_ids(chan_dev)
 
     def multiply(n):
-        copies[2 if n == 0 else 5 + n].wait()
+        copies[2 if n == 0 else 4 + n].wait()
         product_ref[n % 2, :, :CHUNK] = jnp.dot(
             even_ref[...], table_ref[n, :, :CHUNK], preferred_element_type=jnp.float32
         )
@@ -134,7 +125,7 @@
         )
 
     multiply(0)
-    for copy in copies[3:6]:
+    for copy in copies[3:5]:
         copy.wait()
     for n in range(chunks):
         if n + 1 < chunks:
@@ -144,36 +135,32 @@
             sin_cols = pl.ds(CHUNK + tile * LANES, LANES)
             begin = n * CHUNK + tile * LANES
             lanes = (pl.ds(begin, LANES), pl.ds(BAND + begin, LANES))
-            high_turn = [high_turns(high_ref[:, :, part], start_ref[:, part]) for part in lanes]
-            real, imag = [None, None], [None, None]
-            for h in range(highs):
-                part_real, part_imag = [None, None], [None, None]
-                for b in range(LOW):
-                    row = h * span + b * chan_dev
-                    rows = pl.ds(row, chan_dev)
-                    more = pl.ds(rows_all + row, chan_dev)
-                    even_cos = product_ref[n % 2, rows, cols]
-                    odd_cos = product_ref[n % 2, more, cols]
-                    odd_sin = product_ref[n % 2, rows, sin_cols]
-                    even_sin = product_ref[n % 2, more, sin_cols]
-                    parts = (
-                        (even_cos - even_sin, odd_cos + odd_sin),
-                        (even_cos + even_sin, odd_cos - odd_sin),
-                    )
-                    for half, (by_cos, by_sin) in enumerate(parts):
-                        cos_b = low_ref[0, pl.ds(b, 1), lanes[half]]
-                        sin_b = low_ref[1, pl.ds(b, 1), lanes[half]]
-                        re = by_cos * cos_b - by_sin * sin_b
-                        im = by_cos * sin_b + by_sin * cos_b
-                        part_real[half] = re if b == 0 else part_real[half] + re
-                        part_imag[half] = im if b == 0 else part_imag[half] + im
-                for half in range(2):
-                    cos_h = high_turn[half][0][h : h + 1]
-                    sin_h = high_turn[half][1][h : h + 1]
-                    re = part_real[half] * cos_h - part_imag[half] * sin_h
-                    im = part_real[half] * sin_h + part_imag[half] * cos_h
-                    real[half] = re if h == 0 else real[half] + re
-                    imag[half] = im if h == 0 else imag[half] + im
+            part_real, part_imag = [None, None], [None, None]
+            for b in range(blocks):
+                row = b * chan_dev
+                rows = pl.ds(row, chan_dev)
+                more = pl.ds(rows_all + row, chan_dev)
+                even_cos = product_ref[n % 2, rows, cols]
+                odd_cos = product_ref[n % 2, more, cols]
+                odd_sin = product_ref[n % 2, rows, sin_cols]
+                even_sin = product_ref[n % 2, more, sin_cols]
+                parts = (
+                    (even_cos - even_sin, odd_cos + odd_sin),
+                    (even_cos + even_sin, odd_cos - odd_sin),
+                )
+                for half, (by_cos, by_sin) in enumerate(parts):
+                    cos_b = block_ref[0, pl.ds(b, 1), lanes[half]]
+                    sin_b = block_ref[1, pl.ds(b, 1), lanes[half]]
+                    re = by_cos * cos_b - by_sin * sin_b
+                    im = by_cos * sin_b + by_sin * cos_b
+                    part_real[half] = re if b == 0 else part_real[half] + re
+                    part_imag[half] = im if b == 0 else part_imag[half] + im
+            real, imag = [], []
+            for half in range(2):
+                cos_s = start_ref[0:1, lanes[half]]
+                sin_s = start_ref[1:2, lanes[half]]
+                real.append(part_real[half] * cos_s - part_imag[half] * sin_s)
+                imag.append(part_real[half] * sin_s + part_imag[half] * cos_s)
             for half in range(2):
                 re, im = real[half], -imag[half]
                 one, two = owners_of(begin, half == 0)
@@ -185,42 +172,40 @@
                 )
 
 
-def forward(x, table, carrier, low, high, start):
+def forward(x, table, carrier, block, start):
     chan_dev, time_dev = x.shape
     rows = time_dev // INNER * chan_dev
     hbm = pl.BlockSpec(memory_space=pltpu.HBM)
     return pl.pallas_call(
         forward_kernel,
-        in_specs=[hbm] * 6,
+        in_specs=[hbm] * 5,
         out_specs=pl.BlockSpec(memory_space=pltpu.VMEM),
         scratch_shapes=[
             pltpu.VMEM(x.shape, x.dtype),
             pltpu.VMEM(table.shape, table.dtype),
             pltpu.VMEM(carrier.shape, carrier.dtype),
-            pltpu.VMEM(low.shape, low.dtype),
-            pltpu.VMEM(high.shape, high.dtype),
+            pltpu.VMEM(block.shape, block.dtype),
             pltpu.VMEM(start.shape[1:], start.dtype),
             pltpu.VMEM((2 * rows, SIDE), jnp.bfloat16),
             pltpu.VMEM((2 * rows, SIDE), jnp.bfloat16),
             pltpu.VMEM((2, 2 * rows, 2 * CHUNK), jnp.float32),
-            pltpu.SemaphoreType.DMA((BAND // CHUNK + 5,)),
+            pltpu.SemaphoreType.DMA((BAND // CHUNK + 4,)),
         ],
         out_shape=jax.ShapeDtypeStruct((MODES // HALF, chan_dev, LANES), jnp.bfloat16),
         cost_estimate=pl.CostEstimate(
             flops=2 * chan_dev * time_dev * MODES, bytes_accessed=4 << 20, transcendentals=0
         ),
         name="forward_modes",
-    )(x, table, carrier, low, high, start)
+    )(x, table, carrier, block, start)
 
 
 def inverse_kernel(
-    mixed_ref, table_hbm, carrier_ref, low_ref, high_ref, starts_ref, out_ref,
+    mixed_ref, table_hbm, carrier_ref, block_ref, starts_ref, out_ref,
     table_ref, even_ref, odd_ref, cos_ref, sin_ref, sems,
 ):
     chan_dev, time_dev = out_ref.shape
-    highs = high_ref.shape[1]
+    blocks = block_ref.shape[1]
     rows_all = time_dev // INNER * chan_dev
-    span = LOW * chan_dev
     chunks = BAND // CHUNK
     copies = start_copies([(table_hbm.at[n], table_ref.at[n]) for n in range(chunks)], sems)
     time_index = lax.axis_index("tm")
@@ -231,9 +216,6 @@
             cols = pl.ds(tile * LANES, LANES)
             begin = n * CHUNK + tile * LANES
             lanes = (pl.ds(begin, LANES), pl.ds(BAND + begin, LANES))
-            high_turn = [
-                high_turns(high_ref[:, :, part], starts_ref[time_index, :, part]) for part in lanes
-            ]
             modes = []
             for half in range(2):
                 one, two = owners_of(begin, half == 0)
@@ -245,35 +227,34 @@
                         jnp.where(lane < HALF, pltpu.roll(first, HALF, 1), second),
                     )
                 )
-            for h in range(highs):
-                turned_h = []
-                for half, (real, imag) in enumerate(modes):
-                    cos_h = high_turn[half][0][h : h + 1]
-                    sin_h = high_turn[half][1][h : h + 1]
-                    turned_h.append((real * cos_h - imag * sin_h, real * sin_h + imag * cos_h))
-                for b in range(0, LOW, 2):
-                    row = h * span + b * chan_dev
-                    rows = pl.ds(row, 2 * chan_dev)
-                    more = pl.ds(rows_all + row, 2 * chan_dev)
-                    parts = ([], [], [], [])
-                    for c in (b, b + 1):
-                        turned = []
-                        for half, (real, imag) in enumerate(turned_h):
-                            cos_b = low_ref[0, pl.ds(c, 1), lanes[half]]
-                            sin_b = low_ref[1, pl.ds(c, 1), lanes[half]]
-                            turned.append((real * cos_b - imag * sin_b, real * sin_b + imag * cos_b))
-                        (up_re, up_im), (down_re, down_im) = turned
-                        parts[0].append(up_re + down_re)
-                        parts[1].append(up_im + down_im)
-                        parts[2].append(up_re - down_re)
-                        parts[3].append(up_im - down_im)
-                    even_re, even_im, odd_re, odd_im = [
-                        jnp.concatenate(part, axis=0).astype(jnp.bfloat16) for part in parts
-                    ]
-                    even_ref[n % 2, rows, cols] = even_re
-                    even_ref[n % 2, more, cols] = even_im
-                    odd_ref[n % 2, rows, cols] = odd_re
-                    odd_ref[n % 2, more, cols] = odd_im
+            started = []
+            for half, (real, imag) in enumerate(modes):
+                cos_s = starts_ref[time_index, 0:1, lanes[half]]
+                sin_s = starts_ref[time_index, 1:2, lanes[half]]
+                started.append((real * cos_s - imag * sin_s, real * sin_s + imag * cos_s))
+            for b in range(0, blocks, 2):
+                row = b * chan_dev
+                rows = pl.ds(row, 2 * chan_dev)
+                more = pl.ds(rows_all + row, 2 * chan_dev)
+                parts = ([], [], [], [])
+                for c in (b, b + 1):
+                    turned = []
+                    for half, (real, imag) in enumerate(started):
+                        cos_b = block_ref[0, pl.ds(c, 1), lanes[half]]
+                        sin_b = block_ref[1, pl.ds(c, 1), lanes[half]]
+                        turned.append((real * cos_b - imag * sin_b, real * sin_b + imag * cos_b))
+                    (up_re, up_im), (down_re, down_im) = turned
+                    parts[0].append(up_re + down_re)
+                    parts[1].append(up_im + down_im)
+                    parts[2].append(up_re - down_re)
+                    parts[3].append(up_im - down_im)
+                even_re, even_im, odd_re, odd_im = [
+                    jnp.concatenate(part, axis=0).astype(jnp.bfloat16) for part in parts
+                ]
+                even_ref[n % 2, rows, cols] = even_re
+                even_ref[n % 2, more, cols] = even_im
+                odd_ref[n % 2, rows, cols] = odd_re
+                odd_ref[n % 2, more, cols] = odd_im
 
     turn(0)
     for n in range(chunks):
@@ -307,20 +288,20 @@
         piece = jnp.dot(upper[:, cols], mirror, preferred_element_type=jnp.float32)
         pieces.append(piece + jnp.dot(lower[:, cols], mirror, preferred_element_type=jnp.float32))
     before = jnp.concatenate(pieces, axis=1)
-    for b in range(highs * LOW):
+    for b in range(blocks):
         rows = slice(b * chan_dev, (b + 1) * chan_dev)
         out_ref[:, pl.ds(b * INNER, SIDE)] = before[rows]
         out_ref[:, pl.ds(b * INNER + SIDE, SIDE)] = after[rows]
 
 
-def inverse(mixed, table, carrier, low, high, start, time_dev):
+def inverse(mixed, table, carrier, block, start, time_dev):
     owners, chan_dev, _ = mixed.shape
     rows = time_dev // INNER * chan_dev
     hbm = pl.BlockSpec(memory_space=pltpu.HBM)
     vmem = pl.BlockSpec(memory_space=pltpu.VMEM)
     return pl.pallas_call(
         inverse_kernel,
-        in_specs=[vmem, hbm, vmem, vmem, vmem, vmem],
+        in_specs=[vmem, hbm, vmem, vmem, vmem],
         out_specs=pl.BlockSpec(memory_space=pltpu.VMEM),
         scratch_shapes=[
             pltpu.VMEM(table.shape, table.dtype),
@@ -336,7 +317,7 @@
             flops=2 * chan_dev * time_dev * MODES, bytes_accessed=4 << 20, transcendentals=0
         ),
         name="inverse_modes",
-    )(mixed, table, carrier, low, high, start)
+    )(mixed, table, carrier, block, start)
 
 
 def mix_kernel(spec_ref, weight_ref, out_ref, turned_ref, mixed_ref, *, steps_all):
@@ -442,12 +423,12 @@
     tm_count = lax.axis_size("tm")
     chan_count = lax.axis_size("chan")
     steps_all = time_dev * tm_count
-    forward_table, inverse_table, carrier, low, high, start = tables(steps_all, time_dev)
+    forward_table, inverse_table, carrier, block, start = tables(steps_all, time_dev)
     x = records.reshape(chan_dev, time_dev)
 
     gathered = lax.all_gather(x, "chan", axis=0, tiled=True)
 
-    partial = forward(x, forward_table, carrier, low, high, start)
+    partial = forward(x, forward_table, carrier, block, start)
     arrived = lax.all_to_all(partial, "tm", 0, 0, tiled=True)
     spectrum = sum_and_copy(arrived, chan_count)
     spectrum = lax.all_to_all(spectrum, "chan", 0, 0, tiled=True)
@@ -455,7 +436,7 @@
     mixed = lax.all_to_all(mixed.reshape(spectrum.shape), "chan", 0, 0, tiled=True)
     mixed = sum_and_copy(mixed, tm_count)
     mixed = lax.all_to_all(mixed, "tm", 0, 0, tiled=True)
-    spectral = inverse(mixed, inverse_table, carrier, low, high, start, time_dev)
+    spectral = inverse(mixed, inverse_table, carrier, block, start, time_dev)
 
     out = output(skip_weight, skip_bias[None, :], spectral, gathered)
     return out.reshape(groups, chan_dev, time_dev)

time: 88.3 us -> 88.2 us (level)
  no operation moved by 1% of the time
where the time goes in v8:
time: 88.2 us; the launch traced here: 87.9 us
  blocking collectives  61.5 us (70%)
  between operations  13.5 us (15%)
  Pallas kernels  12.1 us (14%)
    all_to_all x1, blocking collectives, shards(): spectrum = lax.all_to_all(spectrum, 'chan', 0, 0, tiled=True)  19.9 us
    all_to_all x1, blocking collectives, shards(): arrived = lax.all_to_all(partial, 'tm', 0, 0, tiled=True)  19.3 us
    all_to_all x1, blocking collectives, shards(): mixed = lax.all_to_all(mixed, 'tm', 0, 0, tiled=True)  11.8 us
    all_to_all x1, blocking collectives, shards(): lax.all_to_all(mixed.reshape(spectrum.shape), 'chan', 0, 0, tiled=True)  10.4 us
    pallas_call x1, Pallas kernels, output(): pl.pallas_call(output_kernel, in_specs=[vmem, vmem, vmem, hbm], out_specs...  4.53 us
    pallas_call x1, Pallas kernels, forward(): pl.pallas_call(forward_kernel, in_specs=[hbm] * 5, out_specs=pl.BlockSpec...  4.08 us
    pallas_call x1, Pallas kernels, inverse(): pl.pallas_call(inverse_kernel, in_specs=[vmem, hbm, vmem, vmem, vmem], ou...  3.09 us
  transfers between devices with their start and end apart: 1, of which 0 were waited for; matrix products, arithmetic and copies ran while one was open for 0% of the time, Pallas kernels for 9%

profile of v8, /device:TPU:1, one launch (start us, length us, event | category | flops | bytes accessed | tf_op | source)
XLA Modules:
  0.0 87.9 jit_solution(13596442229597806140)
XLA Ops:
  6.5 0.0 copy-start
  6.5 0.0 copy-start.1
  6.5 0.0 copy-start.3
  6.5 0.0 copy-start.2
  6.5 0.0 all-gather.3.cloned.1.call-start
  6.6 0.7 all-gather.3.cloned.1.call-update
  7.3 4.1 %forward_modes.1 = bf16[32,8,128]{2,1,0:T(8,128)(2,1)} custom-call(bf16[8,32768]{1,0:T(8,128)(2,1)} %bitcast.10, bf16[4,1024,512]{2,1,0:T(8,128)(2,1)} %constant.14.clone.table_hbm, f32[2,1024]{1,0:T(2,128)} %constant.15.clone.carrier_hbm.carrier_ref, f32[2,16,2048]{2,1,0:T(8,128)} %constant.16.clone.block_hbm.block_ref, ...), custom_call_target="tpu_custom_call" | custom-call | flops 1073741824 | bytes 4194304 | tf_op jit(solution)/shard_map/forward_modes/pallas_call | solution.py:179
  11.4 0.0 copy-start.4
  11.4 0.0 copy-start.5
  11.4 19.3 %all_to_all.20 = bf16[32,8,128]{2,1,0:T(8,128)(2,1)S(1)} all-to-all(bf16[32,8,128]{2,1,0:T(8,128)(2,1)} %forward_modes.1), channel_id=1, replica_groups=mesh['tm'=32,'chan'=16] {'tm'}, dimensions={0} | all-to-all | bytes 131072 | tf_op jit(solution)/shard_map/all_to_all | solution.py:432
  30.8 19.9 %all_to_all.21 = bf16[16,8,128]{2,1,0:T(8,128)(2,1)S(1)} all-to-all(bf16[16,8,128]{2,1,0:T(8,128)(2,1)S(1)} %broadcast_in_dim.7), channel_id=1, replica_groups=mesh['tm'=32,'chan'=16] {'chan'}, dimensions={0} | all-to-all | bytes 65536 | tf_op jit(solution)/shard_map/all_to_all | solution.py:434
  50.7 0.0 copy-done.2
  50.7 0.4 mix_modes.1
  51.1 10.4 %all_to_all.22 = bf16[16,8,128]{2,1,0:T(8,128)(2,1)S(1)} all-to-all(bf16[16,8,128]{2,1,0:T(8,128)(2,1)S(1)} %bitcast.7), channel_id=1, replica_groups=mesh['tm'=32,'chan'=16] {'chan'}, dimensions={0} | all-to-all | bytes 65536 | tf_op jit(solution)/shard_map/all_to_all | solution.py:436
  61.5 11.8 %all_to_all.23.mixed_ref = bf16[32,8,128]{2,1,0:T(8,128)(2,1)S(1)} all-to-all(bf16[32,8,128]{2,1,0:T(8,128)(2,1)S(1)} %broadcast_in_dim.8), channel_id=1, replica_groups=mesh['tm'=32,'chan'=16] {'tm'}, dimensions={0} | all-to-all | bytes 131072 | tf_op jit(solution)/shard_map/all_to_all | solution.py:438
  73.4 0.0 copy-done
  73.4 0.0 copy-done.1
  73.4 0.0 copy-done.3
  73.4 3.1 %inverse_modes.1.spectral_ref = f32[8,32768]{1,0:T(8,128)S(1)} custom-call(bf16[32,8,128]{2,1,0:T(8,128)(2,1)S(1)} %all_to_all.23.mixed_ref, bf16[4,512,1024]{2,1,0:T(8,128)(2,1)} %constant.18.clone.table_hbm, f32[2,1024]{1,0:T(2,128)S(1)} %copy-done.3, f32[2,16,2048]{2,1,0:T(8,128)S(1)} %copy-done.1, f32[32,2,2048]{2,1,0:T(2,128)S(1)} %copy-done), custom_call_target="tpu_custom_call" | custom-call | flops 1073741824 | bytes 4194304 | tf_op jit(solution)/shard_map/inverse_modes/pallas_call | solution.py:302
  76.5 0.0 all-gather.3.cloned.1.call-done
  76.5 0.0 copy-done.4
  76.5 0.0 copy-done.5
  76.5 4.5 %skip_and_output.1 = bf16[8,32768]{1,0:T(8,128)(2,1)} custom-call(bf16[8,128]{1,0:T(8,128)(2,1)S(1)} %copy-done.4, f32[1,8]{1,0:T(1,128)S(1)} %bitcast.8, f32[8,32768]{1,0:T(8,128)S(1)} %inverse_modes.1.spectral_ref, bf16[128,32768]{1,0:T(8,128)(2,1)} %bitcast.9), custom_call_target="tpu_custom_call" | custom-call | flops 134217728 | bytes 10485760 | tf_op jit(solution)/shard_map/skip_and_output/pallas_call | solution.py:397
  (4 shorter events, 0.1 us)
Async XLA Ops:
  6.5 66.8 %copy-start = (f32[32,2,2048]{2,1,0:T(2,128)S(1)}, f32[32,2,2048]{2,1,0:T(2,128)}, u32[]{:S(2)}) copy-start(f32[32,2,2048]{2,1,0:T(2,128)} %constant.17.clone.start_hbm.starts_ref) | copy-start | bytes 1572868
  6.5 66.8 %copy-start.1 = (f32[2,16,2048]{2,1,0:T(8,128)S(1)}, f32[2,16,2048]{2,1,0:T(8,128)}, u32[]{:S(2)}) copy-start(f32[2,16,2048]{2,1,0:T(8,128)} %constant.16.clone.block_hbm.block_ref) | copy-start | bytes 786436
  6.5 66.8 %copy-start.3 = (f32[2,1024]{1,0:T(2,128)S(1)}, f32[2,1024]{1,0:T(2,128)}, u32[]{:S(2)}) copy-start(f32[2,1024]{1,0:T(2,128)} %constant.15.clone.carrier_hbm.carrier_ref) | copy-start | bytes 24580
  6.5 44.1 %copy-start.2 = (bf16[4,2,128,128]{3,2,1,0:T(8,128)(2,1)S(1)}, bf16[4,2,128,128]{3,2,1,0:T(8,128)(2,1)}, u32[]{:S(2)}) copy-start(bf16[4,2,128,128]{3,2,1,0:T(8,128)(2,1)} %refs_1_.1) | copy-start | bytes 786436
  6.5 70.0 %all-gather.3.cloned.1.call-start = ((), (), s32[]{:S(2)}) async-start(), calls=%async_computation.4 | async-start | bytes 8912896 | tf_op jit(solution)/shard_map/all_gather | solution.py:429
  11.4 65.1 %copy-start.4 = (bf16[8,128]{1,0:T(8,128)(2,1)S(1)}, bf16[8,128]{1,0:T(8,128)(2,1)}, u32[]{:S(2)}) copy-start(bf16[8,128]{1,0:T(8,128)(2,1)} %weight_ref.1) | copy-start | bytes 6148
  11.4 65.1 %copy-start.5 = (f32[8]{0:T(128)S(1)}, f32[8]{0:T(128)}, u32[]{:S(2)}) copy-start(f32[8]{0:T(128)} %param.12) | copy-start | bytes 100
Sparse Core Ops, SparseCore 0:
  9.5 66.6 all-gather.2
